TPU v7x, 32 devices: a whole 2x2x4 slice. The times are simulated.
32 devices in a mesh: fsdp: 8 (over z, core), sp: 4 (over y, x).
Axes of the slice: x: 2, y: 2, z: 4, core: 2. Of those that a mesh axis runs over, the one named last changes fastest.
Arguments:
- tokens: bfloat16 [8192, 2048], P(('fsdp', 'sp')), may hold values from -6 to 6
- segments: int32 [8192], P('fsdp'), may hold values from -1 to 2, as said below
- routes: int32 [8192, 4], P('fsdp'), may hold values from 0 to 15, all different within a row; in each aligned block of 1024 rows (0 to 1023, 1024 to 2047, ...) at most 384 rows name the same one
- cotangent: bfloat16 [8192, 2048], P(('fsdp', 'sp')), may hold values from -6 to 6
- gain_attn: bfloat16 [2048], replicated, may hold values from 0.5 to 1.5
- w_query: bfloat16 [2048, 2048], P('fsdp', 'sp'), may hold values from -0.125 to 0.125
- w_key: bfloat16 [2048, 2048], P('fsdp', 'sp'), may hold values from -0.125 to 0.125
- w_value: bfloat16 [2048, 2048], P('fsdp', 'sp'), may hold values from -0.125 to 0.125
- bias_query: bfloat16 [2048], P('sp'), may hold values from -3 to 3
- bias_key: bfloat16 [2048], P('sp'), may hold values from -3 to 3
- bias_value: bfloat16 [2048], P('sp'), may hold values from -3 to 3
- w_out: bfloat16 [2048, 2048], P('sp', 'fsdp'), may hold values from -0.75 to 0.75
- gain_mlp: bfloat16 [2048], replicated, may hold values from 0.5 to 1.5
- router: bfloat16 [2048, 16], replicated, may hold values from -0.0625 to 0.0625
- mix_gate: bfloat16 [2048], replicated, may hold values from -0.125 to 0.125
- shared_gate: bfloat16 [2048, 5632], P('fsdp', 'sp'), may hold values from -0.125 to 0.125
- shared_up: bfloat16 [2048, 5632], P('fsdp', 'sp'), may hold values from -0.125 to 0.125
- shared_down: bfloat16 [5632, 2048], P('sp', 'fsdp'), may hold values from -0.21875 to 0.21875
- expert_gate: bfloat16 [16, 2048, 1408], P('fsdp', None, 'sp'), may hold values from -0.125 to 0.125
- expert_up: bfloat16 [16, 2048, 1408], P('fsdp', None, 'sp'), may hold values from -0.125 to 0.125
- expert_down: bfloat16 [16, 1408, 2048], P('fsdp', 'sp'), may hold values from -2.5 to 2.5
Outputs:
- output: bfloat16 [8192, 2048], P(('fsdp', 'sp'))
- grad_tokens: float32 [8192, 2048], P(('fsdp', 'sp'))
- grad_gain_attn: float32 [2048], replicated
- grad_w_query: float32 [2048, 2048], P('fsdp', 'sp')
- grad_w_key: float32 [2048, 2048], P('fsdp', 'sp')
- grad_w_value: float32 [2048, 2048], P('fsdp', 'sp')
- grad_bias_query: float32 [2048], P('sp')
- grad_bias_key: float32 [2048], P('sp')
- grad_bias_value: float32 [2048], P('sp')
- grad_w_out: float32 [2048, 2048], P('sp', 'fsdp')
- grad_gain_mlp: float32 [2048], replicated
- grad_router: float32 [2048, 16], replicated
- grad_mix_gate: float32 [2048], replicated
- grad_shared_gate: float32 [2048, 5632], P('fsdp', 'sp')
- grad_shared_up: float32 [2048, 5632], P('fsdp', 'sp')
- grad_shared_down: float32 [5632, 2048], P('sp', 'fsdp')
- grad_expert_gate: float32 [16, 2048, 1408], P('fsdp', None, 'sp')
- grad_expert_up: float32 [16, 2048, 1408], P('fsdp', None, 'sp')
- grad_expert_down: float32 [16, 1408, 2048], P('fsdp', 'sp')
Inputs may be any that keep to these rules, and one draw needn't show every extreme that they name: `segments`: each sequence of 1024 tokens holds documents 0, 1 and 2 in this order, then at least one padding token marked -1; document 0 ends within the sequence's first 256 tokens and document 1 within its last 256. `routes`: each row names 4 different experts. Within each sequence no expert is named by more than 384 rows, a bound that some block reaches.
All inputs are finite; a program needn't handle non-finite values.
Results may differ from a plain program's by a relative error of at most 0.025.
Values may be sent and summed in bfloat16 or wider, within the bound.
A program may use at most 384 MiB of HBM per device.

v0:
```python
import jax
import jax.numpy as jnp
from jax import lax
from jax.sharding import PartitionSpec as P

HEAD = 128


EPSILON = 1e-06
ROPE_BASE = 1000000.0


def rms_scale(values):
    return lax.rsqrt(jnp.mean(values * values, axis=-1, keepdims=True) + EPSILON)


def norm_back(grad_rows, values, inverse_rms, gain_vector):
    weighted = grad_rows * gain_vector
    return inverse_rms * (
        weighted
        - values * inverse_rms * inverse_rms * jnp.mean(weighted * values, axis=-1, keepdims=True)
    )


def rope_tables(length, head_width):
    half_size = head_width // 2
    frequency = ROPE_BASE ** (-jnp.arange(half_size, dtype=jnp.float32) * 2.0 / head_width)
    angles = jnp.arange(length, dtype=jnp.float32)[:, None] * frequency[None, :]
    return (jnp.cos(angles)[:, None, :], jnp.sin(angles)[:, None, :])


def rotate(values, cosine, sine_table):
    half_size = values.shape[-1] // 2
    front_half = values[..., :half_size]
    back_half = values[..., half_size:]
    return jnp.concatenate(
        [
            front_half * cosine - back_half * sine_table,
            back_half * cosine + front_half * sine_table,
        ],
        axis=-1,
    )


def unrotate(gradient, cosine, sine_table):
    half_size = gradient.shape[-1] // 2
    front_half = gradient[..., :half_size]
    back_half = gradient[..., half_size:]
    return jnp.concatenate(
        [
            front_half * cosine + back_half * sine_table,
            back_half * cosine - front_half * sine_table,
        ],
        axis=-1,
    )


def silu_slope(activation):
    sigmoid_act = jax.nn.sigmoid(activation)
    return sigmoid_act * (1.0 + activation * (1.0 - sigmoid_act))


def slot_table(routes, expert_count, capacity):
    flat_routes = routes.reshape(-1)
    one_hot = (flat_routes[:, None] == jnp.arange(expert_count, dtype=jnp.int32)[None, :]).astype(
        jnp.int32
    )
    slot_index = jnp.sum(jnp.cumsum(one_hot, axis=0) * one_hot, axis=1) - 1
    destination = flat_routes * capacity + slot_index
    source = jnp.arange(flat_routes.shape[0], dtype=jnp.int32) // routes.shape[1]
    holder = jnp.zeros((expert_count * capacity,), jnp.int32).at[destination].set(source)
    filled = jnp.zeros((expert_count * capacity,), jnp.int32).at[destination].set(1)
    return (destination.reshape(routes.shape), holder, filled)


def expert_forward(inputs, gate_weights, up_weights, down_weights):
    gate_act = jnp.einsum("jrd,jdf->jrf", inputs, gate_weights, preferred_element_type=jnp.float32)
    up_act = jnp.einsum("jrd,jdf->jrf", inputs, up_weights, preferred_element_type=jnp.float32)
    activation = (jax.nn.silu(gate_act) * up_act).astype(jnp.bfloat16)
    results = jnp.einsum(
        "jrf,jfd->jrd", activation, down_weights, preferred_element_type=jnp.float32
    ).astype(jnp.bfloat16)
    return (results, (gate_act, up_act, activation))


def expert_backward(inputs, grad_results, kept_acts, gate_weights, up_weights, down_weights):
    gate_act, up_act, activation = kept_acts
    d_activation = jnp.einsum(
        "jrd,jfd->jrf", grad_results, down_weights, preferred_element_type=jnp.float32
    )
    d_gate = (d_activation * up_act * silu_slope(gate_act)).astype(jnp.bfloat16)
    d_up = (d_activation * jax.nn.silu(gate_act)).astype(jnp.bfloat16)
    d_inputs = jnp.einsum("jrf,jdf->jrd", d_gate, gate_weights, preferred_element_type=jnp.float32)
    d_inputs = (
        d_inputs + jnp.einsum("jrf,jdf->jrd", d_up, up_weights, preferred_element_type=jnp.float32)
    ).astype(jnp.bfloat16)
    grad_gate = jnp.einsum("jrd,jrf->jdf", inputs, d_gate, preferred_element_type=jnp.float32)
    grad_up = jnp.einsum("jrd,jrf->jdf", inputs, d_up, preferred_element_type=jnp.float32)
    grad_down = jnp.einsum(
        "jrf,jrd->jfd", activation, grad_results, preferred_element_type=jnp.float32
    )
    return (d_inputs, (grad_gate, grad_up, grad_down))


def local(
    tokens,
    segments,
    routes,
    cotangent,
    gain_attn,
    w_query,
    w_key,
    w_value,
    bias_query,
    bias_key,
    bias_value,
    w_out,
    gain_mlp,
    router,
    mix_gate,
    shared_gate,
    shared_up,
    shared_down,
    expert_gate,
    expert_up,
    expert_down,
):
    fsdp_count = lax.axis_size("fsdp")
    sp_count = lax.axis_size("sp")
    sp_place = lax.axis_index("sp")
    tok_count = tokens.shape[0]
    seq_len = segments.shape[0]
    width = tokens.shape[1]
    top_count = routes.shape[1]
    expert_count = router.shape[1]
    local_experts = expert_gate.shape[0]
    capacity = 3 * seq_len * top_count // (2 * expert_count)
    local_heads = w_query.shape[1] // HEAD
    row_block = min(512, seq_len)
    block_count = seq_len // row_block
    score_scale = HEAD ** (-0.5)
    own_segments = lax.dynamic_slice_in_dim(segments, sp_place * tok_count, tok_count)
    live_rows = (own_segments >= 0).astype(jnp.float32)[:, None]
    position = jnp.arange(seq_len, dtype=jnp.int32)
    cosine, sine_table = rope_tables(seq_len, HEAD)

    def spread(local_rows):
        return lax.all_gather(local_rows, "sp", axis=0, tiled=True)

    def collect(partial_rows):
        return lax.psum_scatter(partial_rows, "sp", scatter_dimension=0, tiled=True)

    def to_experts(send_rows):
        return lax.all_to_all(send_rows, "fsdp", split_axis=0, concat_axis=2, tiled=True)

    def from_experts(result_rows):
        return lax.all_to_all(result_rows, "fsdp", split_axis=2, concat_axis=0, tiled=True)

    inputs = tokens.astype(jnp.float32)
    attn_rms = rms_scale(inputs)
    gain_one = gain_attn.astype(jnp.float32)
    normed_attn = spread((inputs * attn_rms * gain_one).astype(jnp.bfloat16))
    full_query, full_key, full_value, full_out, full_sgate, full_sup, full_sdown = (
        lax.all_gather(w_query, "fsdp", axis=0, tiled=True),
        lax.all_gather(w_key, "fsdp", axis=0, tiled=True),
        lax.all_gather(w_value, "fsdp", axis=0, tiled=True),
        lax.all_gather(w_out, "fsdp", axis=1, tiled=True),
        lax.all_gather(shared_gate, "fsdp", axis=0, tiled=True),
        lax.all_gather(shared_up, "fsdp", axis=0, tiled=True),
        lax.all_gather(shared_down, "fsdp", axis=1, tiled=True),
    )
    query_lin = jnp.dot(
        normed_attn, full_query, preferred_element_type=jnp.float32
    ) + bias_query.astype(jnp.float32)
    key_lin = jnp.dot(normed_attn, full_key, preferred_element_type=jnp.float32) + bias_key.astype(
        jnp.float32
    )
    value_rows = (
        (
            jnp.dot(normed_attn, full_value, preferred_element_type=jnp.float32)
            + bias_value.astype(jnp.float32)
        )
        .astype(jnp.bfloat16)
        .reshape(seq_len, local_heads, HEAD)
    )
    query_rot = rotate(query_lin.reshape(seq_len, local_heads, HEAD), cosine, sine_table).astype(
        jnp.bfloat16
    )
    key_rot = rotate(key_lin.reshape(seq_len, local_heads, HEAD), cosine, sine_table).astype(
        jnp.bfloat16
    )

    def block_scores(block_index):
        offset = block_index * row_block
        query_block = lax.dynamic_slice_in_dim(query_rot, offset, row_block)
        raw_scores = (
            jnp.einsum("qhd,khd->hqk", query_block, key_rot, preferred_element_type=jnp.float32)
            * score_scale
        )
        seg_block = lax.dynamic_slice_in_dim(segments, offset, row_block)
        pos_block = offset + jnp.arange(row_block, dtype=jnp.int32)
        allowed = (
            (seg_block[:, None] == segments[None, :]) & (position[None, :] <= pos_block[:, None])
        )[None]
        return (query_block, raw_scores, allowed)

    def attend_block(block_index):
        score_parts = block_scores(block_index)
        raw_scores = score_parts[1]
        allowed = score_parts[2]
        row_max = jnp.max(jnp.where(allowed, raw_scores, -jnp.inf), axis=-1, keepdims=True)
        exponent = jnp.exp(jnp.where(allowed, raw_scores - row_max, -jnp.inf))
        row_total = jnp.sum(exponent, axis=-1, keepdims=True)
        probability = (exponent / row_total).astype(jnp.bfloat16)
        attended_block = jnp.einsum(
            "hqk,khd->qhd", probability, value_rows, preferred_element_type=jnp.float32
        ).astype(jnp.bfloat16)
        return (attended_block, (row_max + jnp.log(row_total))[..., 0])

    attended, log_total = lax.map(attend_block, jnp.arange(block_count))
    attended = attended.reshape(seq_len, local_heads * HEAD)
    attn_out = collect(jnp.dot(attended, full_out, preferred_element_type=jnp.float32))
    hidden = inputs + live_rows * attn_out
    mlp_rms = rms_scale(hidden)
    gain_two = gain_mlp.astype(jnp.float32)
    normed_mlp = spread((hidden * mlp_rms * gain_two).astype(jnp.bfloat16))
    shared_gate_act = jnp.dot(normed_mlp, full_sgate, preferred_element_type=jnp.float32)
    shared_up_act = jnp.dot(normed_mlp, full_sup, preferred_element_type=jnp.float32)
    shared_act = (jax.nn.silu(shared_gate_act) * shared_up_act).astype(jnp.bfloat16)
    shared_result = jnp.dot(shared_act, full_sdown, preferred_element_type=jnp.float32)
    switch = jax.nn.sigmoid(jnp.dot(normed_mlp, mix_gate, preferred_element_type=jnp.float32))
    probability = jax.nn.softmax(
        jnp.dot(normed_mlp, router, preferred_element_type=jnp.float32), axis=-1
    )
    one_hot = (
        routes[:, :, None] == jnp.arange(expert_count, dtype=jnp.int32)[None, None, :]
    ).astype(jnp.float32)
    gate_weights = jnp.sum(probability[:, None, :] * one_hot, axis=-1)
    destination, holder, filled = slot_table(routes, expert_count, capacity)
    send_rows = jnp.where(
        filled[:, None] > 0, normed_mlp[holder], jnp.zeros((), jnp.bfloat16)
    ).reshape(fsdp_count, local_experts, capacity, width)
    expert_rows = to_experts(send_rows)[0]
    results, kept_acts = expert_forward(expert_rows, expert_gate, expert_up, expert_down)
    returned = from_experts(results[None]).reshape(expert_count * capacity, width)
    mixer_part = switch[:, None] * shared_result
    for route_slot in range(top_count):
        mixer_part = mixer_part + gate_weights[:, route_slot : route_slot + 1] * returned[
            destination[:, route_slot]
        ].astype(jnp.float32)
    mixer_out = collect(mixer_part)
    output = (hidden + live_rows * mixer_out).astype(jnp.bfloat16)
    back_query, back_key, back_value, back_out, back_sgate, back_sup, back_sdown = (
        lax.all_gather(w_query, "fsdp", axis=0, tiled=True),
        lax.all_gather(w_key, "fsdp", axis=0, tiled=True),
        lax.all_gather(w_value, "fsdp", axis=0, tiled=True),
        lax.all_gather(w_out, "fsdp", axis=1, tiled=True),
        lax.all_gather(shared_gate, "fsdp", axis=0, tiled=True),
        lax.all_gather(shared_up, "fsdp", axis=0, tiled=True),
        lax.all_gather(shared_down, "fsdp", axis=1, tiled=True),
    )
    upstream = cotangent.astype(jnp.float32)
    d_mixer = spread((live_rows * upstream).astype(jnp.bfloat16))
    d_switch = jnp.sum(d_mixer.astype(jnp.float32) * shared_result, axis=-1)
    d_shared = (switch[:, None] * d_mixer.astype(jnp.float32)).astype(jnp.bfloat16)
    gate_columns = []
    for route_slot in range(top_count):
        gate_columns.append(
            jnp.sum(
                d_mixer.astype(jnp.float32)
                * returned[destination[:, route_slot]].astype(jnp.float32),
                axis=-1,
            )
        )
    d_gate_weights = jnp.stack(gate_columns, axis=1)
    slot_gate = (
        jnp.zeros((expert_count * capacity,), jnp.float32)
        .at[destination.reshape(-1)]
        .set(gate_weights.reshape(-1))
    )
    d_send = (
        (slot_gate[:, None] * d_mixer[holder].astype(jnp.float32))
        .astype(jnp.bfloat16)
        .reshape(fsdp_count, local_experts, capacity, width)
    )
    d_expert_in = to_experts(d_send)[0]
    d_expert_rows, own_grads = expert_backward(
        expert_rows, d_expert_in, kept_acts, expert_gate, expert_up, expert_down
    )
    grad_expert_gate, grad_expert_up, grad_expert_down = own_grads
    d_returned = from_experts(d_expert_rows[None]).reshape(expert_count * capacity, width)
    d_shared_act = jnp.dot(d_shared, back_sdown.T, preferred_element_type=jnp.float32)
    d_sgate = (d_shared_act * shared_up_act * silu_slope(shared_gate_act)).astype(jnp.bfloat16)
    d_sup = (d_shared_act * jax.nn.silu(shared_gate_act)).astype(jnp.bfloat16)
    d_probability = jnp.sum(one_hot * d_gate_weights[:, :, None], axis=1)
    d_logits = probability * (
        d_probability - jnp.sum(probability * d_probability, axis=-1, keepdims=True)
    )
    d_gate_in = d_switch * switch * (1.0 - switch)
    router_wide = router.astype(jnp.float32)
    d_normed_mlp = jnp.dot(d_sgate, back_sgate.T, preferred_element_type=jnp.float32) + jnp.dot(
        d_sup, back_sup.T, preferred_element_type=jnp.float32
    )
    d_normed_mlp = (
        d_normed_mlp
        + jnp.dot(d_logits, router_wide.T, precision=lax.Precision.HIGHEST)
        + d_gate_in[:, None] * mix_gate.astype(jnp.float32)[None, :]
    )
    for route_slot in range(top_count):
        d_normed_mlp = d_normed_mlp + d_returned[destination[:, route_slot]].astype(jnp.float32)
    grad_sdown = jnp.dot(shared_act.T, d_shared, preferred_element_type=jnp.float32)
    grad_sgate = jnp.dot(normed_mlp.T, d_sgate, preferred_element_type=jnp.float32)
    grad_sup = jnp.dot(normed_mlp.T, d_sup, preferred_element_type=jnp.float32)
    normed_wide = normed_mlp.astype(jnp.float32)
    grad_router = jnp.dot(normed_wide.T, d_logits, precision=lax.Precision.HIGHEST)
    grad_mix = jnp.dot(d_gate_in, normed_wide, precision=lax.Precision.HIGHEST)
    d_mlp_own = collect(d_normed_mlp)
    grad_gain_two = jnp.sum(d_mlp_own * hidden * mlp_rms, axis=0)
    d_hidden = upstream + norm_back(d_mlp_own, hidden, mlp_rms, gain_two)
    d_attn = spread((live_rows * d_hidden).astype(jnp.bfloat16))
    grad_out = jnp.dot(attended.T, d_attn, preferred_element_type=jnp.float32)
    d_attended = (
        jnp.dot(d_attn, back_out.T, preferred_element_type=jnp.float32)
        .astype(jnp.bfloat16)
        .reshape(seq_len, local_heads, HEAD)
    )

    def attend_back(carry_in, block_index):
        key_grad, value_grad = carry_in
        query_block, raw_scores, allowed = block_scores(block_index)
        offset = block_index * row_block
        log_block = lax.dynamic_index_in_dim(log_total, block_index, keepdims=False)
        prob_full = jnp.exp(jnp.where(allowed, raw_scores - log_block[..., None], -jnp.inf))
        prob_low = prob_full.astype(jnp.bfloat16)
        grad_block = lax.dynamic_slice_in_dim(d_attended, offset, row_block)
        d_prob = jnp.einsum(
            "qhd,khd->hqk", grad_block, value_rows, preferred_element_type=jnp.float32
        )
        d_scores = (
            prob_full * (d_prob - jnp.sum(prob_full * d_prob, axis=-1, keepdims=True))
        ).astype(jnp.bfloat16)
        query_grad = (
            jnp.einsum("hqk,khd->qhd", d_scores, key_rot, preferred_element_type=jnp.float32)
            * score_scale
        )
        key_grad = (
            key_grad
            + jnp.einsum("hqk,qhd->khd", d_scores, query_block, preferred_element_type=jnp.float32)
            * score_scale
        )
        value_grad = value_grad + jnp.einsum(
            "hqk,qhd->khd", prob_low, grad_block, preferred_element_type=jnp.float32
        )
        return ((key_grad, value_grad), query_grad)

    zero_grad = jnp.zeros((seq_len, local_heads, HEAD), jnp.float32)
    (key_grad, value_grad), query_grad = lax.scan(
        attend_back, (zero_grad, zero_grad), jnp.arange(block_count)
    )
    query_grad = query_grad.reshape(seq_len, local_heads, HEAD)
    d_query = (
        unrotate(query_grad, cosine, sine_table)
        .reshape(seq_len, local_heads * HEAD)
        .astype(jnp.bfloat16)
    )
    d_key = (
        unrotate(key_grad, cosine, sine_table)
        .reshape(seq_len, local_heads * HEAD)
        .astype(jnp.bfloat16)
    )
    d_value = value_grad.reshape(seq_len, local_heads * HEAD).astype(jnp.bfloat16)
    d_normed_attn = jnp.dot(d_query, back_query.T, preferred_element_type=jnp.float32)
    d_normed_attn = d_normed_attn + jnp.dot(d_key, back_key.T, preferred_element_type=jnp.float32)
    d_normed_attn = d_normed_attn + jnp.dot(
        d_value, back_value.T, preferred_element_type=jnp.float32
    )
    grad_query = jnp.dot(normed_attn.T, d_query, preferred_element_type=jnp.float32)
    grad_key = jnp.dot(normed_attn.T, d_key, preferred_element_type=jnp.float32)
    grad_value = jnp.dot(normed_attn.T, d_value, preferred_element_type=jnp.float32)
    bias_grads = jnp.stack(
        [
            jnp.sum(d_query.astype(jnp.float32), axis=0),
            jnp.sum(d_key.astype(jnp.float32), axis=0),
            jnp.sum(d_value.astype(jnp.float32), axis=0),
        ]
    )
    d_attn_own = collect(d_normed_attn)
    grad_gain_one = jnp.sum(d_attn_own * inputs * attn_rms, axis=0)
    grad_tokens = d_hidden + norm_back(d_attn_own, inputs, attn_rms, gain_one)
    (
        grad_w_query,
        grad_w_key,
        grad_w_value,
        grad_w_out,
        grad_shared_gate,
        grad_shared_up,
        grad_shared_down,
    ) = (
        lax.psum_scatter(
            grad_query.astype(jnp.bfloat16), "fsdp", scatter_dimension=0, tiled=True
        ).astype(jnp.float32),
        lax.psum_scatter(
            grad_key.astype(jnp.bfloat16), "fsdp", scatter_dimension=0, tiled=True
        ).astype(jnp.float32),
        lax.psum_scatter(
            grad_value.astype(jnp.bfloat16), "fsdp", scatter_dimension=0, tiled=True
        ).astype(jnp.float32),
        lax.psum_scatter(
            grad_out.astype(jnp.bfloat16), "fsdp", scatter_dimension=1, tiled=True
        ).astype(jnp.float32),
        lax.psum_scatter(
            grad_sgate.astype(jnp.bfloat16), "fsdp", scatter_dimension=0, tiled=True
        ).astype(jnp.float32),
        lax.psum_scatter(
            grad_sup.astype(jnp.bfloat16), "fsdp", scatter_dimension=0, tiled=True
        ).astype(jnp.float32),
        lax.psum_scatter(
            grad_sdown.astype(jnp.bfloat16), "fsdp", scatter_dimension=1, tiled=True
        ).astype(jnp.float32),
    )
    bias_width = bias_grads.shape[1]
    bias_place = lax.dynamic_update_slice(
        jnp.zeros((3, sp_count * bias_width), jnp.float32), bias_grads, (0, sp_place * bias_width)
    )
    sum_gain_one, sum_gain_two, sum_router, sum_mix, sum_bias = lax.psum(
        (grad_gain_one, grad_gain_two, grad_router, grad_mix, bias_place), ("fsdp", "sp")
    )
    own_bias = lax.dynamic_slice_in_dim(sum_bias, sp_place * bias_width, bias_width, 1)
    return (
        output,
        grad_tokens,
        sum_gain_one,
        grad_w_query,
        grad_w_key,
        grad_w_value,
        own_bias[0],
        own_bias[1],
        own_bias[2],
        grad_w_out,
        sum_gain_two,
        sum_router,
        sum_mix,
        grad_shared_gate,
        grad_shared_up,
        grad_shared_down,
        grad_expert_gate,
        grad_expert_up,
        grad_expert_down,
    )


def solution(mesh):
    return jax.shard_map(
        local,
        mesh=mesh,
        in_specs=(
            P(("fsdp", "sp"), None),
            P("fsdp"),
            P("fsdp", None),
            P(("fsdp", "sp"), None),
            P(),
            P("fsdp", "sp"),
            P("fsdp", "sp"),
            P("fsdp", "sp"),
            P("sp"),
            P("sp"),
            P("sp"),
            P("sp", "fsdp"),
            P(),
            P(),
            P(),
            P("fsdp", "sp"),
            P("fsdp", "sp"),
            P("sp", "fsdp"),
            P("fsdp", None, "sp"),
            P("fsdp", None, "sp"),
            P("fsdp", "sp", None),
        ),
        out_specs=(
            P(("fsdp", "sp"), None),
            P(("fsdp", "sp"), None),
            P(),
            P("fsdp", "sp"),
            P("fsdp", "sp"),
            P("fsdp", "sp"),
            P("sp"),
            P("sp"),
            P("sp"),
            P("sp", "fsdp"),
            P(),
            P(),
            P(),
            P("fsdp", "sp"),
            P("fsdp", "sp"),
            P("sp", "fsdp"),
            P("fsdp", None, "sp"),
            P("fsdp", None, "sp"),
            P("fsdp", "sp", None),
        ),
        check_vma=False,
    )
```

profile of v0, /device:TPU:0, one launch (start us, length us, event | category | flops | bytes accessed | tf_op | source)
XLA Modules:
  0.0 4110.7 jit_solution(713354049901323939)
XLA Ops:
  18.2 23.3 all-gather.18.cloned.1.call-done
  41.5 54.6 %all-gather.12.cloned.1.call-done = bf16[1024,2048]{1,0:T(8,128)(2,1)} async-done(((bf16[256,2048]{1,0:T(8,128)(2,1)}), bf16[1024,2048]{1,0:T(8,128)(2,1)}) %all-gather.12.cloned.1.call-update) | async-done | bytes 4194320 | tf_op jit(solution)/shard_map/all_gather | solution.py:148
  104.6 22.3 all-gather.16.cloned.1.call-done
  180.6 24.8 while.28
  213.8 85.4 %reduce-scatter.12.cloned.1.call-done = f32[256,2048]{1,0:T(8,128)} async-done(((f32[1024,2048]{1,0:T(8,128)}), f32[256,2048]{1,0:T(8,128)}) %reduce-scatter.12.cloned.1.call-update) | async-done | bytes 2097168 | tf_op jit(solution)/shard_map/reduce_scatter | solution.py:151
  339.9 25.4 scatter_custom_fusion
  365.4 49.1 %gather_fusion = bf16[6144,2048]{1,0:T(8,128)(2,1)} fusion(bf16[1024,2048]{1,0:T(8,128)(2,1)} %all-gather.22.cloned.1.call-done, s32[6144]{0:T(1024)S(1)} %fusion.83), kind=kCustom, calls=%fused_computation | custom fusion | bytes 50356224 | tf_op jit(solution)/shard_map/gather | solution.py:241
  435.4 549.2 %all_to_all.60 = bf16[8,2,384,2048]{3,2,1,0:T(8,128)(2,1)S(1)} all-to-all(bf16[8,2,384,2048]{3,2,1,0:T(8,128)(2,1)} %broadcast_select_fusion), channel_id=1, replica_groups=mesh['fsdp'=8,'sp'=4] {'fsdp'}, dimensions={0} | all-to-all | bytes 50331648 | tf_op jit(solution)/shard_map/all_to_all | solution.py:154
  1049.9 45.5 %copy.146 = bf16[1,2,3072,2048]{3,1,0,2:T(2,128)(2,1)} copy(bf16[1,2,3072,2048]{3,2,1,0:T(8,128)(2,1)} %convert_bitcast_fusion) | data formatting | bytes 50331648 | tf_op jit(solution)/shard_map/broadcast_in_dim | solution.py:245
  1106.5 52.0 %all-gather.30.cloned.1.call-done = bf16[1024,2048]{1,0:T(8,128)(2,1)} async-done(((bf16[256,2048]{1,0:T(8,128)(2,1)}), bf16[1024,2048]{1,0:T(8,128)(2,1)}) %all-gather.30.cloned.1.call-update) | async-done | bytes 4194320 | tf_op jit(solution)/shard_map/all_gather | solution.py:148
  1158.5 49.3 %gather_fusion.5 = bf16[6144,2048]{1,0:T(8,128)(2,1)} fusion(bf16[1024,2048]{1,0:T(8,128)(2,1)} %all-gather.30.cloned.1.call-done, s32[6144]{0:T(1024)S(1)} %fusion.83), kind=kCustom, calls=%fused_computation.5 | custom fusion | bytes 50356224 | tf_op jit(solution)/shard_map/gather | solution.py:282
  1213.3 83.5 %all-gather.26.cloned.1.call-done = bf16[2048,1408]{1,0:T(8,128)(2,1)} async-done(((bf16[256,1408]{1,0:T(8,128)(2,1)}), bf16[2048,1408]{1,0:T(8,128)(2,1)}) %all-gather.26.cloned.1.call-update) | async-done | bytes 5767184 | tf_op jit(solution)/shard_map/all_gather | solution.py:169
  1308.5 111.0 %all-gather.24.cloned.1.call-done = bf16[2048,1408]{1,0:T(8,128)(2,1)} async-done(((bf16[256,1408]{1,0:T(8,128)(2,1)}), bf16[2048,1408]{1,0:T(8,128)(2,1)}) %all-gather.24.cloned.1.call-update) | async-done | bytes 5767184 | tf_op jit(solution)/shard_map/all_gather | solution.py:168
  1431.1 234.8 %all-gather.28.cloned.1.call-done = bf16[1408,2048]{1,0:T(8,128)(2,1)} async-done(((bf16[1408,256]{1,0:T(8,128)(2,1)}), bf16[1408,2048]{1,0:T(8,128)(2,1)}) %all-gather.28.cloned.1.call-update) | async-done | bytes 5767184 | tf_op jit(solution)/shard_map/all_gather | solution.py:170
  1682.7 101.7 %all-to-all-done.1 = bf16[1,2,3072,2048]{3,1,0,2:T(2,128)(2,1)} async-done(((bf16[1,2,3072,2048]{3,1,0,2:T(2,128)(2,1)}), bf16[1,2,3072,2048]{3,1,0,2:T(2,128)(2,1)}, u32[]{:S(2)}, u32[]{:S(2)}) %all-to-all-start.1) | async-done | bytes 25165856 | tf_op jit(solution)/shard_map/all_to_all | solution.py:157
  1784.4 25.8 copy.147
  1941.8 548.9 %all_to_all.61 = bf16[8,2,384,2048]{3,2,1,0:T(8,128)(2,1)} all-to-all(bf16[8,2,384,2048]{3,2,1,0:T(8,128)(2,1)S(1)} %fusion.38), channel_id=1, replica_groups=mesh['fsdp'=8,'sp'=4] {'fsdp'}, dimensions={0} | all-to-all | bytes 50331648 | tf_op jit(solution)/shard_map/all_to_all | solution.py:154
  2533.8 25.2 fusion.106
  2559.0 28.4 fusion.39
  2587.4 45.5 %copy.150 = bf16[1,2,3072,2048]{3,1,0,2:T(2,128)(2,1)} copy(bf16[1,2,3072,2048]{3,2,1,0:T(8,128)(2,1)} %fusion.39) | data formatting | bytes 50331648 | tf_op jit(solution)/shard_map/broadcast_in_dim | solution.py:291
  2662.3 520.5 %all-to-all-done.3 = bf16[1,2,3072,2048]{3,1,0,2:T(2,128)(2,1)} async-done(((bf16[1,2,3072,2048]{3,1,0,2:T(2,128)(2,1)}), bf16[1,2,3072,2048]{3,1,0,2:T(2,128)(2,1)}, u32[]{:S(2)}, u32[]{:S(2)}) %all-to-all-start.3) | async-done | bytes 25165856 | tf_op jit(solution)/shard_map/all_to_all | solution.py:157
  3182.9 25.4 copy.151
  3322.1 69.2 %reduce-scatter.16.cloned.1.call-done = f32[256,2048]{1,0:T(8,128)} async-done(((f32[1024,2048]{1,0:T(8,128)}), f32[256,2048]{1,0:T(8,128)}) %reduce-scatter.16.cloned.1.call-update) | async-done | bytes 2097168 | tf_op jit(solution)/shard_map/reduce_scatter | solution.py:151
  3394.1 86.7 %reduce-scatter.14.cloned.1.call-done = f32[256,2048]{1,0:T(8,128)} async-done(((f32[1024,2048]{1,0:T(8,128)}), f32[256,2048]{1,0:T(8,128)}) %reduce-scatter.14.cloned.1.call-update) | async-done | bytes 2097168 | tf_op jit(solution)/shard_map/reduce_scatter | solution.py:151
  3551.7 44.8 %while.29 = (s32[]{:T(128)}, f32[1024,4,128]{0,2,1:T(8,128)S(1)}, f32[1024,4,128]{0,2,1:T(8,128)}, f32[2,512,4,128]{3,1,0,2:T(8,128)}, s32[2]{0:T(128)S(1)}, /*i...) while((s32[]{:T(128)}, f32[1024,4,128]{0,2,1:T(8,128)S(1)}, ...), condition=%wide.region_28.29_spmd.clone, body=%wide.region_26.28_spmd.clone.sunk | while | flops 2720266752 | bytes 113318352 | solution.py:357
  3646.0 26.3 reduce-scatter.30.cloned.1.call-done
  3674.6 63.8 %reduce-scatter.32.cloned.1.call-done = bf16[1408,256]{1,0:T(8,128)(2,1)} async-done(((bf16[1408,2048]{1,0:T(8,128)(2,1)}), bf16[1408,256]{1,0:T(8,128)(2,1)}) %reduce-scatter.32.cloned.1.call-update) | async-done | bytes 720912 | tf_op jit(solution)/shard_map/reduce_scatter | solution.py:417
  3813.5 34.9 reduce-scatter.20.cloned.1.call-done
  3850.2 35.1 reduce-scatter.22.cloned.1.call-done
  3887.1 86.8 %reduce-scatter.18.cloned.1.call-done = f32[256,2048]{1,0:T(8,128)} async-done(((f32[1024,2048]{1,0:T(8,128)}), f32[256,2048]{1,0:T(8,128)}) %reduce-scatter.18.cloned.1.call-update) | async-done | bytes 2097168 | tf_op jit(solution)/shard_map/reduce_scatter | solution.py:151
  3976.0 40.5 all-reduce
  4023.2 79.2 %all-reduce.3.cloned.1.call-done = f32[2048,16]{0,1:T(8,128)} async-done(((f32[2048,16]{0,1:T(8,128)}), f32[2048,16]{0,1:T(8,128)}) %all-reduce.3.cloned.1.call-update) | async-done | bytes 131088 | tf_op jit(solution)/shard_map/psum | solution.py:425
  (436 shorter events, 858.7 us)
Async XLA Ops:
  7.2 1023.9 %copy-start = (bf16[2,352,2048]{2,1,0:T(8,128)(2,1)S(1)}, bf16[2,352,2048]{2,1,0:T(8,128)(2,1)}, u32[]{:S(2)}) copy-start(bf16[2,352,2048]{2,1,0:T(8,128)(2,1)} %param.45) | copy-start | bytes 8650756
  7.2 34.3 all-gather.18.cloned.1.call-start
  8.0 88.2 %all-gather.12.cloned.1.call-start = ((), (), s32[]{:S(2)}) async-start(), calls=%async_computation.15 | async-start | bytes 5242880 | tf_op jit(solution)/shard_map/all_gather | solution.py:148
  13.4 113.5 %all-gather.16.cloned.1.call-start = ((), (), s32[]{:S(2)}) async-start(), calls=%async_computation.17 | async-start | bytes 2359296 | tf_op jit(solution)/shard_map/all_gather | solution.py:165
  14.2 142.8 %all-gather.14.cloned.1.call-start = ((), (), s32[]{:S(2)}) async-start(), calls=%async_computation.16 | async-start | bytes 2359296 | tf_op jit(solution)/shard_map/all_gather | solution.py:164
  14.7 190.7 %all-gather.20.cloned.1.call-start = ((), (), s32[]{:S(2)}) async-start(), calls=%async_computation.19 | async-start | bytes 2359296 | tf_op jit(solution)/shard_map/all_gather | solution.py:167
  15.3 283.8 %reduce-scatter.12.cloned.1.call-start = ((), (), s32[]{:S(2)}) async-start(), calls=%async_computation.20 | async-start | bytes 10485760 | tf_op jit(solution)/shard_map/reduce_scatter | solution.py:151
  213.0 152.4 %all-gather.22.cloned.1.call-start = ((), (), s32[]{:S(2)}) async-start(), calls=%async_computation.21 | async-start | bytes 5242880 | tf_op jit(solution)/shard_map/all_gather | solution.py:148
  1095.4 689.0 %all-to-all-start.1 = ((bf16[1,2,3072,2048]{3,1,0,2:T(2,128)(2,1)}), bf16[1,2,3072,2048]{3,1,0,2:T(2,128)(2,1)}, u32[]{:S(2)}, u32[]{:S(2)}) async-start(bf16[1,2,3072,2048]{3,1,0,2:T(2,128)(2,1)} %copy.146), calls=%async_computation.2 | async-start | bytes 50331648 | tf_op jit(solution)/shard_map/all_to_all | solution.py:157
  1102.0 56.5 %all-gather.30.cloned.1.call-start = ((), (), s32[]{:S(2)}) async-start(), calls=%async_computation.26 | async-start | bytes 5242880 | tf_op jit(solution)/shard_map/all_gather | solution.py:148
  1102.7 194.1 %all-gather.26.cloned.1.call-start = ((), (), s32[]{:S(2)}) async-start(), calls=%async_computation.23 | async-start | bytes 6488064 | tf_op jit(solution)/shard_map/all_gather | solution.py:169
  1103.5 316.0 %all-gather.24.cloned.1.call-start = ((), (), s32[]{:S(2)}) async-start(), calls=%async_computation.22 | async-start | bytes 6488064 | tf_op jit(solution)/shard_map/all_gather | solution.py:168
  1104.1 561.9 %all-gather.28.cloned.1.call-start = ((), (), s32[]{:S(2)}) async-start(), calls=%async_computation.24 | async-start | bytes 6488064 | tf_op jit(solution)/shard_map/all_gather | solution.py:170
  1105.9 704.3 %copy-start.56 = (s32[1024]{0:T(1024)}, s32[1024]{0:T(1024)S(1)}, u32[]{:S(2)}) copy-start(s32[1024]{0:T(1024)S(1)} %get-tuple-element.398) | copy-start | bytes 12292
  1105.9 724.6 %copy-start.54 = (s32[1024]{0:T(1024)}, s32[1024]{0:T(1024)S(1)}, u32[]{:S(2)}) copy-start(s32[1024]{0:T(1024)S(1)} %get-tuple-element.399) | copy-start | bytes 12292
  1213.3 452.7 %copy-start.70 = (f32[1024]{0:T(1024)}, f32[1024]{0:T(1024)S(1)}, u32[]{:S(2)}) copy-start(f32[1024]{0:T(1024)S(1)} %add_divide_fusion.2) | copy-start | bytes 12292
  1213.3 698.1 %copy-start.24 = (f32[1024,16]{0,1:T(8,128)}, f32[1024,16]{0,1:T(8,128)S(1)}, u32[]{:S(2)}) copy-start(f32[1024,16]{0,1:T(8,128)S(1)} %fusion.81) | copy-start | bytes 196612
  2632.9 550.0 %all-to-all-start.3 = ((bf16[1,2,3072,2048]{3,1,0,2:T(2,128)(2,1)}), bf16[1,2,3072,2048]{3,1,0,2:T(2,128)(2,1)}, u32[]{:S(2)}, u32[]{:S(2)}) async-start(bf16[1,2,3072,2048]{3,1,0,2:T(2,128)(2,1)} %copy.150), calls=%async_computation.5 | async-start | bytes 50331648 | tf_op jit(solution)/shard_map/all_to_all | solution.py:157
  2639.4 751.9 %reduce-scatter.16.cloned.1.call-start = ((), (), s32[]{:S(2)}) async-start(), calls=%async_computation.27 | async-start | bytes 10485760 | tf_op jit(solution)/shard_map/reduce_scatter | solution.py:151
  2662.3 627.6 %copy-start.52 = (f32[1024]{0:T(1024)}, f32[1024]{0:T(1024)S(1)}, u32[]{:S(2)}) copy-start(f32[1024]{0:T(1024)S(1)} %multiply_reduce_fusion.4) | copy-start | bytes 12292
  2662.3 627.6 %copy-start.50 = (f32[1024]{0:T(1024)}, f32[1024]{0:T(1024)S(1)}, u32[]{:S(2)}) copy-start(f32[1024]{0:T(1024)S(1)} %subtract_multiply_fusion.3) | copy-start | bytes 12292
  3306.9 173.9 %reduce-scatter.14.cloned.1.call-start = ((), (), s32[]{:S(2)}) async-start(), calls=%async_computation.25 | async-start | bytes 10485760 | tf_op jit(solution)/shard_map/reduce_scatter | solution.py:151
  3322.1 216.4 %all-gather.32.cloned.1.call-start = ((), (), s32[]{:S(2)}) async-start(), calls=%async_computation.28 | async-start | bytes 5242880 | tf_op jit(solution)/shard_map/all_gather | solution.py:148
  3485.7 158.0 %reduce-scatter.28.cloned.1.call-start = ((), (), s32[]{:S(2)}) async-start(), calls=%async_computation.35 | async-start | bytes 6488064 | tf_op jit(solution)/shard_map/reduce_scatter | solution.py:411
  3496.9 175.4 %reduce-scatter.30.cloned.1.call-start = ((), (), s32[]{:S(2)}) async-start(), calls=%async_computation.36 | async-start | bytes 6488064 | tf_op jit(solution)/shard_map/reduce_scatter | solution.py:414
  3508.0 230.4 %reduce-scatter.32.cloned.1.call-start = ((), (), s32[]{:S(2)}) async-start(), calls=%async_computation.37 | async-start | bytes 6488064 | tf_op jit(solution)/shard_map/reduce_scatter | solution.py:417
  3518.8 279.7 %reduce-scatter.26.cloned.1.call-start = ((), (), s32[]{:S(2)}) async-start(), calls=%async_computation.33 | async-start | bytes 2359296 | tf_op jit(solution)/shard_map/reduce_scatter | solution.py:408
  3544.7 266.9 %reduce-scatter.24.cloned.1.call-start = ((), (), s32[]{:S(2)}) async-start(), calls=%async_computation.32 | async-start | bytes 2359296 | tf_op jit(solution)/shard_map/reduce_scatter | solution.py:405
  3605.3 243.1 %reduce-scatter.20.cloned.1.call-start = ((), (), s32[]{:S(2)}) async-start(), calls=%async_computation.30 | async-start | bytes 2359296 | tf_op jit(solution)/shard_map/reduce_scatter | solution.py:399
  3621.6 263.6 %reduce-scatter.22.cloned.1.call-start = ((), (), s32[]{:S(2)}) async-start(), calls=%async_computation.31 | async-start | bytes 2359296 | tf_op jit(solution)/shard_map/reduce_scatter | solution.py:402
  3630.5 343.3 %reduce-scatter.18.cloned.1.call-start = ((), (), s32[]{:S(2)}) async-start(), calls=%async_computation.29 | async-start | bytes 10485760 | tf_op jit(solution)/shard_map/reduce_scatter | solution.py:151
  3643.6 458.8 %all-reduce.3.cloned.1.call-start = ((), (), s32[]{:S(2)}) async-start(), calls=%async_computation.34 | async-start | bytes 262144 | tf_op jit(solution)/shard_map/psum | solution.py:425
  (94 other events, 3498.3 us)
Sparse Core Ops, SparseCore 0:
  9.7 31.7 all-gather.17
  43.9 52.1 all-gather.11
  97.8 29.0 all-gather.15
  128.4 28.5 all-gather.13
  158.4 30.3 all-gather.19
  213.1 85.9 reduce-scatter.11
  305.6 52.6 all-gather.21
  1105.4 53.0 all-gather.29
  1160.2 136.5 all-gather.25
  1298.4 121.0 all-gather.23
  1421.1 244.7 all-gather.27
  3307.0 84.2 reduce-scatter.15
  3394.4 86.3 reduce-scatter.13
  3485.8 52.6 all-gather.31
  3541.3 64.8 reduce-scatter.27
  3609.1 63.1 reduce-scatter.29
  3675.1 63.2 reduce-scatter.31
  3740.6 34.2 reduce-scatter.25
  3777.3 34.3 reduce-scatter.23
  3813.9 34.4 reduce-scatter.19
  3850.8 34.4 reduce-scatter.21
  3888.6 85.1 reduce-scatter.17
  3980.0 122.4 all-reduce.2
where the time goes:
time: 4120 us; the launch traced here: 4110 us
  waiting for transfers between devices  1830 us (44%)
  blocking collectives  1140 us (28%)
  local copies, waits for them, and re-layouts  534 us (13%)
  matrix products  436 us (11%)
  other arithmetic  137 us (3%)
    all_to_all x2, blocking collectives, to_experts(): lax.all_to_all(send_rows, 'fsdp', split_axis=0, concat_axis=2, tiled=True)  1100 us
    all_to_all x2, waiting for transfers between devices, from_experts(): lax.all_to_all(result_rows, 'fsdp', split_axis=2, concat_axis=0, tiled=True)  622 us
    reduce_scatter x4, waiting for transfers between devices, collect(): return lax.psum_scatter(partial_rows, 'sp', scatter_dimension=0, tiled=True)  328 us
    all_gather x1, waiting for transfers between devices, local(): lax.all_gather(shared_down, 'fsdp', axis=1, tiled=True)  235 us
    all_gather x4, waiting for transfers between devices, spread(): return lax.all_gather(local_rows, 'sp', axis=0, tiled=True)  126 us
    all_gather x1, waiting for transfers between devices, local(): lax.all_gather(shared_gate, 'fsdp', axis=0, tiled=True)  111 us
    all_gather x1, waiting for transfers between devices, local(): lax.all_gather(shared_up, 'fsdp', axis=0, tiled=True)  83.5 us
  transfers between devices with their start and end apart: 25, of which 21 were waited for; matrix products, arithmetic and copies ran while one was open for 12% of the time, Pallas kernels for 0%

commit v1 on v0

v1 whole, which is shorter than its diff:
```python
import functools

import jax
import jax.numpy as jnp
from jax import lax
from jax.experimental import pallas as pl
from jax.experimental.pallas import tpu as pltpu
from jax.sharding import PartitionSpec as P

HEAD = 128


EPSILON = 1e-06
ROPE_BASE = 1000000.0


def rms_scale(values):
    return lax.rsqrt(jnp.mean(values * values, axis=-1, keepdims=True) + EPSILON)


def norm_back(grad_rows, values, inverse_rms, gain_vector):
    weighted = grad_rows * gain_vector
    return inverse_rms * (
        weighted
        - values * inverse_rms * inverse_rms * jnp.mean(weighted * values, axis=-1, keepdims=True)
    )


def rope_tables(length, head_width):
    half_size = head_width // 2
    frequency = ROPE_BASE ** (-jnp.arange(half_size, dtype=jnp.float32) * 2.0 / head_width)
    angles = jnp.arange(length, dtype=jnp.float32)[:, None] * frequency[None, :]
    return (jnp.cos(angles)[:, None, :], jnp.sin(angles)[:, None, :])


def rotate(values, cosine, sine_table):
    half_size = values.shape[-1] // 2
    front_half = values[..., :half_size]
    back_half = values[..., half_size:]
    return jnp.concatenate(
        [
            front_half * cosine - back_half * sine_table,
            back_half * cosine + front_half * sine_table,
        ],
        axis=-1,
    )


def unrotate(gradient, cosine, sine_table):
    half_size = gradient.shape[-1] // 2
    front_half = gradient[..., :half_size]
    back_half = gradient[..., half_size:]
    return jnp.concatenate(
        [
            front_half * cosine + back_half * sine_table,
            back_half * cosine - front_half * sine_table,
        ],
        axis=-1,
    )


def silu_slope(activation):
    sigmoid_act = jax.nn.sigmoid(activation)
    return sigmoid_act * (1.0 + activation * (1.0 - sigmoid_act))


BF = jnp.bfloat16
F32 = jnp.float32


def dot(left, right):
    return jnp.dot(left, right, preferred_element_type=F32)


def swap(values, axis_name, mask):
    count = lax.axis_size(axis_name)
    return lax.ppermute(values, axis_name, [(i, i ^ mask) for i in range(count)])


def reorder(blocks, place):
    return jnp.stack(
        [lax.dynamic_index_in_dim(blocks, i ^ place, keepdims=False) for i in range(blocks.shape[0])]
    )


def after(value, other):
    return lax.optimization_barrier((value, other))[0]


MESH = pl.DeviceIdType.MESH


def flip(index, mask):
    bit = 1
    while bit <= mask:
        if mask & bit:
            index = index + bit - 2 * bit * lax.rem(lax.div(index, bit), 2)
        bit *= 2
    return index


def sp_bits():
    return ((1, 2), (2, 1))


def greet(barrier_partners):
    barrier = pltpu.get_barrier_semaphore()
    for axis, place in barrier_partners:
        pl.semaphore_signal(barrier, inc=1, device_id={axis: place}, device_id_type=MESH)
    pl.semaphore_wait(barrier, len(barrier_partners))


class Copies:
    def __init__(self, send_sems, recv_sems):
        self.send_sems, self.recv_sems, self.made = send_sems, recv_sems, []

    def start(self, source, target, axis, place):
        number = len(self.made)
        copy = pltpu.make_async_remote_copy(
            src_ref=source,
            dst_ref=target,
            send_sem=self.send_sems.at[number],
            recv_sem=self.recv_sems.at[number],
            device_id={axis: place},
            device_id_type=MESH,
        )
        copy.start()
        self.made.append(copy)
        return copy

    def finish(self):
        for copy in self.made:
            copy.wait_send()


def gather_kernel(pair_count, with_core, x_ref, out_ref, own_sem, send_sems, recv_sems):
    f, s = lax.axis_index("fsdp"), lax.axis_index("sp")
    middle = x_ref.shape[0] // 2
    partners = [("sp", flip(s, 1)), ("sp", flip(s, 2))]
    partners += [("fsdp", flip(f, 1))] if with_core else []
    partners += [("fsdp", flip(f, 2 * k)) for k in range(1, pair_count)]
    greet(partners)
    copies = Copies(send_sems, recv_sems)

    def row(k):
        return flip(f, 2 * k) if with_core else 0

    def block(k, j, h):
        return out_ref.at[row(k), flip(s, j), pl.ds(h * middle, middle)]

    def own(h):
        return x_ref.at[pl.ds(h * middle, middle)]

    local = pltpu.make_async_copy(x_ref, out_ref.at[row(0), s], own_sem)
    local.start()
    distant = {}
    for k in range(1, pair_count):
        for h in range(2):
            distant[k, h] = copies.start(own(h), block(0, 0, h), "fsdp", flip(f, 2 * k))
    near, crossing = {}, []

    def core(k, j, h):
        if with_core:
            source = own(h) if k == 0 and j == 0 else block(k, j, h)
            crossing.append(copies.start(source, block(k, j, h), "fsdp", flip(f, 1)))

    def first(k):
        for h in range(2):
            if k:
                distant[k, h].wait_recv()
            source = own(h) if k == 0 else block(k, 0, h)
            a, b = sp_bits()[h]
            near[k, a, h] = copies.start(source, block(k, 0, h), "sp", flip(s, a))
        for h in range(2):
            source = own(h) if k == 0 else block(k, 0, h)
            a, b = sp_bits()[h]
            near[k, b, h] = copies.start(source, block(k, 0, h), "sp", flip(s, b))
            core(k, 0, h)

    def second(k):
        for h in range(2):
            a, b = sp_bits()[h]
            near[k, a, h].wait_recv()
            near[k, 3, h] = copies.start(block(k, a, h), block(k, a, h), "sp", flip(s, b))
            core(k, a, h)

    def third(k):
        for h in range(2):
            a, b = sp_bits()[h]
            near[k, b, h].wait_recv()
            core(k, b, h)

    def fourth(k):
        for h in range(2):
            near[k, 3, h].wait_recv()
            core(k, 3, h)

    for step in range(pair_count + 2):
        if step < pair_count:
            first(step)
        if 0 <= step - 1 < pair_count:
            second(step - 1)
            third(step - 1)
        if 0 <= step - 2 < pair_count:
            fourth(step - 2)
    local.wait()
    for copy in crossing:
        copy.wait_recv()
    copies.finish()


def gather_call(rows, pair_count, with_core, number):
    height, width = rows.shape
    fsdp_count, sp_count = lax.axis_size("fsdp"), lax.axis_size("sp")
    count = 2 * (pair_count - 1) + 6 * pair_count + (8 * pair_count if with_core else 0)
    outer = fsdp_count if with_core else 1
    return pl.pallas_call(
        functools.partial(gather_kernel, pair_count, with_core),
        out_shape=jax.ShapeDtypeStruct((outer, sp_count, height, width), rows.dtype),
        in_specs=[pl.BlockSpec(memory_space=pl.ANY)],
        out_specs=pl.BlockSpec(memory_space=pl.ANY),
        scratch_shapes=[
            pltpu.SemaphoreType.DMA,
            pltpu.SemaphoreType.DMA((count,)),
            pltpu.SemaphoreType.DMA((count,)),
        ],
        compiler_params=pltpu.CompilerParams(collective_id=number, has_side_effects=True),
    )(rows)


def scatter_kernel(
    pair_count, with_core, p_ref, out_ref, held, loads, came, last, far, load_sems, send_sems, recv_sems
):
    f, s = lax.axis_index("fsdp"), lax.axis_index("sp")
    middle = held.shape[3]
    partners = [("sp", flip(s, 1)), ("sp", flip(s, 2))]
    partners += [("fsdp", flip(f, 1))] if with_core else []
    partners += [("fsdp", flip(f, 2 * k)) for k in range(1, pair_count)]
    greet(partners)
    copies = Copies(send_sems, recv_sems)
    order = list(range(pair_count))[::-1]

    def rows_of(k, h):
        return p_ref.at[flip(f, 2 * k) if with_core else 0, :, pl.ds(h * middle, middle)]

    crossing, loading = {}, {}
    if with_core:
        for k in order:
            for h in range(2):
                source = p_ref.at[flip(flip(f, 2 * k), 1), :, pl.ds(h * middle, middle)]
                crossing[k, h] = copies.start(source, held.at[k, h], "fsdp", flip(f, 1))

    def load(k):
        for h in range(2):
            target = loads.at[k % 2, h] if with_core else held.at[k, h]
            loading[k, h] = pltpu.make_async_copy(rows_of(k, h), target, load_sems.at[k % 2, h])
            loading[k, h].start()

    def add(target, source):
        def body(n, _):
            part = block_of(n, 16)
            target[part, :] = (target[part, :].astype(F32) + source[part, :].astype(F32)).astype(BF)
            return 0

        lax.fori_loop(0, middle // 16, body, 0)

    near, late, distant = {}, {}, {}

    def first(n):
        k = order[n]
        if with_core and n + 1 < pair_count:
            load(order[n + 1])
        for h in range(2):
            loading[k, h].wait()
            a, b = sp_bits()[h]
            if with_core:
                crossing[k, h].wait_recv()
            for i, j in enumerate((a, 3)):
                piece = held.at[k, h, flip(s, j)]
                if with_core:
                    add(piece, loads.at[k % 2, h, flip(s, j)])
                near[k, h, i] = copies.start(piece, came.at[k, h, i], "sp", flip(s, a))
        if with_core:
            for h in range(2):
                a, b = sp_bits()[h]
                for j in (0, b):
                    add(held.at[k, h, flip(s, j)], loads.at[k % 2, h, flip(s, j)])

    def second(n):
        k = order[n]
        for h in range(2):
            a, b = sp_bits()[h]
            near[k, h, 1].wait_recv()
            piece = held.at[k, h, flip(s, b)]
            add(piece, came.at[k, h, 1])
            late[k, h] = copies.start(piece, last.at[k, h], "sp", flip(s, b))
        for h in range(2):
            near[k, h, 0].wait_recv()
            add(held.at[k, h, s], came.at[k, h, 0])

    def third(n):
        k = order[n]
        for h in range(2):
            late[k, h].wait_recv()
            piece = held.at[k, h, s]
            add(piece, last.at[k, h])
            if k:
                distant[k, h] = copies.start(piece, far.at[k - 1, h], "fsdp", flip(f, 2 * k))

    load(order[0])
    for step in range(pair_count + 2):
        if step < pair_count:
            first(step)
        if 0 <= step - 1 < pair_count:
            second(step - 1)
        if 0 <= step - 2 < pair_count:
            third(step - 2)
    for h in range(2):
        for k in range(1, pair_count):
            distant[k, h].wait_recv()

        def total(n, _):
            part = block_of(n, 16)
            value = held[0, h, s, part, :].astype(F32)
            for k in range(1, pair_count):
                value = value + far[k - 1, h, part, :].astype(F32)
            out_ref[pl.ds(pl.multiple_of(h * middle + n * 16, 16), 16), :] = value
            return 0

        lax.fori_loop(0, middle // 16, total, 0)
    copies.finish()


def scatter_call(blocks, pair_count, with_core, number):
    _, sp_count, height, width = blocks.shape
    middle = height // 2
    count = 6 * pair_count + 2 * (pair_count - 1) + (2 * pair_count if with_core else 0)
    used = 2 * pair_count * (sp_count + 3) + (4 * sp_count if with_core else 0) + 2 * pair_count
    return pl.pallas_call(
        functools.partial(scatter_kernel, pair_count, with_core),
        out_shape=jax.ShapeDtypeStruct((height, width), F32),
        in_specs=[pl.BlockSpec(memory_space=pl.ANY)],
        out_specs=pl.BlockSpec(memory_space=pltpu.VMEM),
        scratch_shapes=[
            pltpu.VMEM((pair_count, 2, sp_count, middle, width), BF),
            pltpu.VMEM((2, 2, sp_count if with_core else 1, middle if with_core else 16, width), BF),
            pltpu.VMEM((pair_count, 2, 2, middle, width), BF),
            pltpu.VMEM((pair_count, 2, middle, width), BF),
            pltpu.VMEM((max(pair_count - 1, 1), 2, middle if pair_count > 1 else 16, width), BF),
            pltpu.SemaphoreType.DMA((2, 2)),
            pltpu.SemaphoreType.DMA((count,)),
            pltpu.SemaphoreType.DMA((count,)),
        ],
        compiler_params=pltpu.CompilerParams(
            collective_id=number,
            has_side_effects=True,
            vmem_limit_bytes=min(60 * 1024 * 1024, (2 * used * middle + 4 * height) * width + (8 << 20)),
        ),
    )(blocks)


def nt_dot(left, right):
    return lax.dot_general(left, right, (((1,), (1,)), ((), ())), preferred_element_type=F32)


def silu_pair(values):
    gate = jax.nn.sigmoid(values)
    return values * gate, gate * (1.0 + values * (1.0 - gate))


def block_of(index, size):
    return pl.ds(pl.multiple_of(index * size, size), size)


def moe_kernel(
    hidden,
    expert_count,
    share,
    x_ref,
    dm_ref,
    slot_ref,
    col_ref,
    own_ref,
    wgu_ref,
    wd_ref,
    sgu_ref,
    sd_ref,
    mixer_ref,
    dout_ref,
    rows_ref,
    drows_ref,
    act_ref,
    dgu_ref,
    sact_ref,
    dsgu_ref,
    pick,
    gu,
    y_all,
    dx_all,
    put,
    sgu,
):
    step = pl.program_id(1)
    experts, width, both = wgu_ref.shape
    hp = both // 2
    shared_pad = sd_ref.shape[0]
    capacity = pick.shape[0]
    length = x_ref.shape[1]
    tile = 512
    span = 64
    low = hidden // 128 * 128

    @pl.when(step < experts)
    def _():
        e = step
        slots = lax.broadcasted_iota(jnp.int32, (capacity, length), 0)
        pick[...] = jnp.where(slot_ref[0, pl.ds(e, 1), :] == slots, 1.0, 0.0).astype(BF)

        def take(n, _):
            cols = block_of(n, tile)
            rows_ref[0, 0, :, cols] = dot(pick[...], x_ref[0, :, cols]).astype(BF)
            drows_ref[0, 0, :, cols] = dot(pick[...], dm_ref[0, :, cols]).astype(BF)
            return 0

        lax.fori_loop(0, width // tile, take, 0)
        gu[:, : 2 * hp] = dot(rows_ref[0, 0], wgu_ref[e])
        gu[:, 2 * hp :] = nt_dot(drows_ref[0, 0], wd_ref[e])

        def middle(n, _):
            part = block_of(n, span)
            g, u, d = gu[part, :hp], gu[part, hp : 2 * hp], gu[part, 2 * hp :]
            lane = lax.broadcasted_iota(jnp.int32, (span, 128), 1) + low
            inside = (lane >= hidden) & (lane < hidden + expert_count)
            logits = jnp.where(inside, g[:, low : low + 128], -1e30)
            exponent = jnp.exp(logits - jnp.max(logits, axis=-1, keepdims=True))
            prob = exponent / jnp.sum(exponent, axis=-1, keepdims=True)
            own = own_ref[pl.ds(e, 1), :]
            gate = jnp.sum(prob * own, axis=-1, keepdims=True)
            s, slope = silu_pair(g)
            scaled = gate * (s * u)
            act_ref[0, 0, part, :] = scaled.astype(BF)
            pull = jnp.sum(scaled * d, axis=-1, keepdims=True)
            d = d * gate
            dg = d * u * slope
            extra = pull * jnp.where(inside, own - prob, 0.0)
            dgu_ref[0, 0, part, :hp] = dg.astype(BF)
            dgu_ref[0, 0, part, low : low + 128] = (dg[:, low : low + 128] + extra).astype(BF)
            dgu_ref[0, 0, part, hp:] = (d * s).astype(BF)
            return 0

        lax.fori_loop(0, capacity // span, middle, 0)
        place = block_of(e, capacity)

        def back(n, _):
            cols = block_of(n, tile)
            y_all[place, cols] = dot(act_ref[0, 0], wd_ref[e, :, cols]).astype(BF)
            dx_all[place, cols] = nt_dot(dgu_ref[0, 0], wgu_ref[e, cols, :]).astype(BF)
            return 0

        lax.fori_loop(0, width // tile, back, 0)

    @pl.when(step >= experts)
    def _():
        rows = mixer_ref.shape[1]
        here = block_of(step - experts, rows)
        slots = lax.broadcasted_iota(jnp.int32, (rows, capacity), 1)
        for e in range(experts):
            put[:, e * capacity : (e + 1) * capacity] = jnp.where(
                col_ref[0, :, e : e + 1] == slots, 1.0, 0.0
            ).astype(BF)
        sgu[:, : 2 * shared_pad] = dot(x_ref[0, here, :], sgu_ref[...])
        sgu[:, 2 * shared_pad :] = nt_dot(dm_ref[0, here, :], sd_ref[...])

        def middle(n, _):
            part = block_of(n, span)
            g, u = sgu[part, :shared_pad], sgu[part, shared_pad : 2 * shared_pad]
            d = sgu[part, 2 * shared_pad :]
            mixing = lax.broadcasted_iota(jnp.int32, (span, shared_pad), 1) == share
            switch = jax.nn.sigmoid(
                jnp.sum(jnp.where(mixing, g, 0.0), axis=-1, keepdims=True)
            )
            s, slope = silu_pair(g)
            scaled = switch * (s * u)
            sact_ref[0, part, :] = scaled.astype(BF)
            pull = jnp.sum(scaled * d, axis=-1, keepdims=True) * (1.0 - switch)
            d = d * switch
            dsgu_ref[0, part, :shared_pad] = jnp.where(mixing, pull, d * u * slope).astype(BF)
            dsgu_ref[0, part, shared_pad:] = (d * s).astype(BF)
            return 0

        lax.fori_loop(0, rows // span, middle, 0)

        def finish(n, _):
            cols = block_of(n, tile)
            mixer_ref[0, :, cols] = (
                dot(put[...], y_all[:, cols]) + dot(sact_ref[0], sd_ref[:, cols])
            ).astype(BF)
            dout_ref[0, :, cols] = (
                dot(put[...], dx_all[:, cols]) + nt_dot(dsgu_ref[0], sgu_ref[cols, :])
            ).astype(BF)
            return 0

        lax.fori_loop(0, width // tile, finish, 0)


def moe_call(rows, d_rows, codes, own, weights, sizes):
    hidden, expert_count, share, capacity = sizes
    wide_gu, wide_down, shared_gu, shared_down = weights
    seqs, length, width = rows.shape
    experts, _, both = wide_gu.shape
    hp = both // 2
    shared_pad = shared_down.shape[0]
    token_rows = min(512, length)
    token_steps = length // token_rows
    last = experts - 1

    def fixed(array):
        return pl.BlockSpec(
            array.shape, lambda s, i: (0,) * array.ndim, pipeline_mode=pl.Buffered(1)
        )

    def token_block(columns):
        return pl.BlockSpec(
            (1, token_rows, columns), lambda s, i: (s, jnp.maximum(i - experts, 0), 0)
        )

    def slot_block(columns):
        return pl.BlockSpec(
            (1, 1, capacity, columns), lambda s, i: (jnp.minimum(i, last), s, 0, 0)
        )

    def token_out(columns):
        return jax.ShapeDtypeStruct((seqs, length, columns), BF)

    def slot_out(columns):
        return jax.ShapeDtypeStruct((experts, seqs, capacity, columns), BF)

    slots = experts * capacity
    flops = seqs * 2 * (
        slots * width * (2 * length + 3 * both) + length * width * (2 * slots + 6 * shared_pad)
    )
    return pl.pallas_call(
        functools.partial(moe_kernel, hidden, expert_count, share),
        grid=(seqs, experts + token_steps),
        in_specs=[
            pl.BlockSpec((1, length, width), lambda s, i: (s, 0, 0)),
            pl.BlockSpec((1, length, width), lambda s, i: (s, 0, 0)),
            pl.BlockSpec((1, experts, length), lambda s, i: (s, 0, 0)),
            token_block(experts),
            fixed(own),
            fixed(wide_gu),
            fixed(wide_down),
            fixed(shared_gu),
            fixed(shared_down),
        ],
        out_specs=[
            token_block(width),
            token_block(width),
            slot_block(width),
            slot_block(width),
            slot_block(hp),
            slot_block(both),
            token_block(shared_pad),
            token_block(2 * shared_pad),
        ],
        out_shape=[
            token_out(width),
            token_out(width),
            slot_out(width),
            slot_out(width),
            slot_out(hp),
            slot_out(both),
            token_out(shared_pad),
            token_out(2 * shared_pad),
        ],
        scratch_shapes=[
            pltpu.VMEM((capacity, length), BF),
            pltpu.VMEM((capacity, 3 * hp), F32),
            pltpu.VMEM((slots, width), BF),
            pltpu.VMEM((slots, width), BF),
            pltpu.VMEM((token_rows, slots), BF),
            pltpu.VMEM((token_rows, 3 * shared_pad), F32),
        ],
        compiler_params=pltpu.CompilerParams(
            dimension_semantics=("arbitrary", "arbitrary"), vmem_limit_bytes=60 * 1024 * 1024
        ),
        cost_estimate=pl.CostEstimate(
            flops=flops, bytes_accessed=seqs * 24 * length * width, transcendentals=0
        ),
    )(rows, d_rows, codes, codes.transpose(0, 2, 1), own, *weights)


def moe_grads(rows, d_rows, slot_rows, slot_d_rows, act, d_gu, s_act, d_sgu):
    def flat(array):
        return array.reshape(array.shape[0], -1, array.shape[-1])

    def tokens_of(array):
        return array.reshape(-1, array.shape[-1])

    return (
        jnp.einsum("ecd,ecf->edf", flat(slot_rows), flat(d_gu), preferred_element_type=F32),
        jnp.einsum("ecf,ecd->efd", flat(act), flat(slot_d_rows), preferred_element_type=F32),
        dot(tokens_of(rows).T, tokens_of(d_sgu)),
        dot(tokens_of(d_rows).T, tokens_of(s_act)),
    )


def pad_last(array, size):
    return jnp.pad(array, [(0, 0)] * (array.ndim - 1) + [(0, size - array.shape[-1])])


def round_up(value, unit):
    return -(-value // unit) * unit


def local(
    tokens,
    segments,
    routes,
    cotangent,
    gain_attn,
    w_query,
    w_key,
    w_value,
    bias_query,
    bias_key,
    bias_value,
    w_out,
    gain_mlp,
    router,
    mix_gate,
    shared_gate,
    shared_up,
    shared_down,
    expert_gate,
    expert_up,
    expert_down,
):
    fsdp_count = lax.axis_size("fsdp")
    sp_count = lax.axis_size("sp")
    sp_place = lax.axis_index("sp")
    fsdp_place = lax.axis_index("fsdp")
    pair_count = fsdp_count // 2
    tok_count = tokens.shape[0]
    seq_len = segments.shape[0]
    width = tokens.shape[1]
    top_count = routes.shape[1]
    expert_count = router.shape[1]
    local_experts = expert_gate.shape[0]
    capacity = 3 * seq_len * top_count // (2 * expert_count)
    local_heads = w_query.shape[1] // HEAD
    head_width = w_query.shape[1]
    row_block = min(512, seq_len)
    block_count = seq_len // row_block
    score_scale = HEAD ** (-0.5)
    own_segments = lax.dynamic_slice_in_dim(segments, sp_place * tok_count, tok_count)
    live_rows = (own_segments >= 0).astype(F32)[:, None]
    position = jnp.arange(seq_len, dtype=jnp.int32)
    cosine, sine_table = rope_tables(seq_len, HEAD)
    whole_axes = ("fsdp", "sp")
    own_kernels = sp_count == 4 and pair_count == 4

    def spread(local_rows, number):
        if not own_kernels:
            return lax.all_gather(local_rows, "sp", axis=0, tiled=True)
        return gather_call(local_rows, 1, False, number).reshape(seq_len, width)

    def collect(partial_rows, number):
        partial_rows = partial_rows.astype(BF)
        if not own_kernels:
            rows = lax.psum_scatter(partial_rows, "sp", scatter_dimension=0, tiled=True)
            return rows.astype(F32)
        blocks = partial_rows.reshape(1, sp_count, tok_count, width)
        return scatter_call(blocks, 1, False, number)

    def home(parts, number):
        return scatter_call(
            parts.reshape(fsdp_count, sp_count, tok_count, width), pair_count, True, number
        )

    inputs = tokens.astype(F32)
    attn_rms = rms_scale(inputs)
    gain_one = gain_attn.astype(F32)
    normed_attn = spread((inputs * attn_rms * gain_one).astype(BF), 1)
    full_qkv = lax.all_gather(
        jnp.concatenate([w_query, w_key, w_value], 1), "fsdp", axis=0, tiled=True
    )
    full_out = lax.all_gather(after(w_out, full_qkv), "fsdp", axis=1, tiled=True)
    upstream = cotangent.astype(F32)
    d_mixer = after((live_rows * upstream).astype(BF), full_out)
    if own_kernels:
        all_d_rows = lax.all_gather(d_mixer, whole_axes, axis=0, tiled=True)
        all_d_rows = all_d_rows.reshape(fsdp_count, seq_len, width)
    share = shared_gate.shape[1] // fsdp_count
    packed = jnp.concatenate(
        [
            shared_gate.reshape(-1, fsdp_count, share),
            shared_up.reshape(-1, fsdp_count, share),
            shared_down.T.reshape(-1, fsdp_count, share),
        ],
        2,
    ).transpose(1, 0, 2)
    packed = lax.all_to_all(
        after(packed, full_qkv), "fsdp", split_axis=0, concat_axis=0, tiled=True
    ).reshape(width, 3 * share)
    hidden_units = expert_gate.shape[2]
    hp = round_up(hidden_units + expert_count, 128)
    shared_pad = round_up(share + 1, 128)
    experts_like = jnp.broadcast_to(router, (local_experts, width, expert_count))
    wide_gu = jnp.concatenate(
        [
            pad_last(jnp.concatenate([expert_gate, experts_like], 2), hp),
            pad_last(expert_up, hp),
        ],
        2,
    )
    wide_down = jnp.pad(expert_down, ((0, 0), (0, hp - hidden_units), (0, 0)))
    shared_gu = jnp.concatenate(
        [
            pad_last(jnp.concatenate([packed[:, :share], mix_gate[:, None]], 1), shared_pad),
            pad_last(packed[:, share : 2 * share], shared_pad),
        ],
        1,
    )
    shared_down_rows = pad_last(packed[:, 2 * share :], shared_pad).T
    all_routes = routes.T[None]
    bit = 1
    while bit < fsdp_count:
        all_routes = jnp.concatenate([all_routes, swap(all_routes, "fsdp", bit)], 0)
        bit *= 2
    all_routes = reorder(all_routes, fsdp_place)
    first_expert = fsdp_place * local_experts
    wanted = first_expert + jnp.arange(local_experts, dtype=jnp.int32)
    named = jnp.any(all_routes[:, None] == wanted[None, :, None, None], axis=2)
    tally = jnp.cumsum(named.astype(jnp.int32), axis=2) - 1
    codes = jnp.where(named, tally, -1)
    lane = jnp.arange(128, dtype=jnp.int32)[None, :] + hidden_units // 128 * 128 - hidden_units
    own = (lane == wanted[:, None]).astype(F32)

    normed_attn = after(normed_attn, (codes, wide_gu, wide_down))
    qkv_lin = dot(normed_attn, full_qkv)
    query_lin = qkv_lin[:, :head_width] + bias_query.astype(F32)
    key_lin = qkv_lin[:, head_width : 2 * head_width] + bias_key.astype(F32)
    value_rows = (
        (qkv_lin[:, 2 * head_width :] + bias_value.astype(F32))
        .astype(BF)
        .reshape(seq_len, local_heads, HEAD)
    )
    query_rot = rotate(query_lin.reshape(seq_len, local_heads, HEAD), cosine, sine_table).astype(BF)
    key_rot = rotate(key_lin.reshape(seq_len, local_heads, HEAD), cosine, sine_table).astype(BF)

    def block_scores(block_index):
        offset = block_index * row_block
        query_block = lax.dynamic_slice_in_dim(query_rot, offset, row_block)
        raw_scores = (
            jnp.einsum("qhd,khd->hqk", query_block, key_rot, preferred_element_type=jnp.float32)
            * score_scale
        )
        seg_block = lax.dynamic_slice_in_dim(segments, offset, row_block)
        pos_block = offset + jnp.arange(row_block, dtype=jnp.int32)
        allowed = (
            (seg_block[:, None] == segments[None, :]) & (position[None, :] <= pos_block[:, None])
        )[None]
        return (query_block, raw_scores, allowed)

    def attend_block(block_index):
        score_parts = block_scores(block_index)
        raw_scores = score_parts[1]
        allowed = score_parts[2]
        row_max = jnp.max(jnp.where(allowed, raw_scores, -jnp.inf), axis=-1, keepdims=True)
        exponent = jnp.exp(jnp.where(allowed, raw_scores - row_max, -jnp.inf))
        row_total = jnp.sum(exponent, axis=-1, keepdims=True)
        probability = (exponent / row_total).astype(jnp.bfloat16)
        attended_block = jnp.einsum(
            "hqk,khd->qhd", probability, value_rows, preferred_element_type=jnp.float32
        ).astype(jnp.bfloat16)
        return (attended_block, (row_max + jnp.log(row_total))[..., 0])

    attended, log_total = lax.map(attend_block, jnp.arange(block_count))
    attended = attended.reshape(seq_len, local_heads * HEAD)
    attn_out = collect(dot(attended, full_out), 2)
    hidden = inputs + live_rows * attn_out
    mlp_rms = rms_scale(hidden)
    gain_two = gain_mlp.astype(F32)
    normed_mlp = (hidden * mlp_rms * gain_two).astype(BF)
    weights = (wide_gu, wide_down, shared_gu, shared_down_rows)
    sizes = (hidden_units, expert_count, share, capacity)
    if own_kernels:
        all_rows = gather_call(normed_mlp, pair_count, True, 3)
        all_rows = all_rows.reshape(fsdp_count, seq_len, width)
        mixer_parts, d_parts, *kept = moe_call(all_rows, all_d_rows, codes, own, weights, sizes)
        d_mlp_own = home(d_parts, 4)
    else:
        seq_rows, seq_d_rows, near_codes = spread(normed_mlp, 3), spread(d_mixer, 4), reorder(codes, fsdp_place)
        mixer_sum = d_sum = jnp.zeros((seq_len, width), F32)
        grads = None
        together = max(1, fsdp_count // 4)
        for start in range(0, fsdp_count, together):
            some = range(start, start + together)
            all_rows = jnp.stack([swap(seq_rows, "fsdp", m) for m in some])
            all_d_rows = jnp.stack([swap(seq_d_rows, "fsdp", m) for m in some])
            mixer_parts, d_parts, *kept = moe_call(
                all_rows, all_d_rows, near_codes[start : start + together], own, weights, sizes
            )
            more = moe_grads(all_rows, all_d_rows, *kept)
            grads = more if grads is None else jax.tree.map(jnp.add, grads, more)
            for n, m in enumerate(some):
                mixer_sum = mixer_sum + swap(mixer_parts[n], "fsdp", m).astype(F32)
                d_sum = d_sum + swap(d_parts[n], "fsdp", m).astype(F32)
            grads, mixer_sum, d_sum, seq_rows = lax.optimization_barrier(
                (grads, mixer_sum, d_sum, seq_rows)
            )
        mixer_out, d_mlp_own = collect(mixer_sum, 7), collect(d_sum, 8)
    grad_gain_two = jnp.sum(d_mlp_own * hidden * mlp_rms, axis=0)
    d_hidden = upstream + norm_back(d_mlp_own, hidden, mlp_rms, gain_two)
    d_attn = spread((live_rows * d_hidden).astype(BF), 5)
    grad_out = dot(attended.T, d_attn)
    d_attended = dot(d_attn, full_out.T).astype(BF).reshape(seq_len, local_heads, HEAD)

    def attend_back(carry_in, block_index):
        key_grad, value_grad = carry_in
        query_block, raw_scores, allowed = block_scores(block_index)
        offset = block_index * row_block
        log_block = lax.dynamic_index_in_dim(log_total, block_index, keepdims=False)
        prob_full = jnp.exp(jnp.where(allowed, raw_scores - log_block[..., None], -jnp.inf))
        prob_low = prob_full.astype(jnp.bfloat16)
        grad_block = lax.dynamic_slice_in_dim(d_attended, offset, row_block)
        d_prob = jnp.einsum(
            "qhd,khd->hqk", grad_block, value_rows, preferred_element_type=jnp.float32
        )
        d_scores = (
            prob_full * (d_prob - jnp.sum(prob_full * d_prob, axis=-1, keepdims=True))
        ).astype(jnp.bfloat16)
        query_grad = (
            jnp.einsum("hqk,khd->qhd", d_scores, key_rot, preferred_element_type=jnp.float32)
            * score_scale
        )
        key_grad = (
            key_grad
            + jnp.einsum("hqk,qhd->khd", d_scores, query_block, preferred_element_type=jnp.float32)
            * score_scale
        )
        value_grad = value_grad + jnp.einsum(
            "hqk,qhd->khd", prob_low, grad_block, preferred_element_type=jnp.float32
        )
        return ((key_grad, value_grad), query_grad)

    zero_grad = jnp.zeros((seq_len, local_heads, HEAD), jnp.float32)
    (key_grad, value_grad), query_grad = lax.scan(
        attend_back, (zero_grad, zero_grad), jnp.arange(block_count)
    )
    query_grad = query_grad.reshape(seq_len, local_heads, HEAD)
    d_query = (
        unrotate(query_grad, cosine, sine_table)
        .reshape(seq_len, local_heads * HEAD)
        .astype(jnp.bfloat16)
    )
    d_key = (
        unrotate(key_grad, cosine, sine_table)
        .reshape(seq_len, local_heads * HEAD)
        .astype(jnp.bfloat16)
    )
    d_value = value_grad.reshape(seq_len, local_heads * HEAD).astype(jnp.bfloat16)
    d_qkv = jnp.concatenate([d_query, d_key, d_value], 1)
    d_normed_attn = dot(d_qkv, full_qkv.T)
    d_attn_own = collect(d_normed_attn, 6)
    grad_qkv = dot(normed_attn.T, d_qkv)
    bias_grads = jnp.sum(d_qkv.astype(F32), axis=0)
    grad_gain_one = jnp.sum(d_attn_own * inputs * attn_rms, axis=0)
    grad_tokens = d_hidden + norm_back(d_attn_own, inputs, attn_rms, gain_one)
    grad_qkv = lax.psum_scatter(
        grad_qkv.astype(BF), "fsdp", scatter_dimension=0, tiled=True
    ).astype(F32)
    grad_w_out = lax.psum_scatter(
        grad_out.astype(BF), "fsdp", scatter_dimension=1, tiled=True
    ).astype(F32)
    if own_kernels:
        mixer_out = home(after(mixer_parts, d_attn_own), 7)
        grads = moe_grads(all_rows, all_d_rows, *kept)
    output = (hidden + live_rows * mixer_out).astype(BF)
    grad_gu, grad_ed, grad_sgu, grad_sdown_t = grads
    grad_sdown_t = grad_sdown_t[:, :share]
    grad_expert_gate = grad_gu[..., :hidden_units]
    grad_expert_up = grad_gu[..., hp : hp + hidden_units]
    grad_expert_down = grad_ed[:, :hidden_units]
    grad_router = jnp.sum(grad_gu[..., hidden_units : hidden_units + expert_count], axis=0)
    grad_mix = grad_sgu[:, share]
    packed_grad = jnp.concatenate(
        [grad_sgu[:, :share], grad_sgu[:, shared_pad : shared_pad + share], grad_sdown_t], 1
    ).astype(BF)
    packed_grad = lax.all_to_all(
        packed_grad.reshape(fsdp_count, -1, 3 * share), "fsdp", split_axis=0, concat_axis=0, tiled=True
    ).transpose(1, 0, 2)
    grad_shared_gate, grad_shared_up, grad_shared_down = (
        packed_grad[:, :, n * share : (n + 1) * share].reshape(-1, fsdp_count * share).astype(F32)
        for n in range(3)
    )
    sum_router, sum_mix, sum_gain_two = lax.psum((grad_router, grad_mix, grad_gain_two), whole_axes)
    sum_gain_one = lax.psum(grad_gain_one, whole_axes)
    own_bias = lax.psum(bias_grads, "fsdp")
    return (
        output,
        grad_tokens,
        sum_gain_one,
        grad_qkv[:, :head_width],
        grad_qkv[:, head_width : 2 * head_width],
        grad_qkv[:, 2 * head_width :],
        own_bias[:head_width],
        own_bias[head_width : 2 * head_width],
        own_bias[2 * head_width :],
        grad_w_out,
        sum_gain_two,
        sum_router,
        sum_mix,
        grad_shared_gate,
        grad_shared_up,
        grad_shared_down.T,
        grad_expert_gate,
        grad_expert_up,
        grad_expert_down,
    )


def solution(mesh):
    return jax.shard_map(
        local,
        mesh=mesh,
        in_specs=(
            P(("fsdp", "sp"), None),
            P("fsdp"),
            P("fsdp", None),
            P(("fsdp", "sp"), None),
            P(),
            P("fsdp", "sp"),
            P("fsdp", "sp"),
            P("fsdp", "sp"),
            P("sp"),
            P("sp"),
            P("sp"),
            P("sp", "fsdp"),
            P(),
            P(),
            P(),
            P("fsdp", "sp"),
            P("fsdp", "sp"),
            P("sp", "fsdp"),
            P("fsdp", None, "sp"),
            P("fsdp", None, "sp"),
            P("fsdp", "sp", None),
        ),
        out_specs=(
            P(("fsdp", "sp"), None),
            P(("fsdp", "sp"), None),
            P(),
            P("fsdp", "sp"),
            P("fsdp", "sp"),
            P("fsdp", "sp"),
            P("sp"),
            P("sp"),
            P("sp"),
            P("sp", "fsdp"),
            P(),
            P(),
            P(),
            P("fsdp", "sp"),
            P("fsdp", "sp"),
            P("sp", "fsdp"),
            P("fsdp", None, "sp"),
            P("fsdp", None, "sp"),
            P("fsdp", "sp", None),
        ),
        check_vma=False,
    )
```

time: 4120 us -> 1660 us (0.40)
  waiting for transfers between devices: 1830 us -> 44.2 us
  Pallas kernels: 0 us -> 1170 us
  blocking collectives: 1140 us -> 54.5 us
  local copies, waits for them, and re-layouts: 534 us -> 77 us
  matrix products: 436 us -> 193 us
  other arithmetic: 137 us -> 81 us
    pallas_call x0 -> x8, Pallas kernels: none -> 1170 us  [the longest x4 442 us: scatter_call(): pl.pallas_call(functools.partial(scatter_kernel, pair_count, with_core),...]
    all_to_all x2 -> x0, blocking collectives: 1100 us -> none  [to_experts(): lax.all_to_all(send_rows, 'fsdp', split_axis=0, concat_axis=2, tiled=True)]
    all_to_all x2, waiting for transfers between devices: 622 us -> 0.01 us  [the longest x1 0.01 us: local(): lax.all_to_all(after(packed, full_qkv), 'fsdp', split_axis=0, concat_axis...]
    all_gather x11 -> x3, waiting for transfers between devices: 621 us -> 1.57 us  [the longest x1 1.57 us: local(): lax.all_gather(after(w_out, full_qkv), 'fsdp', axis=1, tiled=True)]
    reduce_scatter x11 -> x2, waiting for transfers between devices: 500 us -> 0.01 us  [the longest x1 0.01 us: local(): lax.psum_scatter(grad_out.astype(BF), 'fsdp', scatter_dimension=1, tiled=...]
    gather x10 -> x0, local copies, waits for them, and re-layouts: 261 us -> none  [the longest x4 81.5 us: local(): d_returned[destination[:, route_slot]].astype(jnp.float32)]
    dot_general x35 -> x10, matrix products: 395 us -> 136 us  [the longest x8 91.1 us: dot(): return jnp.dot(left, right, preferred_element_type=F32)]
    broadcast_in_dim x4 -> x2, local copies, waits for them, and re-layouts: 91.1 us -> 0.08 us  [the longest x1 0.07 us: local(): jnp.broadcast_to(router, (local_experts, width, expert_count))]
  transfers between devices with their start and end apart: 25 -> 11, of which waited for: 21 -> 3; matrix products, arithmetic and copies ran while one was open for 12% -> 18% of each run, Pallas kernels for 0% -> 35%
where the time goes in v1:
time: 1660 us
  Pallas kernels  1170 us (70%)
  matrix products  193 us (12%)
  other arithmetic  81 us (5%)
  local copies, waits for them, and re-layouts  77 us (5%)
  blocking collectives  54.5 us (3%)
  waiting for transfers between devices  44.2 us (3%)
    pallas_call x4, Pallas kernels, scatter_call(): pl.pallas_call(functools.partial(scatter_kernel, pair_count, with_core),...  442 us
    pallas_call x3, Pallas kernels, gather_call(): pl.pallas_call(functools.partial(gather_kernel, pair_count, with_core), o...  393 us
    pallas_call x1, Pallas kernels, moe_call(): pl.pallas_call(functools.partial(moe_kernel, hidden, expert_count, share)...  333 us
    dot_general x8, matrix products, dot(): return jnp.dot(left, right, preferred_element_type=F32)  91.1 us
    psum x1, waiting for transfers between devices, local(): lax.psum((grad_router, grad_mix, grad_gain_two), whole_axes)  39.2 us
    psum x1, blocking collectives, local(): sum_gain_one = lax.psum(grad_gain_one, whole_axes)  37.5 us
  transfers between devices with their start and end apart: 11, of which 3 were waited for; matrix products, arithmetic and copies ran while one was open for 18% of the time, Pallas kernels for 35%

profile of v1, /device:TPU:0, one launch (start us, length us, event | category | flops | bytes accessed | tf_op | source)
XLA Modules:
  0.0 1655.2 jit_solution(2744758868550397406)
XLA Ops:
  9.9 4.6 copy.145
  14.8 4.7 copy.146
  33.3 37.9 %shard_map.348 = bf16[1,4,256,2048]{3,2,1,0:T(8,128)(2,1)} custom-call(bf16[256,2048]{1,0:T(8,128)(2,1)} %fusion.48.x_ref), custom_call_target="tpu_custom_call" | custom-call | tf_op jit(solution)/shard_map/pallas_call | solution.py:217
  94.0 10.2 fusion.79
  124.3 21.1 %while.28 = (s32[]{:T(128)}, bf16[2,512,4,128]{3,2,1,0:T(4,128)(2,1)}, f32[2,4,512]{2,1,0:T(4,128)S(1)}, s32[2]{0:T(128)S(1)}, s32[1024]{0:T(1024)S(1)}, /*index...) while((s32[]{:T(128)}, ...), condition=%wide.region_7.8_spmd.clone, body=%wide.region_4.7_spmd.clone.sunk | while | flops 1100741120 | bytes 31537856 | solution.py:779
  151.3 39.2 %shard_map.349 = f32[256,2048]{1,0:T(8,128)S(1)} custom-call(bf16[1,4,256,2048]{3,2,1,0:T(8,128)(2,1)S(1)} %bitcast.153), custom_call_target="tpu_custom_call" | custom-call | tf_op jit(solution)/shard_map/pallas_call | solution.py:339
  207.3 317.3 %shard_map.350 = bf16[8,4,256,2048]{3,2,1,0:T(8,128)(2,1)} custom-call(bf16[256,2048]{1,0:T(8,128)(2,1)} %multiply_convert_fusion.2.x_ref), custom_call_target="tpu_custom_call" | custom-call | tf_op jit(solution)/shard_map/pallas_call | solution.py:217
  530.7 332.8 %shard_map.351 = (bf16[8,1024,2048]{2,1,0:T(8,128)(2,1)}, bf16[8,1024,2048]{2,1,0:T(8,128)(2,1)}, bf16[2,8,384,2048]{3,2,1,0:T(8,128)(2,1)}, bf16[2,8,384,2048]{...) custom-call(bf16[8,1024,2048]{2,1,0:T(8,128)(2,1)} %bitcast.157, ...), custom_call_target="tpu_custom_call" | custom-call | flops 212600881152 | bytes 402653184 | tf_op jit(solution)/shard_map/pallas_call | solution.py:542
  863.6 183.0 %shard_map.352 = f32[256,2048]{1,0:T(8,128)S(1)} custom-call(bf16[8,4,256,2048]{3,2,1,0:T(8,128)(2,1)} %bitcast.160), custom_call_target="tpu_custom_call" | custom-call | tf_op jit(solution)/shard_map/pallas_call | solution.py:339
  1050.4 38.1 %shard_map.353 = bf16[1,4,256,2048]{3,2,1,0:T(8,128)(2,1)} custom-call(bf16[256,2048]{1,0:T(8,128)(2,1)} %multiply_convert_fusion.1.x_ref), custom_call_target="tpu_custom_call" | custom-call | tf_op jit(solution)/shard_map/pallas_call | solution.py:217
  1088.5 6.2 convolution_convert_fusion.3
  1094.9 6.3 convolution_convert_fusion.4
  1101.2 66.9 %while.29 = (s32[]{:T(128)}, f32[1024,4,128]{0,2,1:T(8,128)S(1)}, f32[1024,4,128]{0,2,1:T(8,128)}, f32[2,512,4,128]{3,1,0,2:T(8,128)}, s32[2]{0:T(128)S(1)}, /*i...) while((s32[]{:T(128)}, f32[1024,4,128]{0,2,1:T(8,128)S(1)}, ...), condition=%wide.region_12.13_spmd.clone, body=%wide.region_10.12_spmd.clone.sunk | while | flops 2720266752 | bytes 163650544 | solution.py:849
  1104.2 5.6 fusion.135
  1111.7 7.6 multiply_reduce_fusion.5
  1137.0 5.6 fusion.135
  1144.6 7.5 multiply_reduce_fusion.5
  1162.9 5.2 bitcast_add_fusion.5
  1170.3 6.3 add_convert_fusion.2
  1181.9 12.2 convolution_convert_fusion
  1194.1 17.7 %fusion.81 = bf16[2048,256]{0,1:T(8,128)(2,1)} fusion(bf16[8192,2048]{1,0:T(8,128)(2,1)} %all-gather.8.cloned.1.call-done, bf16[8192,256]{1,0:T(8,128)(2,1)} %bitcast.200), kind=kOutput, calls=%fused_computation.169 | convolution fusion | flops 8589934592 | bytes 38797312 | tf_op jit(solution)/shard_map/dot_general | solution.py:72
  1213.1 25.3 %fusion.78 = (bf16[2048,512]{0,1:T(8,128)(2,1)S(1)}, f32[2048,512]{0,1:T(8,128)}) fusion(bf16[8192,2048]{1,0:T(8,128)(2,1)} %bitcast.158, bf16[8192,512]{1,0:T(8,128)(2,1)} %bitcast.198), kind=kOutput, calls=%fused_computation.166 | convolution fusion | flops 17180917760 | bytes 48234496 | tf_op jit(solution)/shard_map/dot_general | solution.py:72
  1245.4 8.9 convolution_convert_fusion.1
  1254.3 38.7 %shard_map.354 = f32[256,2048]{1,0:T(8,128)S(1)} custom-call(bf16[1,4,256,2048]{3,2,1,0:T(8,128)(2,1)S(1)} %bitcast.152), custom_call_target="tpu_custom_call" | custom-call | tf_op jit(solution)/shard_map/pallas_call | solution.py:339
  1294.3 180.9 %shard_map.355 = f32[256,2048]{1,0:T(8,128)S(1)} custom-call(bf16[8,4,256,2048]{3,2,1,0:T(8,128)(2,1)} %bitcast.159), custom_call_target="tpu_custom_call" | custom-call | tf_op jit(solution)/shard_map/pallas_call | solution.py:339
  1477.1 16.9 %psum.36 = f32[1536]{0:T(1024)S(1)} all-reduce(f32[1536]{0:T(1024)S(1)} %convert_reduce_fusion), channel_id=1, replica_groups=mesh['fsdp'=8,'sp'=4] {'fsdp'}, use_global_device_ids=true, to_apply=%region_18.19 | all-reduce | flops 1536 | bytes 12288 | tf_op jit(solution)/shard_map/psum | solution.py:900
  1494.1 27.8 %fusion.80 = f32[2,2048,768]{1,2,0:T(8,128)} fusion(bf16[2,3072,2048]{2,1,0:T(8,128)(2,1)} %bitcast.196, bf16[2,3072,768]{2,1,0:T(8,128)(2,1)} %bitcast.197), kind=kOutput, calls=%fused_computation.168 | convolution fusion | flops 19327352832 | bytes 47185920 | tf_op jit(solution)/shard_map/ecd,ecf->edf/dot_general | solution.py:601
  1526.5 37.5 %all-reduce.6 = (f32[2048]{0:T(1024)}, f32[2048]{0:T(1024)}, f32[2048]{0:T(1024)}) all-reduce(f32[2048]{0:T(1024)S(1)} %get-tuple-element.353, f32[2048]{0:T(1024)S(1)} %copy-done.40, f32[2048]{0:T(1024)S(1)} %bitcast.191), channel_id=1, replica_groups=mesh['fsdp'=8,'sp'=4] {'fsdp','sp'}, use_global_device_ids=true, to_apply=%region_15.16 | all-reduce | flops 6144 | bytes 49152 | tf_op jit(solution)/shard_map/psum | solution.py:899
  1564.0 5.0 fusion.52
  1569.0 10.7 fusion.70
  1579.7 17.0 %fusion.42 = f32[2,352,2048]{2,1,0:T(8,128)} fusion(bf16[2,3072,2048]{2,1,0:T(8,128)(2,1)} %bitcast.195, bf16[2,3072,384]{2,1,0:T(8,128)(2,1)} %bitcast.199), kind=kOutput, calls=%fused_computation.57 | convolution fusion | flops 8858370048 | bytes 35651584 | tf_op jit(solution)/shard_map/ecf,ecd->efd/dot_general | solution.py:602
  1607.2 39.2 %all-reduce.9.cloned.1.call-done = f32[2048,16]{0,1:T(8,128)} async-done(((f32[2048,16]{0,1:T(8,128)}), f32[2048,16]{0,1:T(8,128)}) %all-reduce.9.cloned.1.call-update) | async-done | bytes 131088 | tf_op jit(solution)/shard_map/psum | solution.py:898
  (300 shorter events, 176.6 us)
Async XLA Ops:
  7.2 86.8 %all-gather.4.cloned.1.call-start = ((), (), s32[]{:S(2)}) async-start(), calls=%async_computation.4 | async-start | bytes 7077888 | tf_op jit(solution)/shard_map/all_gather | solution.py:685
  9.3 137.7 %all-gather.6.cloned.1.call-start = ((), (), s32[]{:S(2)}) async-start(), calls=%async_computation.5 | async-start | bytes 2359296 | tf_op jit(solution)/shard_map/all_gather | solution.py:688
  9.4 21.3 %collective-permute-start = (s32[1,4,1024]{2,1,0:T(4,128)S(1)}, s32[1,4,1024]{2,1,0:T(4,128)S(1)}, u32[]{:S(2)}, u32[]{:S(2)}) collective-permute-start(s32[1,4,1024]{2,1,0:T(4,128)S(1)} %bitcast.187), channel_id=1, source_target_pairs={{0,4},{4,0},{8,12},{12,8},{16,20},{20,16},{24,28},{28,24},{1,5},{5... | collective-permute-start | bytes 49160 | tf_op jit(solution)/shard_map/ppermute | solution.py:77
  9.9 16.7 %copy-start.35 = (f32[2048]{0:T(1024)}, f32[2048]{0:T(1024)S(1)}, u32[]{:S(2)}) copy-start(f32[2048]{0:T(1024)S(1)} %convert_element_type.138) | copy-start | bytes 24580
  30.7 42.7 %collective-permute-start.1 = (s32[2,4,1024]{2,1,0:T(4,128)S(1)}, s32[2,4,1024]{2,1,0:T(4,128)S(1)}, u32[]{:S(2)}, u32[]{:S(2)}) collective-permute-start(s32[2,4,1024]{2,1,0:T(4,128)S(1)} %pad_add_fusion.2), channel_id=1, source_target_pairs={{0,8},{4,12},{8,0},{12,4},{16,24},{20,28},{24,16},{28,20},{1,9},{5... | collective-permute-start | bytes 98312 | tf_op jit(solution)/shard_map/ppermute | solution.py:77
  33.3 157.3 %copy-start.46 = (f32[256]{0:T(256)}, f32[256]{0:T(256)S(1)}, u32[]{:S(2)}) copy-start(f32[256]{0:T(256)S(1)} %compare_convert_fusion.1) | copy-start | bytes 3076
  33.3 38.0 %copy-start.54 = (bf16[512]{0:T(512)(128)(2,1)S(1)}, bf16[512]{0:T(512)(128)(2,1)}, u32[]{:S(2)}) copy-start(bf16[512]{0:T(512)(128)(2,1)} %param.33) | copy-start | bytes 3076
  33.3 38.0 %copy-start.55 = (bf16[512]{0:T(512)(128)(2,1)S(1)}, bf16[512]{0:T(512)(128)(2,1)}, u32[]{:S(2)}) copy-start(bf16[512]{0:T(512)(128)(2,1)} %param.34) | copy-start | bytes 3076
  33.3 38.0 %copy-start.56 = (bf16[512]{0:T(512)(128)(2,1)S(1)}, bf16[512]{0:T(512)(128)(2,1)}, u32[]{:S(2)}) copy-start(bf16[512]{0:T(512)(128)(2,1)} %param.35) | copy-start | bytes 3076
  33.3 38.1 %copy-start.27 = (bf16[2,352,2048]{2,1,0:T(8,128)(2,1)S(1)}, bf16[2,352,2048]{2,1,0:T(8,128)(2,1)}, u32[]{:S(2)}) copy-start(bf16[2,352,2048]{2,1,0:T(8,128)(2,1)} %param.45) | copy-start | bytes 8650756
  73.4 6.0 collective-permute-start.2
  117.5 413.2 %all-gather.8.cloned.1.call-start = ((), (), s32[]{:S(2)}) async-start(), calls=%async_computation.6 | async-start | bytes 34603008 | tf_op jit(solution)/shard_map/all_gather | solution.py:692
  151.3 39.3 %copy-start.16 = (bf16[256,2048]{1,0:T(8,128)(2,1)S(1)}, bf16[256,2048]{1,0:T(8,128)(2,1)}, u32[]{:S(2)}) copy-start(bf16[256,2048]{1,0:T(8,128)(2,1)} %param.25) | copy-start | bytes 3145732
  151.3 39.3 %copy-start.19 = (bf16[256,2048]{1,0:T(8,128)(2,1)S(1)}, bf16[256,2048]{1,0:T(8,128)(2,1)}, u32[]{:S(2)}) copy-start(bf16[256,2048]{1,0:T(8,128)(2,1)} %param.28) | copy-start | bytes 3145732
  192.2 13.9 copy-start.12
  197.0 327.7 %all-to-all-start = ((bf16[8,256,528]{1,2,0:T(8,128)(2,1)}), bf16[8,256,528]{1,2,0:T(8,128)(2,1)}, u32[]{:S(2)}, u32[]{:S(2)}) async-start(bf16[8,256,528]{1,2,0:T(8,128)(2,1)} %maximum_bitcast_fusion), calls=%async_computation | async-start | bytes 4325376 | tf_op jit(solution)/shard_map/all_to_all | solution.py:703
  201.5 1401.6 %reduce-scatter.5.cloned.1.call-start = ((), (), s32[]{:S(2)}) async-start(), calls=%async_computation.8 | async-start | bytes 2359296 | tf_op jit(solution)/shard_map/reduce_scatter | solution.py:874
  206.1 318.5 %copy-start.41 = (f32[256]{0:T(256)}, f32[256]{0:T(256)S(1)}, u32[]{:S(2)}) copy-start(f32[256]{0:T(256)S(1)} %add_rsqrt_fusion) | copy-start | bytes 3076
  863.5 183.1 %copy-start.13 = (f32[256,2048]{1,0:T(8,128)S(1)}, f32[256,2048]{1,0:T(8,128)}, u32[]{:S(2)}) copy-start(f32[256,2048]{1,0:T(8,128)} %copy-done.12) | copy-start | bytes 6291460
  863.6 183.1 %copy-start.32 = (f32[2048]{0:T(1024)S(1)}, f32[2048]{0:T(1024)}, u32[]{:S(2)}) copy-start(f32[2048]{0:T(1024)} %copy-done.31) | copy-start | bytes 24580
  863.6 183.1 %copy-start.42 = (f32[256]{0:T(256)S(1)}, f32[256]{0:T(256)}, u32[]{:S(2)}) copy-start(f32[256]{0:T(256)} %copy-done.41) | copy-start | bytes 3076
  1094.8 510.0 %reduce-scatter.3.cloned.1.call-start = ((), (), s32[]{:S(2)}) async-start(), calls=%async_computation.7 | async-start | bytes 7077888 | tf_op jit(solution)/shard_map/reduce_scatter | solution.py:871
  1240.1 356.6 %all-to-all-start.1 = ((bf16[8,256,528]{1,2,0:T(8,128)(2,1)}), bf16[8,256,528]{1,2,0:T(8,128)(2,1)}, u32[]{:S(2)}, u32[]{:S(2)}) async-start(bf16[8,256,528]{1,2,0:T(8,128)(2,1)} %pad_maximum_fusion.1), calls=%async_computation.3 | async-start | bytes 4325376 | tf_op jit(solution)/shard_map/all_to_all | solution.py:891
  1244.5 401.9 %all-reduce.9.cloned.1.call-start = ((), (), s32[]{:S(2)}) async-start(), calls=%async_computation.9 | async-start | bytes 262144 | tf_op jit(solution)/shard_map/psum | solution.py:898
  1494.0 29.7 %copy-start.17 = (bf16[256,2048]{1,0:T(8,128)(2,1)S(1)}, bf16[256,2048]{1,0:T(8,128)(2,1)}, u32[]{:S(2)}) copy-start(bf16[256,2048]{1,0:T(8,128)(2,1)} %param.25) | copy-start | bytes 3145732
  1494.0 29.7 %copy-start.36 = (f32[2048]{0:T(1024)S(1)}, f32[2048]{0:T(1024)}, u32[]{:S(2)}) copy-start(f32[2048]{0:T(1024)} %copy-done.35) | copy-start | bytes 24580
  1494.0 29.7 %copy-start.45 = (f32[256]{0:T(256)S(1)}, f32[256]{0:T(256)}, u32[]{:S(2)}) copy-start(f32[256]{0:T(256)} %copy-done.44) | copy-start | bytes 3076
  1521.9 42.1 %copy-start.1 = (f32[256,2048]{1,0:T(8,128)S(1)}, f32[256,2048]{1,0:T(8,128)}, u32[]{:S(2)}) copy-start(f32[256,2048]{1,0:T(8,128)} %copy-done) | copy-start | bytes 6291460
  1521.9 42.1 %copy-start.33 = (f32[2048]{0:T(1024)S(1)}, f32[2048]{0:T(1024)}, u32[]{:S(2)}) copy-start(f32[2048]{0:T(1024)} %copy-done.31) | copy-start | bytes 24580
  1521.9 42.1 %copy-start.43 = (f32[256]{0:T(256)S(1)}, f32[256]{0:T(256)}, u32[]{:S(2)}) copy-start(f32[256]{0:T(256)} %copy-done.41) | copy-start | bytes 3076
  1521.9 42.1 %copy-start.48 = (f32[256]{0:T(256)S(1)}, f32[256]{0:T(256)}, u32[]{:S(2)}) copy-start(f32[256]{0:T(256)} %copy-done.46) | copy-start | bytes 3076
  1521.9 42.1 %copy-start.50 = (f32[256]{0:T(256)S(1)}, f32[256]{0:T(256)}, u32[]{:S(2)}) copy-start(f32[256]{0:T(256)} %copy-done.49) | copy-start | bytes 3076
  (45 other events, 198.8 us)
Sparse Core Ops, SparseCore 0:
  10.3 67.4 all-gather.3
  117.6 29.3 all-gather.5
  192.4 322.7 all-gather.7
  1094.9 33.4 reduce-scatter.4
  1194.2 78.2 reduce-scatter.2
  1526.6 119.7 all-reduce.8

commit v2 on v1

--- a/solution.py
+++ b/solution.py
@@ -77,6 +77,10 @@
     return lax.ppermute(values, axis_name, [(i, i ^ mask) for i in range(count)])
 
 
+def add_low(left, right):
+    return (left.astype(F32) + right.astype(F32)).astype(BF)
+
+
 def reorder(blocks, place):
     return jnp.stack(
         [lax.dynamic_index_in_dim(blocks, i ^ place, keepdims=False) for i in range(blocks.shape[0])]
@@ -133,128 +137,90 @@
             copy.wait_send()
 
 
-def gather_kernel(pair_count, with_core, x_ref, out_ref, own_sem, send_sems, recv_sems):
-    f, s = lax.axis_index("fsdp"), lax.axis_index("sp")
-    middle = x_ref.shape[0] // 2
-    partners = [("sp", flip(s, 1)), ("sp", flip(s, 2))]
-    partners += [("fsdp", flip(f, 1))] if with_core else []
-    partners += [("fsdp", flip(f, 2 * k)) for k in range(1, pair_count)]
-    greet(partners)
+def gather_kernel(count, *refs):
+    given, made = refs[:count], refs[count : 2 * count]
+    bounce, own_sems, send_sems, recv_sems = refs[2 * count :]
+    s = lax.axis_index("sp")
+    height = given[0].shape[0]
+    middle = height // 2
+    greet([("sp", flip(s, 1)), ("sp", flip(s, 2))])
     copies = Copies(send_sems, recv_sems)
 
-    def row(k):
-        return flip(f, 2 * k) if with_core else 0
-
-    def block(k, j, h):
-        return out_ref.at[row(k), flip(s, j), pl.ds(h * middle, middle)]
-
-    def own(h):
-        return x_ref.at[pl.ds(h * middle, middle)]
-
-    local = pltpu.make_async_copy(x_ref, out_ref.at[row(0), s], own_sem)
-    local.start()
-    distant = {}
-    for k in range(1, pair_count):
-        for h in range(2):
-            distant[k, h] = copies.start(own(h), block(0, 0, h), "fsdp", flip(f, 2 * k))
-    near, crossing = {}, []
-
-    def core(k, j, h):
-        if with_core:
-            source = own(h) if k == 0 and j == 0 else block(k, j, h)
-            crossing.append(copies.start(source, block(k, j, h), "fsdp", flip(f, 1)))
-
-    def first(k):
-        for h in range(2):
-            if k:
-                distant[k, h].wait_recv()
-            source = own(h) if k == 0 else block(k, 0, h)
-            a, b = sp_bits()[h]
-            near[k, a, h] = copies.start(source, block(k, 0, h), "sp", flip(s, a))
-        for h in range(2):
-            source = own(h) if k == 0 else block(k, 0, h)
-            a, b = sp_bits()[h]
-            near[k, b, h] = copies.start(source, block(k, 0, h), "sp", flip(s, b))
-            core(k, 0, h)
-
-    def second(k):
+    def block(t, j, h):
+        start = pl.multiple_of(flip(s, j) * height + h * middle, middle)
+        return made[t].at[pl.ds(start, middle)]
+
+    local, near = [], {}
+    for t in range(count):
+        target = made[t].at[pl.ds(pl.multiple_of(s * height, height), height)]
+        pltpu.make_async_copy(given[t], bounce.at[t], own_sems.at[t]).start()
+        local.append(pltpu.make_async_copy(bounce.at[t], target, own_sems.at[t]))
+        for turn in range(2):
+            for h in range(2):
+                bit = sp_bits()[h][turn]
+                source = given[t].at[pl.ds(h * middle, middle)]
+                near[t, h, bit] = copies.start(source, block(t, 0, h), "sp", flip(s, bit))
+    for t in range(count):
+        pltpu.make_async_copy(given[t], bounce.at[t], own_sems.at[t]).wait()
+        local[t].start()
         for h in range(2):
             a, b = sp_bits()[h]
-            near[k, a, h].wait_recv()
-            near[k, 3, h] = copies.start(block(k, a, h), block(k, a, h), "sp", flip(s, b))
-            core(k, a, h)
-
-    def third(k):
+            near[t, h, a].wait_recv()
+            near[t, h, 3] = copies.start(block(t, a, h), block(t, a, h), "sp", flip(s, b))
+    for t in range(count):
         for h in range(2):
-            a, b = sp_bits()[h]
-            near[k, b, h].wait_recv()
-            core(k, b, h)
-
-    def fourth(k):
-        for h in range(2):
-            near[k, 3, h].wait_recv()
-            core(k, 3, h)
-
-    for step in range(pair_count + 2):
-        if step < pair_count:
-            first(step)
-        if 0 <= step - 1 < pair_count:
-            second(step - 1)
-            third(step - 1)
-        if 0 <= step - 2 < pair_count:
-            fourth(step - 2)
-    local.wait()
-    for copy in crossing:
-        copy.wait_recv()
+            near[t, h, sp_bits()[h][1]].wait_recv()
+            near[t, h, 3].wait_recv()
+        local[t].wait()
     copies.finish()
 
 
-def gather_call(rows, pair_count, with_core, number):
-    height, width = rows.shape
-    fsdp_count, sp_count = lax.axis_size("fsdp"), lax.axis_size("sp")
-    count = 2 * (pair_count - 1) + 6 * pair_count + (8 * pair_count if with_core else 0)
-    outer = fsdp_count if with_core else 1
+def gather_call(arrays, number):
+    height, width = arrays[0].shape
+    count, sp_count = len(arrays), lax.axis_size("sp")
+    whole = jax.ShapeDtypeStruct((sp_count * height, width), arrays[0].dtype)
     return pl.pallas_call(
-        functools.partial(gather_kernel, pair_count, with_core),
-        out_shape=jax.ShapeDtypeStruct((outer, sp_count, height, width), rows.dtype),
-        in_specs=[pl.BlockSpec(memory_space=pl.ANY)],
-        out_specs=pl.BlockSpec(memory_space=pl.ANY),
+        functools.partial(gather_kernel, count),
+        out_shape=[whole] * count,
+        in_specs=[pl.BlockSpec(memory_space=pl.ANY)] * count,
+        out_specs=[pl.BlockSpec(memory_space=pl.ANY)] * count,
         scratch_shapes=[
-            pltpu.SemaphoreType.DMA,
+            pltpu.VMEM((count, height, width), BF),
             pltpu.SemaphoreType.DMA((count,)),
-            pltpu.SemaphoreType.DMA((count,)),
+            pltpu.SemaphoreType.DMA((6 * count,)),
+            pltpu.SemaphoreType.DMA((6 * count,)),
         ],
         compiler_params=pltpu.CompilerParams(collective_id=number, has_side_effects=True),
-    )(rows)
+    )(*arrays)
 
 
 def scatter_kernel(
-    pair_count, with_core, p_ref, out_ref, held, loads, came, last, far, load_sems, send_sems, recv_sems
+    pair_count, p_ref, q_ref, out_ref, held, loads, came, last, far, load_sems, send_sems, recv_sems
 ):
     f, s = lax.axis_index("fsdp"), lax.axis_index("sp")
     middle = held.shape[3]
     partners = [("sp", flip(s, 1)), ("sp", flip(s, 2))]
-    partners += [("fsdp", flip(f, 1))] if with_core else []
     partners += [("fsdp", flip(f, 2 * k)) for k in range(1, pair_count)]
     greet(partners)
     copies = Copies(send_sems, recv_sems)
     order = list(range(pair_count))[::-1]
 
-    def rows_of(k, h):
-        return p_ref.at[flip(f, 2 * k) if with_core else 0, :, pl.ds(h * middle, middle)]
-
-    crossing, loading = {}, {}
-    if with_core:
-        for k in order:
-            for h in range(2):
-                source = p_ref.at[flip(flip(f, 2 * k), 1), :, pl.ds(h * middle, middle)]
-                crossing[k, h] = copies.start(source, held.at[k, h], "fsdp", flip(f, 1))
+    loading = {}
 
     def load(k):
         for h in range(2):
-            target = loads.at[k % 2, h] if with_core else held.at[k, h]
-            loading[k, h] = pltpu.make_async_copy(rows_of(k, h), target, load_sems.at[k % 2, h])
-            loading[k, h].start()
+            rows = pl.ds(h * middle, middle)
+            loading[k, h] = [
+                pltpu.make_async_copy(p_ref.at[k, :, rows], held.at[k, h], load_sems.at[k % 2, h, 0])
+            ]
+            if q_ref is not None:
+                loading[k, h].append(
+                    pltpu.make_async_copy(
+                        q_ref.at[k, :, rows], loads.at[k % 2, h], load_sems.at[k % 2, h, 1]
+                    )
+                )
+            for copy in loading[k, h]:
+                copy.start()
 
     def add(target, source):
         def body(n, _):
@@ -268,19 +234,18 @@
 
     def first(n):
         k = order[n]
-        if with_core and n + 1 < pair_count:
+        if n + 1 < pair_count:
             load(order[n + 1])
         for h in range(2):
-            loading[k, h].wait()
+            for copy in loading[k, h]:
+                copy.wait()
             a, b = sp_bits()[h]
-            if with_core:
-                crossing[k, h].wait_recv()
-            for i, j in enumerate((a, 3)):
+            for i, j in ((1, 3), (0, a)):
                 piece = held.at[k, h, flip(s, j)]
-                if with_core:
+                if q_ref is not None:
                     add(piece, loads.at[k % 2, h, flip(s, j)])
                 near[k, h, i] = copies.start(piece, came.at[k, h, i], "sp", flip(s, a))
-        if with_core:
+        if q_ref is not None:
             for h in range(2):
                 a, b = sp_bits()[h]
                 for j in (0, b):
@@ -331,23 +296,28 @@
     copies.finish()
 
 
-def scatter_call(blocks, pair_count, with_core, number):
-    _, sp_count, height, width = blocks.shape
+def sum_kernel(pair_count, p_ref, *refs):
+    scatter_kernel(pair_count, p_ref, None, *refs)
+
+
+def scatter_call(number, blocks, more=None):
+    pair_count, sp_count, height, width = blocks.shape
     middle = height // 2
-    count = 6 * pair_count + 2 * (pair_count - 1) + (2 * pair_count if with_core else 0)
-    used = 2 * pair_count * (sp_count + 3) + (4 * sp_count if with_core else 0) + 2 * pair_count
+    count = 6 * pair_count + 2 * (pair_count - 1)
+    given = [blocks] if more is None else [blocks, more]
+    used = 2 * pair_count * (sp_count + 3) + (4 * sp_count if more is not None else 0) + 2 * pair_count
     return pl.pallas_call(
-        functools.partial(scatter_kernel, pair_count, with_core),
+        functools.partial(sum_kernel if more is None else scatter_kernel, pair_count),
         out_shape=jax.ShapeDtypeStruct((height, width), F32),
-        in_specs=[pl.BlockSpec(memory_space=pl.ANY)],
+        in_specs=[pl.BlockSpec(memory_space=pl.ANY)] * len(given),
         out_specs=pl.BlockSpec(memory_space=pltpu.VMEM),
         scratch_shapes=[
             pltpu.VMEM((pair_count, 2, sp_count, middle, width), BF),
-            pltpu.VMEM((2, 2, sp_count if with_core else 1, middle if with_core else 16, width), BF),
+            pltpu.VMEM((2, 2, sp_count, middle, width) if len(given) > 1 else (2, 2, 1, 16, width), BF),
             pltpu.VMEM((pair_count, 2, 2, middle, width), BF),
             pltpu.VMEM((pair_count, 2, middle, width), BF),
             pltpu.VMEM((max(pair_count - 1, 1), 2, middle if pair_count > 1 else 16, width), BF),
-            pltpu.SemaphoreType.DMA((2, 2)),
+            pltpu.SemaphoreType.DMA((2, 2, 2)),
             pltpu.SemaphoreType.DMA((count,)),
             pltpu.SemaphoreType.DMA((count,)),
         ],
@@ -356,7 +326,10 @@
             has_side_effects=True,
             vmem_limit_bytes=min(60 * 1024 * 1024, (2 * used * middle + 4 * height) * width + (8 << 20)),
         ),
-    )(blocks)
+        cost_estimate=pl.CostEstimate(
+            flops=0, bytes_accessed=140_000_000 * pair_count, transcendentals=0
+        ),
+    )(*given)
 
 
 def nt_dot(left, right):
@@ -372,7 +345,13 @@
     return pl.ds(pl.multiple_of(index * size, size), size)
 
 
-def moe_kernel(
+def moe_kernel(hidden, expert_count, share, x_ref, dm_ref, *refs):
+    ins, (mixer_ref, dout_ref), rest = refs[:7], refs[7:9], refs[9:]
+    rows, d_rows, out, d_out = x_ref.at[0], dm_ref.at[0], mixer_ref.at[0], dout_ref.at[0]
+    moe_step(hidden, expert_count, share, rows, d_rows, *ins, out, d_out, *rest)
+
+
+def moe_step(
     hidden,
     expert_count,
     share,
@@ -405,7 +384,7 @@
     hp = both // 2
     shared_pad = sd_ref.shape[0]
     capacity = pick.shape[0]
-    length = x_ref.shape[1]
+    length = x_ref.shape[0]
     tile = 512
     span = 64
     low = hidden // 128 * 128
@@ -418,8 +397,8 @@
 
         def take(n, _):
             cols = block_of(n, tile)
-            rows_ref[0, 0, :, cols] = dot(pick[...], x_ref[0, :, cols]).astype(BF)
-            drows_ref[0, 0, :, cols] = dot(pick[...], dm_ref[0, :, cols]).astype(BF)
+            rows_ref[0, 0, :, cols] = dot(pick[...], x_ref[:, cols]).astype(BF)
+            drows_ref[0, 0, :, cols] = dot(pick[...], dm_ref[:, cols]).astype(BF)
             return 0
 
         lax.fori_loop(0, width // tile, take, 0)
@@ -461,15 +440,15 @@
 
     @pl.when(step >= experts)
     def _():
-        rows = mixer_ref.shape[1]
+        rows = mixer_ref.shape[0]
         here = block_of(step - experts, rows)
         slots = lax.broadcasted_iota(jnp.int32, (rows, capacity), 1)
         for e in range(experts):
             put[:, e * capacity : (e + 1) * capacity] = jnp.where(
                 col_ref[0, :, e : e + 1] == slots, 1.0, 0.0
             ).astype(BF)
-        sgu[:, : 2 * shared_pad] = dot(x_ref[0, here, :], sgu_ref[...])
-        sgu[:, 2 * shared_pad :] = nt_dot(dm_ref[0, here, :], sd_ref[...])
+        sgu[:, : 2 * shared_pad] = dot(x_ref[here, :], sgu_ref[...])
+        sgu[:, 2 * shared_pad :] = nt_dot(dm_ref[here, :], sd_ref[...])
 
         def middle(n, _):
             part = block_of(n, span)
@@ -492,10 +471,10 @@
 
         def finish(n, _):
             cols = block_of(n, tile)
-            mixer_ref[0, :, cols] = (
+            mixer_ref[:, cols] = (
                 dot(put[...], y_all[:, cols]) + dot(sact_ref[0], sd_ref[:, cols])
             ).astype(BF)
-            dout_ref[0, :, cols] = (
+            dout_ref[:, cols] = (
                 dot(put[...], dx_all[:, cols]) + nt_dot(dsgu_ref[0], sgu_ref[cols, :])
             ).astype(BF)
             return 0
@@ -503,10 +482,229 @@
         lax.fori_loop(0, width // tile, finish, 0)
 
 
-def moe_call(rows, d_rows, codes, own, weights, sizes):
+def moe_gather_kernel(hidden, expert_count, share, pair_count, x_own, dm_seq, dm_far, *refs):
+    ins, (x_all, dm_all), outs, crossed, rest = refs[:7], refs[7:9], refs[9:11], refs[11:13], refs[13:-11]
+    x_buf, dm_buf, m_buf, d_buf, own_sems, load_sems, far_sems, near_sems, core_sems = refs[-11:-2]
+    out_sems, cross_sems = refs[-2:]
+    m, step = pl.program_id(0), pl.program_id(1)
+    steps = pl.num_programs(1)
+    f, s = lax.axis_index("fsdp"), lax.axis_index("sp")
+    height = x_own.shape[0]
+    middle = height // 2
+    alls, bufs = (x_all, dm_all), (x_buf, dm_buf)
+    both = (0, 1)
+
+    def rows(place):
+        return pl.ds(pl.multiple_of(place * height, height), height)
+
+    def half(t, k, place, h):
+        start = pl.multiple_of(place * height + h * middle, middle)
+        return alls[t].at[2 * k, pl.ds(start, middle)]
+
+    def remote(source, target, sems, at, axis, place):
+        return pltpu.make_async_remote_copy(
+            src_ref=source,
+            dst_ref=target,
+            send_sem=sems.at[(0, *at)],
+            recv_sem=sems.at[(1, *at)],
+            device_id={axis: place},
+            device_id_type=MESH,
+        )
+
+    def far(k, t=0):
+        source = x_own if t == 0 else dm_seq.at[rows(s)]
+        return remote(source, alls[t].at[2 * k, rows(s)], far_sems, (k, t), "fsdp", flip(f, 2 * k))
+
+    early = dm_far.shape[0]
+
+    def near(t, k, h, i):
+        a, b = sp_bits()[h]
+        source = half(t, k, flip(s, a) if i == 2 else s, h)
+        return remote(source, source, near_sems, (k, t, 3 * h + i), "sp", flip(s, a if i == 0 else b))
+
+    def core(t, k, j):
+        place = rows(flip(s, j))
+        target = alls[t].at[2 * k + 1, place]
+        return remote(alls[t].at[2 * k, place], target, core_sems, (k, t, j), "fsdp", flip(f, 1))
+
+    def distant(k):
+        far(k).start()
+        if k > early:
+            far(k, 1).start()
+
+    def first(k, tensors):
+        if k:
+            far(k).wait_recv()
+        if k > early:
+            far(k, 1).wait_recv()
+        for t in tensors:
+            for h in range(2):
+                near(t, k, h, 0).start()
+        if 2 <= k < pair_count - 1:
+            distant(k + 1)
+
+    def direct(k, tensors):
+        for t in tensors:
+            for h in range(2):
+                near(t, k, h, 1).start()
+            core(t, k, 0).start()
+
+    def second(k, tensors):
+        for t in tensors:
+            for h in range(2):
+                near(t, k, h, 0).wait_recv()
+                near(t, k, h, 2).start()
+
+    def third(k, tensors):
+        for t in tensors:
+            for h in range(2):
+                near(t, k, h, 1).wait_recv()
+            core(t, k, 1).start()
+            core(t, k, 2).start()
+
+    def fourth(k, tensors):
+        for t in tensors:
+            for h in range(2):
+                near(t, k, h, 2).wait_recv()
+            core(t, k, 3).start()
+
+    def load(n, t):
+        return pltpu.make_async_copy(alls[t].at[n], bufs[t].at[n % 2], load_sems.at[n % 2, t])
+
+    def at_start():
+        partners = [("sp", flip(s, 1)), ("sp", flip(s, 2)), ("fsdp", flip(f, 1))]
+        partners += [("fsdp", flip(f, 2 * k)) for k in range(1, pair_count)]
+        greet(partners)
+        moves = [(x_own, x_buf.at[1, pl.ds(0, height)], x_all.at[0, rows(s)])]
+        for k in range(1, early + 1):
+            piece = dm_buf.at[1, pl.ds((k - 1) * height, height)]
+            moves.append((dm_far.at[k - 1], piece, dm_all.at[2 * k, rows(s)]))
+        moves.append((dm_seq, dm_buf.at[0], dm_all.at[0]))
+        came = [
+            pltpu.make_async_copy(source, stop, own_sems.at[n])
+            for n, (source, stop, _) in enumerate(moves)
+        ]
+        left = [
+            pltpu.make_async_copy(stop, target, own_sems.at[n])
+            for n, (_, stop, target) in enumerate(moves)
+        ]
+        for copy in came:
+            copy.start()
+        for n, copy in enumerate(came):
+            copy.wait()
+            left[n].start()
+        left[0].wait()
+        first(0, (0,))
+        far(1).start()
+        direct(0, (0,))
+        for copy in left[1:]:
+            copy.wait()
+        second(0, (0,))
+        distant(2)
+        for j in range(4):
+            core(1, 0, j).start()
+        third(0, (0,))
+        fourth(0, (0,))
+        load(0, 0).start()
+
+    def whole(n):
+        if n % 2:
+            for t in both:
+                for j in range(4):
+                    core(t, n // 2, j).wait_recv()
+        for t in both:
+            load(n, t).start()
+
+    plan = {0: [at_start]}
+    for k in range(1, pair_count):
+        base = 8 * (k - 1) + (k > 1)
+        last = 8 * k - 1
+        places = (base - (k == 2), base + 1 - (k == 2), base + 3, last - 2 + (k > 2), last)
+        for event, place in zip((first, direct, second, third, fourth), places, strict=True):
+            plan.setdefault(place, []).append(functools.partial(event, k, both))
+    for n in range(1, 2 * pair_count):
+        plan.setdefault(4 * n - 1, []).append(functools.partial(whole, n))
+    now = m * steps + step
+    for place, events in sorted(plan.items()):
+
+        @pl.when(now == place)
+        def _():
+            for event in events:
+                event()
+
+    for n in range(2 * pair_count):
+
+        @pl.when(now == n * steps)
+        def _():
+            for t in both if n else (0,):
+                load(n, t).wait()
+
+    token_step = step - ins[4].shape[0]
+    even, pair = lax.rem(m, 2) == 0, lax.div(m, 2)
+    out_bufs = (m_buf, d_buf)
+    tile = m_buf.shape[1]
+    tile_slot = lax.rem(token_step + 2, 2)
+
+    def stay(t, k, i):
+        target = outs[t].at[k, pl.ds(pl.multiple_of(i * tile, tile), tile)]
+        slot = lax.rem(i + 2, 2)
+        return pltpu.make_async_copy(out_bufs[t].at[slot], target, out_sems.at[t, slot])
+
+    def leave(t, k, i):
+        target = crossed[t].at[k, pl.ds(pl.multiple_of(i * tile, tile), tile)]
+        source = out_bufs[t].at[lax.rem(i + 2, 2)]
+        return remote(source, target, cross_sems, (t, k, i), "fsdp", flip(f, 1))
+
+    @pl.when((token_step >= 0) & even & (m > 0))
+    def _():
+        for t in both:
+            leave(t, pair - 1, token_step).wait_send()
+
+    @pl.when((token_step >= 0) & (~even))
+    def _():
+        for t in both:
+            stay(t, pair, token_step).wait()
+
+    slot = lax.rem(m, 2)
+    tiles = m_buf.at[tile_slot], d_buf.at[tile_slot]
+    moe_step(hidden, expert_count, share, x_buf.at[slot], dm_buf.at[slot], *ins, *tiles, *rest)
+
+    @pl.when((token_step >= 0) & even)
+    def _():
+        for t in both:
+            stay(t, pair, token_step).start()
+
+    @pl.when((token_step >= 0) & (~even))
+    def _():
+        for t in both:
+            leave(t, pair, token_step).start()
+
+    @pl.when(now == 2 * pair_count * steps - 1)
+    def _():
+        for k in range(pair_count):
+            if k:
+                far(k).wait_send()
+            if k > early:
+                far(k, 1).wait_send()
+            for t in both:
+                if k or t == 0:
+                    for h in range(2):
+                        for i in range(3):
+                            near(t, k, h, i).wait_send()
+                for j in range(4):
+                    core(t, k, j).wait_send()
+                for i in range(x_buf.shape[1] // tile):
+                    if k == pair_count - 1:
+                        leave(t, k, i).wait_send()
+                    leave(t, k, i).wait_recv()
+
+
+def moe_call(rows, d_rows, codes, own, weights, sizes, number=None, far_d_rows=None):
     hidden, expert_count, share, capacity = sizes
     wide_gu, wide_down, shared_gu, shared_down = weights
-    seqs, length, width = rows.shape
+    seqs, _, length = codes.shape
+    width = rows.shape[-1]
+    pair_count = seqs // 2
     experts, _, both = wide_gu.shape
     hp = both // 2
     shared_pad = shared_down.shape[0]
@@ -539,12 +737,37 @@
     flops = seqs * 2 * (
         slots * width * (2 * length + 3 * both) + length * width * (2 * slots + 6 * shared_pad)
     )
+    if number is None:
+        kernel = functools.partial(moe_kernel, hidden, expert_count, share)
+        tokens_spec = pl.BlockSpec((1, length, width), lambda s, i: (s, 0, 0))
+        sums, sum_specs = [token_out(width)] * 2, [token_block(width)] * 2
+        sems, extra = [], []
+    else:
+        kernel = functools.partial(moe_gather_kernel, hidden, expert_count, share, pair_count)
+        tokens_spec = pl.BlockSpec(memory_space=pl.ANY)
+        half = jax.ShapeDtypeStruct((pair_count, length, width), BF)
+        sums, sum_specs = [token_out(width)] * 2 + [half] * 4, [tokens_spec] * 6
+        extra = [far_d_rows]
+        sems = [
+            pltpu.VMEM((2, length, width), BF),
+            pltpu.VMEM((2, length, width), BF),
+            pltpu.VMEM((2, token_rows, width), BF),
+            pltpu.VMEM((2, token_rows, width), BF),
+            pltpu.SemaphoreType.DMA((1 + pair_count,)),
+            pltpu.SemaphoreType.DMA((2, 2)),
+            pltpu.SemaphoreType.DMA((2, pair_count, 2)),
+            pltpu.SemaphoreType.DMA((2, pair_count, 2, 6)),
+            pltpu.SemaphoreType.DMA((2, pair_count, 2, 4)),
+            pltpu.SemaphoreType.DMA((2, 2)),
+            pltpu.SemaphoreType.DMA((2, 2, pair_count, token_steps)),
+        ]
     return pl.pallas_call(
-        functools.partial(moe_kernel, hidden, expert_count, share),
+        kernel,
         grid=(seqs, experts + token_steps),
         in_specs=[
-            pl.BlockSpec((1, length, width), lambda s, i: (s, 0, 0)),
-            pl.BlockSpec((1, length, width), lambda s, i: (s, 0, 0)),
+            tokens_spec,
+            tokens_spec,
+            *([tokens_spec] * len(extra)),
             pl.BlockSpec((1, experts, length), lambda s, i: (s, 0, 0)),
             token_block(experts),
             fixed(own),
@@ -554,8 +777,7 @@
             fixed(shared_down),
         ],
         out_specs=[
-            token_block(width),
-            token_block(width),
+            *sum_specs,
             slot_block(width),
             slot_block(width),
             slot_block(hp),
@@ -564,8 +786,7 @@
             token_block(2 * shared_pad),
         ],
         out_shape=[
-            token_out(width),
-            token_out(width),
+            *sums,
             slot_out(width),
             slot_out(width),
             slot_out(hp),
@@ -580,29 +801,38 @@
             pltpu.VMEM((slots, width), BF),
             pltpu.VMEM((token_rows, slots), BF),
             pltpu.VMEM((token_rows, 3 * shared_pad), F32),
+            *sems,
         ],
         compiler_params=pltpu.CompilerParams(
-            dimension_semantics=("arbitrary", "arbitrary"), vmem_limit_bytes=60 * 1024 * 1024
+            dimension_semantics=("arbitrary", "arbitrary"),
+            vmem_limit_bytes=60 * 1024 * 1024,
+            collective_id=number,
+            has_side_effects=number is not None,
         ),
         cost_estimate=pl.CostEstimate(
-            flops=flops, bytes_accessed=seqs * 24 * length * width, transcendentals=0
+            flops=flops, bytes_accessed=seqs * 64 * length * width, transcendentals=0
         ),
-    )(rows, d_rows, codes, codes.transpose(0, 2, 1), own, *weights)
-
-
-def moe_grads(rows, d_rows, slot_rows, slot_d_rows, act, d_gu, s_act, d_sgu):
+    )(rows, d_rows, *extra, codes, codes.transpose(0, 2, 1), own, *weights)
+
+
+def shared_grads(rows, d_rows, s_act, d_sgu):
+    def tokens_of(array):
+        return array.reshape(-1, array.shape[-1])
+
+    return (
+        dot(tokens_of(rows).T, tokens_of(d_sgu)),
+        dot(tokens_of(d_rows).T, tokens_of(s_act)),
+    )
+
+
+def expert_grads(rows, d_rows, act, d_gu):
     def flat(array):
         return array.reshape(array.shape[0], -1, array.shape[-1])
 
-    def tokens_of(array):
-        return array.reshape(-1, array.shape[-1])
-
-    return (
-        jnp.einsum("ecd,ecf->edf", flat(slot_rows), flat(d_gu), preferred_element_type=F32),
-        jnp.einsum("ecf,ecd->efd", flat(act), flat(slot_d_rows), preferred_element_type=F32),
-        dot(tokens_of(rows).T, tokens_of(d_sgu)),
-        dot(tokens_of(d_rows).T, tokens_of(s_act)),
-    )
+    grad_gu = jnp.einsum("ecd,ecf->edf", flat(rows), flat(d_gu), preferred_element_type=F32)
+    act = after(act, grad_gu)
+    grad_ed = jnp.einsum("ecf,ecd->efd", flat(act), flat(d_rows), preferred_element_type=F32)
+    return grad_gu, grad_ed
 
 
 def pad_last(array, size):
@@ -663,7 +893,7 @@
     def spread(local_rows, number):
         if not own_kernels:
             return lax.all_gather(local_rows, "sp", axis=0, tiled=True)
-        return gather_call(local_rows, 1, False, number).reshape(seq_len, width)
+        return gather_call([local_rows], number)[0]
 
     def collect(partial_rows, number):
         partial_rows = partial_rows.astype(BF)
@@ -671,26 +901,57 @@
             rows = lax.psum_scatter(partial_rows, "sp", scatter_dimension=0, tiled=True)
             return rows.astype(F32)
         blocks = partial_rows.reshape(1, sp_count, tok_count, width)
-        return scatter_call(blocks, 1, False, number)
-
-    def home(parts, number):
-        return scatter_call(
-            parts.reshape(fsdp_count, sp_count, tok_count, width), pair_count, True, number
+        return scatter_call(number, blocks)
+
+    orders = sp_bits()
+
+    def slow_start(parts, crossed):
+        shape = (pair_count, sp_count, 2, tok_count // 2, width)
+        mine, crossed = parts.reshape(shape), crossed.reshape(shape)
+
+        def pick(h, j):
+            place = sp_place ^ j
+            return add_low(
+                lax.dynamic_index_in_dim(mine, place, 1, False)[:, h],
+                lax.dynamic_index_in_dim(crossed, place, 1, False)[:, h],
+            )
+
+        sent = [jnp.stack([pick(h, orders[h][0]), pick(h, 3)]) for h in range(2)]
+        kept = [jnp.stack([pick(h, 0), pick(h, orders[h][1])]) for h in range(2)]
+        return sent, kept
+
+    def slow_first(sent):
+        return [swap(sent[h], "sp", orders[h][0]) for h in range(2)]
+
+    def slow_second(kept, came):
+        kept = [add_low(kept[h], came[h]) for h in range(2)]
+        return [kept[h][0] for h in range(2)], [
+            swap(kept[h][1], "sp", orders[h][1]) for h in range(2)
+        ]
+
+    def slow_third(kept, came):
+        rows = jnp.concatenate([add_low(kept[h], came[h]) for h in range(2)], 1)
+        rows = reorder(rows, fsdp_place // 2).reshape(pair_count * tok_count, width)
+        cores = [[2 * z + c for z in range(pair_count)] for c in range(2)]
+        return lax.psum_scatter(
+            rows, "fsdp", scatter_dimension=0, axis_index_groups=cores, tiled=True
         )
 
     inputs = tokens.astype(F32)
     attn_rms = rms_scale(inputs)
     gain_one = gain_attn.astype(F32)
-    normed_attn = spread((inputs * attn_rms * gain_one).astype(BF), 1)
+    normed_attn = (inputs * attn_rms * gain_one).astype(BF)
+    upstream = cotangent.astype(F32)
+    d_mixer = (live_rows * upstream).astype(BF)
+    d_mixer_own = d_mixer
+    if own_kernels:
+        normed_attn, d_mixer = gather_call([normed_attn, d_mixer], 1)
+    else:
+        normed_attn, d_mixer = spread(normed_attn, 1), spread(d_mixer, 1)
     full_qkv = lax.all_gather(
         jnp.concatenate([w_query, w_key, w_value], 1), "fsdp", axis=0, tiled=True
     )
-    full_out = lax.all_gather(after(w_out, full_qkv), "fsdp", axis=1, tiled=True)
-    upstream = cotangent.astype(F32)
-    d_mixer = after((live_rows * upstream).astype(BF), full_out)
-    if own_kernels:
-        all_d_rows = lax.all_gather(d_mixer, whole_axes, axis=0, tiled=True)
-        all_d_rows = all_d_rows.reshape(fsdp_count, seq_len, width)
+    full_out_t = lax.all_gather(after(w_out.T, full_qkv), "fsdp", axis=0, tiled=True)
     share = shared_gate.shape[1] // fsdp_count
     packed = jnp.concatenate(
         [
@@ -715,20 +976,11 @@
         2,
     )
     wide_down = jnp.pad(expert_down, ((0, 0), (0, hp - hidden_units), (0, 0)))
-    shared_gu = jnp.concatenate(
-        [
-            pad_last(jnp.concatenate([packed[:, :share], mix_gate[:, None]], 1), shared_pad),
-            pad_last(packed[:, share : 2 * share], shared_pad),
-        ],
-        1,
-    )
-    shared_down_rows = pad_last(packed[:, 2 * share :], shared_pad).T
     all_routes = routes.T[None]
     bit = 1
     while bit < fsdp_count:
         all_routes = jnp.concatenate([all_routes, swap(all_routes, "fsdp", bit)], 0)
         bit *= 2
-    all_routes = reorder(all_routes, fsdp_place)
     first_expert = fsdp_place * local_experts
     wanted = first_expert + jnp.arange(local_experts, dtype=jnp.int32)
     named = jnp.any(all_routes[:, None] == wanted[None, :, None, None], axis=2)
@@ -747,6 +999,18 @@
         .reshape(seq_len, local_heads, HEAD)
     )
     query_rot = rotate(query_lin.reshape(seq_len, local_heads, HEAD), cosine, sine_table).astype(BF)
+    query_rot, packed = lax.optimization_barrier((query_rot, packed))
+    if own_kernels:
+        d_mixer_own = after(d_mixer_own, packed)
+        d_mixer_far = jnp.stack([swap(d_mixer_own, "fsdp", 2 * k) for k in range(1, 2)])
+    shared_gu = jnp.concatenate(
+        [
+            pad_last(jnp.concatenate([packed[:, :share], mix_gate[:, None]], 1), shared_pad),
+            pad_last(packed[:, share : 2 * share], shared_pad),
+        ],
+        1,
+    )
+    shared_down_rows = pad_last(packed[:, 2 * share :], shared_pad).T
     key_rot = rotate(key_lin.reshape(seq_len, local_heads, HEAD), cosine, sine_table).astype(BF)
 
     def block_scores(block_index):
@@ -778,7 +1042,7 @@
 
     attended, log_total = lax.map(attend_block, jnp.arange(block_count))
     attended = attended.reshape(seq_len, local_heads * HEAD)
-    attn_out = collect(dot(attended, full_out), 2)
+    attn_out = collect(nt_dot(attended, full_out_t), 2)
     hidden = inputs + live_rows * attn_out
     mlp_rms = rms_scale(hidden)
     gain_two = gain_mlp.astype(F32)
@@ -786,23 +1050,24 @@
     weights = (wide_gu, wide_down, shared_gu, shared_down_rows)
     sizes = (hidden_units, expert_count, share, capacity)
     if own_kernels:
-        all_rows = gather_call(normed_mlp, pair_count, True, 3)
-        all_rows = all_rows.reshape(fsdp_count, seq_len, width)
-        mixer_parts, d_parts, *kept = moe_call(all_rows, all_d_rows, codes, own, weights, sizes)
-        d_mlp_own = home(d_parts, 4)
+        all_rows, all_d_rows, mixer_parts, d_parts, mixer_crossed, d_crossed, *kept = moe_call(
+            normed_mlp, d_mixer, codes, own, weights, sizes, 3, d_mixer_far
+        )
+        blocks = (pair_count, sp_count, tok_count, width)
+        d_mlp_own = scatter_call(4, d_parts.reshape(blocks), d_crossed.reshape(blocks))
     else:
-        seq_rows, seq_d_rows, near_codes = spread(normed_mlp, 3), spread(d_mixer, 4), reorder(codes, fsdp_place)
+        seq_rows = spread(normed_mlp, 3)
         mixer_sum = d_sum = jnp.zeros((seq_len, width), F32)
         grads = None
         together = max(1, fsdp_count // 4)
         for start in range(0, fsdp_count, together):
             some = range(start, start + together)
             all_rows = jnp.stack([swap(seq_rows, "fsdp", m) for m in some])
-            all_d_rows = jnp.stack([swap(seq_d_rows, "fsdp", m) for m in some])
+            all_d_rows = jnp.stack([swap(d_mixer, "fsdp", m) for m in some])
             mixer_parts, d_parts, *kept = moe_call(
-                all_rows, all_d_rows, near_codes[start : start + together], own, weights, sizes
+                all_rows, all_d_rows, codes[start : start + together], own, weights, sizes
             )
-            more = moe_grads(all_rows, all_d_rows, *kept)
+            more = expert_grads(*kept[:4]) + shared_grads(all_rows, all_d_rows, *kept[4:])
             grads = more if grads is None else jax.tree.map(jnp.add, grads, more)
             for n, m in enumerate(some):
                 mixer_sum = mixer_sum + swap(mixer_parts[n], "fsdp", m).astype(F32)
@@ -814,8 +1079,37 @@
     grad_gain_two = jnp.sum(d_mlp_own * hidden * mlp_rms, axis=0)
     d_hidden = upstream + norm_back(d_mlp_own, hidden, mlp_rms, gain_two)
     d_attn = spread((live_rows * d_hidden).astype(BF), 5)
-    grad_out = dot(attended.T, d_attn)
-    d_attended = dot(d_attn, full_out.T).astype(BF).reshape(seq_len, local_heads, HEAD)
+    if own_kernels:
+        slow = slow_start(*after((mixer_parts, mixer_crossed), d_mlp_own))
+        d_attn, slow = lax.optimization_barrier((d_attn, slow))
+        slow = slow[1], slow_first(slow[0])
+        grad_out_t = dot(d_attn.T, attended).astype(BF)
+        grad_sgu, grad_sdown = shared_grads(
+            all_rows, all_d_rows, *after(kept[4:], (d_attn, grad_out_t))
+        )
+    else:
+        grad_out_t = dot(d_attn.T, attended).astype(BF)
+        grad_gu, grad_ed, grad_sgu, grad_sdown = grads
+    grad_w_out = lax.psum_scatter(
+        grad_out_t, "fsdp", scatter_dimension=0, tiled=True
+    ).astype(F32)
+    packed_grad = jnp.concatenate(
+        [
+            grad_sgu[:, :share],
+            grad_sgu[:, shared_pad : shared_pad + share],
+            grad_sdown[:, :share],
+        ],
+        1,
+    ).astype(BF)
+    d_attn, packed_grad = lax.optimization_barrier((d_attn, packed_grad))
+    packed_grad = lax.all_to_all(
+        packed_grad.reshape(fsdp_count, -1, 3 * share), "fsdp", split_axis=0, concat_axis=0, tiled=True
+    ).transpose(1, 0, 2)
+    d_attended = dot(d_attn, full_out_t).astype(BF).reshape(seq_len, local_heads, HEAD)
+
+    if own_kernels:
+        d_attended, slow = lax.optimization_barrier((d_attended, slow))
+        slow = slow_second(*slow)
 
     def attend_back(carry_in, block_index):
         key_grad, value_grad = carry_in
@@ -849,6 +1143,11 @@
     (key_grad, value_grad), query_grad = lax.scan(
         attend_back, (zero_grad, zero_grad), jnp.arange(block_count)
     )
+    if own_kernels:
+        query_grad, slow, packed_grad, grad_w_out = lax.optimization_barrier(
+            (query_grad, slow, packed_grad, grad_w_out)
+        )
+        mixer_out = slow_third(*slow).astype(F32)
     query_grad = query_grad.reshape(seq_len, local_heads, HEAD)
     d_query = (
         unrotate(query_grad, cosine, sine_table)
@@ -862,42 +1161,39 @@
     )
     d_value = value_grad.reshape(seq_len, local_heads * HEAD).astype(jnp.bfloat16)
     d_qkv = jnp.concatenate([d_query, d_key, d_value], 1)
-    d_normed_attn = dot(d_qkv, full_qkv.T)
+    grad_qkv = dot(normed_attn.T, d_qkv).astype(BF)
+    d_normed_attn = dot(after(d_qkv, grad_qkv), full_qkv.T)
     d_attn_own = collect(d_normed_attn, 6)
-    grad_qkv = dot(normed_attn.T, d_qkv)
     bias_grads = jnp.sum(d_qkv.astype(F32), axis=0)
     grad_gain_one = jnp.sum(d_attn_own * inputs * attn_rms, axis=0)
     grad_tokens = d_hidden + norm_back(d_attn_own, inputs, attn_rms, gain_one)
-    grad_qkv = lax.psum_scatter(
-        grad_qkv.astype(BF), "fsdp", scatter_dimension=0, tiled=True
-    ).astype(F32)
-    grad_w_out = lax.psum_scatter(
-        grad_out.astype(BF), "fsdp", scatter_dimension=1, tiled=True
-    ).astype(F32)
+    grad_qkv = lax.psum_scatter(grad_qkv, "fsdp", scatter_dimension=0, tiled=True).astype(F32)
     if own_kernels:
-        mixer_out = home(after(mixer_parts, d_attn_own), 7)
-        grads = moe_grads(all_rows, all_d_rows, *kept)
+        grad_gu, grad_ed = expert_grads(*after(kept[:4], d_attn_own))
     output = (hidden + live_rows * mixer_out).astype(BF)
-    grad_gu, grad_ed, grad_sgu, grad_sdown_t = grads
-    grad_sdown_t = grad_sdown_t[:, :share]
     grad_expert_gate = grad_gu[..., :hidden_units]
     grad_expert_up = grad_gu[..., hp : hp + hidden_units]
     grad_expert_down = grad_ed[:, :hidden_units]
     grad_router = jnp.sum(grad_gu[..., hidden_units : hidden_units + expert_count], axis=0)
     grad_mix = grad_sgu[:, share]
-    packed_grad = jnp.concatenate(
-        [grad_sgu[:, :share], grad_sgu[:, shared_pad : shared_pad + share], grad_sdown_t], 1
-    ).astype(BF)
-    packed_grad = lax.all_to_all(
-        packed_grad.reshape(fsdp_count, -1, 3 * share), "fsdp", split_axis=0, concat_axis=0, tiled=True
-    ).transpose(1, 0, 2)
     grad_shared_gate, grad_shared_up, grad_shared_down = (
         packed_grad[:, :, n * share : (n + 1) * share].reshape(-1, fsdp_count * share).astype(F32)
         for n in range(3)
     )
-    sum_router, sum_mix, sum_gain_two = lax.psum((grad_router, grad_mix, grad_gain_two), whole_axes)
-    sum_gain_one = lax.psum(grad_gain_one, whole_axes)
-    own_bias = lax.psum(bias_grads, "fsdp")
+    bias_place = lax.dynamic_update_slice(
+        jnp.zeros((3, sp_count * head_width), F32), bias_grads.reshape(3, -1), (0, sp_place * head_width)
+    )
+    small = jnp.concatenate(
+        [jnp.stack([grad_gain_one, grad_gain_two, grad_mix]), bias_place, grad_router.T], 0
+    )
+    for axis_name in ("sp", "fsdp"):
+        bit = 1
+        while bit < lax.axis_size(axis_name):
+            small = small + swap(small, axis_name, bit)
+            bit *= 2
+    sum_gain_one, sum_gain_two, sum_mix = small[0], small[1], small[2]
+    own_bias = lax.dynamic_slice_in_dim(small[3:6], sp_place * head_width, head_width, 1)
+    sum_router = small[6:].T
     return (
         output,
         grad_tokens,
@@ -905,10 +1201,10 @@
         grad_qkv[:, :head_width],
         grad_qkv[:, head_width : 2 * head_width],
         grad_qkv[:, 2 * head_width :],
-        own_bias[:head_width],
-        own_bias[head_width : 2 * head_width],
-        own_bias[2 * head_width :],
-        grad_w_out,
+        own_bias[0],
+        own_bias[1],
+        own_bias[2],
+        grad_w_out.T,
         sum_gain_two,
         sum_router,
         sum_mix,

time: 1660 us -> 1390 us (0.84)
  Pallas kernels: 1170 us -> 759 us
  waiting for transfers between devices: 44.2 us -> 124 us
  local copies, waits for them, and re-layouts: 77 us -> 151 us
  blocking collectives: 54.5 us -> 0 us
  other arithmetic: 81 us -> 111 us
    pallas_call x8 -> x6, Pallas kernels: 1170 us -> 759 us  [the longest x1 402 us: moe_call(): pl.pallas_call(kernel, grid=(seqs, experts + token_steps), in_specs=[toke...]
    ppermute x3 -> x13, waiting for transfers between devices: 3.35 us -> 81.7 us  [swap(): lax.ppermute(values, axis_name, [(i, i ^ mask) for i in range(count)])]
    psum x2 -> x0, blocking collectives: 54.5 us -> none  [the longest x1 37.5 us: local(): sum_gain_one = lax.psum(grad_gain_one, whole_axes)]
    dynamic_slice x0 -> x10, local copies, waits for them, and re-layouts: none -> 42.8 us  [the longest x5 24 us: pick(): lax.dynamic_index_in_dim(crossed, place, 1, False)[:, h]]
    all_to_all x1, waiting for transfers between devices: 0.01 us -> 42.2 us  [local(): lax.all_to_all(after(packed, full_qkv), 'fsdp', split_axis=0, concat_axis...]
    psum x1 -> x0, waiting for transfers between devices: 39.2 us -> none  [local(): lax.psum((grad_router, grad_mix, grad_gain_two), whole_axes)]
    convert_element_type x2 -> x10, other arithmetic: 3.05 us -> 26.9 us  [the longest x8 23.4 us: add_low(): return (left.astype(F32) + right.astype(F32)).astype(BF)]
    unnamed x119 -> x150, local copies, waits for them, and re-layouts: 21.9 us -> 38.1 us
  transfers between devices with their start and end apart: 11 -> 20, of which waited for: 3 -> 8; matrix products, arithmetic and copies ran while one was open for 18% -> 25% of each run, Pallas kernels for 35% -> 8%
where the time goes in v2:
time: 1390 us; the launch traced here: 1380 us
  Pallas kernels  759 us (55%)
  matrix products  188 us (14%)
  local copies, waits for them, and re-layouts  151 us (11%)
  waiting for transfers between devices  124 us (9%)
  other arithmetic  111 us (8%)
  starting transfers between devices  22.8 us (2%)
  between operations  15.2 us (1%)
    pallas_call x1, Pallas kernels, moe_call(): pl.pallas_call(kernel, grid=(seqs, experts + token_steps), in_specs=[toke...  402 us
    pallas_call x3, Pallas kernels, scatter_call(): pl.pallas_call(functools.partial(sum_kernel if more is None else scatter_...  249 us
    pallas_call x2, Pallas kernels, gather_call(): pl.pallas_call(functools.partial(gather_kernel, count), out_shape=[whole]...  108 us
    ppermute x13, waiting for transfers between devices, swap(): lax.ppermute(values, axis_name, [(i, i ^ mask) for i in range(count)])  81.7 us
    dot_general x7, matrix products, dot(): return jnp.dot(left, right, preferred_element_type=F32)  80.7 us
    all_to_all x1, waiting for transfers between devices, local(): lax.all_to_all(after(packed, full_qkv), 'fsdp', split_axis=0, concat_axis...  42.2 us
    unnamed x150, local copies, waits for them, and re-layouts  38.1 us
    dot_general x1, matrix products, expert_grads(): jnp.einsum('ecd,ecf->edf', flat(rows), flat(d_gu), preferred_element_type...  28.6 us
  transfers between devices with their start and end apart: 20, of which 8 were waited for; matrix products, arithmetic and copies ran while one was open for 25% of the time, Pallas kernels for 8%

profile of v2, /device:TPU:0, one launch (start us, length us, event | category | flops | bytes accessed | tf_op | source)
XLA Modules:
  0.0 1378.0 jit_solution(16416657731139498107)
XLA Ops:
  15.4 4.7 copy.175
  42.2 71.7 %shard_map.348 = (bf16[1024,2048]{1,0:T(8,128)(2,1)}, bf16[1024,2048]{1,0:T(8,128)(2,1)}) custom-call(bf16[256,2048]{1,0:T(8,128)(2,1)} %get-tuple-element.560.refs_0_, bf16[256,2048]{1,0:T(8,128)(2,1)} %get-tuple-element.189.refs_1_), custom_call_target="tpu_custom_call" | custom-call | tf_op jit(solution)/shard_map/pallas_call | solution.py:182
  138.4 10.2 fusion.92
  163.2 42.2 %all-to-all-done = bf16[8,256,528]{1,2,0:T(8,128)(2,1)} async-done(((bf16[8,256,528]{1,2,0:T(8,128)(2,1)}), bf16[8,256,528]{1,2,0:T(8,128)(2,1)}, u32[]{:S(2)}, u32[]{:S(2)}) %all-to-all-start) | async-done | bytes 2162720 | tf_op jit(solution)/shard_map/all_to_all | solution.py:964
  208.7 21.6 %while.28 = (s32[]{:T(128)}, bf16[2,512,4,128]{3,2,1,0:T(4,128)(2,1)}, f32[2,4,512]{2,1,0:T(4,128)S(1)}, s32[2]{0:T(128)S(1)}, s32[1024]{0:T(1024)S(1)}, /*index...) while((s32[]{:T(128)}, ...), condition=%wide.region_7.8_spmd.clone, body=%wide.region_4.7_spmd.clone.sunk | while | flops 1100741120 | bytes 31537856 | solution.py:1043
  238.7 37.0 %shard_map.349 = f32[256,2048]{1,0:T(8,128)S(1)} custom-call(bf16[1,4,256,2048]{3,2,1,0:T(8,128)(2,1)S(1)} %bitcast.208), custom_call_target="tpu_custom_call" | custom-call | bytes 140000000 | tf_op jit(solution)/shard_map/pallas_call | solution.py:309
  286.3 14.6 %collective-permute-done.3 = bf16[256,2048]{1,0:T(8,128)(2,1)} collective-permute-done((bf16[256,2048]{1,0:T(8,128)(2,1)S(1)}, bf16[256,2048]{1,0:T(8,128)(2,1)}, u32[]{:S(2)}, u32[]{:S(2)}) %collective-permute-start.3) | collective-permute-done | bytes 1048608 | tf_op jit(solution)/shard_map/ppermute | solution.py:77
  300.9 402.4 %shard_map.350 = (bf16[8,1024,2048]{2,1,0:T(8,128)(2,1)}, bf16[8,1024,2048]{2,1,0:T(8,128)(2,1)}, bf16[4,1024,2048]{2,1,0:T(8,128)(2,1)}, bf16[4,1024,2048]{2,1,...) custom-call(bf16[256,2048]{1,0:T(8,128)(2,1)} %multiply_convert_fusi, ...), custom_call_target="tpu_custom_call" | custom-call | flops 212600881152 | bytes 1073741824 | tf_op jit(solution)/shard_map/pallas_call | solution.py:764
  703.4 177.6 %shard_map.351 = f32[256,2048]{1,0:T(8,128)S(1)} custom-call(bf16[4,4,256,2048]{3,2,1,0:T(8,128)(2,1)} %bitcast.223, bf16[4,4,256,2048]{3,2,1,0:T(8,128)(2,1)} %bitcast.224), custom_call_target="tpu_custom_call" | custom-call | bytes 560000000 | tf_op jit(solution)/shard_map/pallas_call | solution.py:309
  882.2 8.7 constant_dynamic-slice_fusion.2
  893.5 11.8 constant_dynamic-slice_fusion.1
  905.4 4.9 copy.260
  929.7 36.2 %shard_map.352 = bf16[1024,2048]{1,0:T(8,128)(2,1)} custom-call(bf16[256,2048]{1,0:T(8,128)(2,1)} %multiply_convert_fusion.1.refs_0_), custom_call_target="tpu_custom_call" | custom-call | tf_op jit(solution)/shard_map/pallas_call | solution.py:182
  993.2 5.2 convolution_convert_fusion.3
  998.4 16.8 %convolution_bitcast_fusion.1 = bf16[2048,256]{0,1:T(8,128)(2,1)S(1)} fusion(bf16[8,1024,2048]{2,1,0:T(8,128)(2,1)} %get-tuple-element.201, bf16[8,1024,256]{2,1,0:T(8,128)(2,1)} %get-tuple-element.202), kind=kOutput, calls=%fused_computation.106 | convolution fusion | flops 8589934592 | bytes 38797312 | tf_op jit(solution)/shard_map/dot_general | solution.py:72
  1017.2 25.1 %fusion.91 = (bf16[2048,512]{0,1:T(8,128)(2,1)S(1)}, f32[2048,512]{0,1:T(8,128)}) fusion(bf16[8,1024,2048]{2,1,0:T(8,128)(2,1)} %get-tuple-element.197, bf16[8,1024,512]{2,1,0:T(8,128)(2,1)} %get-tuple-element.200), kind=kOutput, calls=%fused_computation.220 | convolution fusion | flops 17180917760 | bytes 48234496 | tf_op jit(solution)/shard_map/dot_general | solution.py:72
  1049.7 5.7 convolution_convert_fusion.4
  1055.4 51.2 %collective-permute-done.4 = bf16[2,4,128,2048]{3,2,1,0:T(8,128)(2,1)} collective-permute-done((bf16[2,4,128,2048]{3,2,1,0:T(8,128)(2,1)}, bf16[2,4,128,2048]{3,2,1,0:T(8,128)(2,1)}, u32[]{:S(2)}, u32[]{:S(2)}) %collective-permute-start.4) | collective-permute-done | bytes 4194336 | tf_op jit(solution)/shard_map/ppermute | solution.py:77
  1123.0 66.9 %while.29 = (s32[]{:T(128)}, f32[1024,4,128]{0,2,1:T(8,128)S(1)}, f32[1024,4,128]{0,2,1:T(8,128)}, f32[2,512,4,128]{3,1,2,0:T(8,128)}, s32[2]{0:T(128)S(1)}, /*i...) while((s32[]{:T(128)}, f32[1024,4,128]{0,2,1:T(8,128)S(1)}, ...), condition=%wide.region_12.13_spmd.clone, body=%wide.region_10.12_spmd.clone.sunk | while | flops 2720266752 | bytes 163650544 | solution.py:1143
  1126.1 5.6 fusion.149
  1133.7 7.5 multiply_reduce_fusion.5
  1158.7 5.6 fusion.149
  1166.4 7.5 multiply_reduce_fusion.5
  1184.7 5.2 bitcast_add_fusion.5
  1218.6 9.0 convolution_convert_fusion
  1229.4 8.9 convolution_convert_fusion.1
  1238.3 34.0 %shard_map.353 = f32[256,2048]{1,0:T(8,128)S(1)} custom-call(bf16[1,4,256,2048]{3,2,1,0:T(8,128)(2,1)S(1)} %bitcast.207), custom_call_target="tpu_custom_call" | custom-call | bytes 140000000 | tf_op jit(solution)/shard_map/pallas_call | solution.py:309
  1272.4 28.6 %fusion.93 = f32[2,2048,768]{1,2,0:T(8,128)} fusion(bf16[2,3072,2048]{2,1,0:T(8,128)(2,1)} %bitcast.254, bf16[2,3072,768]{2,1,0:T(8,128)(2,1)} %bitcast.255), kind=kOutput, calls=%fused_computation.222 | convolution fusion | flops 19327352832 | bytes 47185920 | tf_op jit(solution)/shard_map/ecd,ecf->edf/dot_general | solution.py:832
  1304.5 10.8 fusion.82
  1315.3 17.4 %fusion.42 = f32[2,352,2048]{2,1,0:T(8,128)} fusion(bf16[2,3072,2048]{2,1,0:T(8,128)(2,1)} %bitcast.253, bf16[2,3072,384]{2,1,0:T(8,128)(2,1)} %bitcast.256), kind=kOutput, calls=%fused_computation.67 | convolution fusion | flops 8858370048 | bytes 35651584 | tf_op jit(solution)/shard_map/ecf,ecd->efd/dot_general | solution.py:834
  1352.5 9.6 collective-permute-done.12
  1364.1 4.7 fusion.52
  (382 shorter events, 274.9 us)
Async XLA Ops:
  7.2 126.5 %all-gather.3.cloned.1.call-start = ((), (), s32[]{:S(2)}) async-start(), calls=%async_computation.5 | async-start | bytes 7077888 | tf_op jit(solution)/shard_map/all_gather | solution.py:951
  9.3 20.9 %collective-permute-start = (s32[1,4,1024]{2,1,0:T(4,128)}, s32[1,4,1024]{2,1,0:T(4,128)S(1)}, u32[]{:S(2)}, u32[]{:S(2)}) collective-permute-start(s32[1,4,1024]{2,1,0:T(4,128)} %bitcast.239), channel_id=1, source_target_pairs={{0,4},{4,0},{8,12},{12,8},{16,20},{20,16},{24,28},{28,24},{1,5},{5... | collective-permute-start | bytes 49160 | tf_op jit(solution)/shard_map/ppermute | solution.py:77
  20.2 255.5 %copy-start.62 = (f32[256]{0:T(256)}, f32[256]{0:T(256)S(1)}, u32[]{:S(2)}) copy-start(f32[256]{0:T(256)S(1)} %compare_convert_fusion.1) | copy-start | bytes 3076
  30.2 5.7 collective-permute-start.1
  35.9 79.9 %collective-permute-start.2 = (s32[4,4,1024]{2,1,0:T(4,128)S(1)}, s32[4,4,1024]{2,1,0:T(4,128)S(1)}, u32[]{:S(2)}, u32[]{:S(2)}) collective-permute-start(s32[4,4,1024]{2,1,0:T(4,128)S(1)} %pad_add_fusion.1), channel_id=1, source_target_pairs={{0,16},{4,20},{8,24},{12,28},{16,0},{20,4},{24,8},{28,12},{1,17},{... | collective-permute-start | bytes 196616 | tf_op jit(solution)/shard_map/ppermute | solution.py:77
  38.8 75.0 %copy-start.43 = (bf16[2,352,2048]{2,1,0:T(8,128)(2,1)S(1)}, bf16[2,352,2048]{2,1,0:T(8,128)(2,1)}, u32[]{:S(2)}) copy-start(bf16[2,352,2048]{2,1,0:T(8,128)(2,1)} %param.45) | copy-start | bytes 8650756
  42.1 242.9 %copy-start.52 = (f32[2048]{0:T(1024)}, f32[2048]{0:T(1024)S(1)}, u32[]{:S(2)}) copy-start(f32[2048]{0:T(1024)S(1)} %convert_element_type.467) | copy-start | bytes 24580
  133.7 71.7 %all-to-all-start = ((bf16[8,256,528]{1,2,0:T(8,128)(2,1)}), bf16[8,256,528]{1,2,0:T(8,128)(2,1)}, u32[]{:S(2)}, u32[]{:S(2)}) async-start(bf16[8,256,528]{1,2,0:T(8,128)(2,1)} %maximum_bitcast_fusion), calls=%async_computation | async-start | bytes 4325376 | tf_op jit(solution)/shard_map/all_to_all | solution.py:964
  138.1 96.3 %all-gather.5.cloned.1.call-start = ((), (), s32[]{:S(2)}) async-start(), calls=%async_computation.6 | async-start | bytes 2359296 | tf_op jit(solution)/shard_map/all_gather | solution.py:954
  156.2 1033.7 %reduce-scatter.4.cloned.1.call-start = ((), (), s32[]{:S(2)}) async-start(), calls=%async_computation.7 | async-start | bytes 2359296 | tf_op jit(solution)/shard_map/reduce_scatter | solution.py:1093
  238.7 37.0 %copy-start.15 = (bf16[256,2048]{1,0:T(8,128)(2,1)S(1)}, bf16[256,2048]{1,0:T(8,128)(2,1)}, u32[]{:S(2)}) copy-start(bf16[256,2048]{1,0:T(8,128)(2,1)} %param.25) | copy-start | bytes 3145732
  277.0 23.9 %collective-permute-start.3 = (bf16[256,2048]{1,0:T(8,128)(2,1)S(1)}, bf16[256,2048]{1,0:T(8,128)(2,1)}, u32[]{:S(2)}, u32[]{:S(2)}) collective-permute-start(bf16[256,2048]{1,0:T(8,128)(2,1)S(1)} %copy-done.40), channel_id=1, source_target_pairs={{0,8},{4,12},{8,0},{12,4},{16,24},{20,28},{24,16},{28,20},{1,9},{5... | collective-permute-start | bytes 3145736 | tf_op jit(solution)/shard_map/ppermute | solution.py:77
  282.9 420.4 %copy-start.64 = (f32[256]{0:T(256)}, f32[256]{0:T(256)S(1)}, u32[]{:S(2)}) copy-start(f32[256]{0:T(256)S(1)} %add_rsqrt_fusion) | copy-start | bytes 3076
  703.3 177.6 %copy-start.12 = (f32[256,2048]{1,0:T(8,128)S(1)}, f32[256,2048]{1,0:T(8,128)}, u32[]{:S(2)}) copy-start(f32[256,2048]{1,0:T(8,128)} %copy-done.11) | copy-start | bytes 6291460
  703.3 177.6 %copy-start.53 = (f32[2048]{0:T(1024)S(1)}, f32[2048]{0:T(1024)}, u32[]{:S(2)}) copy-start(f32[2048]{0:T(1024)} %copy-done.52) | copy-start | bytes 24580
  703.3 177.6 %copy-start.65 = (f32[256]{0:T(256)S(1)}, f32[256]{0:T(256)}, u32[]{:S(2)}) copy-start(f32[256]{0:T(256)} %copy-done.64) | copy-start | bytes 3076
  881.0 46.3 %copy-start = (f32[256,2048]{1,0:T(8,128)}, f32[256,2048]{1,0:T(8,128)S(1)}, u32[]{:S(2)}) copy-start(f32[256,2048]{1,0:T(8,128)S(1)} %shard_map.351) | copy-start | bytes 6291460
  1015.2 91.4 %collective-permute-start.4 = (bf16[2,4,128,2048]{3,2,1,0:T(8,128)(2,1)}, bf16[2,4,128,2048]{3,2,1,0:T(8,128)(2,1)}, u32[]{:S(2)}, u32[]{:S(2)}) collective-permute-start(bf16[2,4,128,2048]{3,2,1,0:T(8,128)(2,1)} %pad_maximum_fusion), channel_id=1, source_target_pairs={{0,1},{1,0},{2,3},{3,2},{4,5},{5,4},{6,7},{7,6},{8,9},{9,8},{10,11... | collective-permute-start | bytes 12582920 | tf_op jit(solution)/shard_map/ppermute | solution.py:77
  1016.8 91.0 %collective-permute-start.5 = (bf16[2,4,128,2048]{3,2,1,0:T(8,128)(2,1)}, bf16[2,4,128,2048]{3,2,1,0:T(8,128)(2,1)}, u32[]{:S(2)}, u32[]{:S(2)}) collective-permute-start(bf16[2,4,128,2048]{3,2,1,0:T(8,128)(2,1)} %pad_maximum_fusion.1), channel_id=1, source_target_pairs={{0,2},{1,3},{2,0},{3,1},{4,6},{5,7},{6,4},{7,5},{8,10},{9,11},{10,... | collective-permute-start | bytes 12582920 | tf_op jit(solution)/shard_map/ppermute | solution.py:77
  1045.1 146.6 %all-to-all-start.1 = ((bf16[8,256,528]{1,2,0:T(8,128)(2,1)}), bf16[8,256,528]{1,2,0:T(8,128)(2,1)}, u32[]{:S(2)}, u32[]{:S(2)}) async-start(bf16[8,256,528]{1,2,0:T(8,128)(2,1)} %bitcast.174), calls=%async_computation.1 | async-start | bytes 4325376 | tf_op jit(solution)/shard_map/all_to_all | solution.py:1105
  1049.6 314.5 %reduce-scatter.6.cloned.1.call-start = ((), (), s32[]{:S(2)}) async-start(), calls=%async_computation.8 | async-start | bytes 5242880 | tf_op jit(solution)/shard_map/reduce_scatter | solution.py:936
  1049.7 58.1 %copy-start.19 = (bf16[2,4,128,2048]{3,2,1,0:T(8,128)(2,1)S(1)}, bf16[2,4,128,2048]{3,2,1,0:T(8,128)(2,1)}, u32[]{:S(2)}) copy-start(bf16[2,4,128,2048]{3,2,1,0:T(8,128)(2,1)} %pad_maximum_fusion.3) | copy-start | bytes 12582916
  1114.4 77.4 %collective-permute-start.7 = (bf16[4,128,2048]{2,1,0:T(8,128)(2,1)}, bf16[4,128,2048]{2,1,0:T(8,128)(2,1)}, u32[]{:S(2)}, u32[]{:S(2)}) collective-permute-start(bf16[4,128,2048]{2,1,0:T(8,128)(2,1)} %get-tuple-element.521), channel_id=1, source_target_pairs={{0,1},{1,0},{2,3},{3,2},{4,5},{5,4},{6,7},{7,6},{8,9},{9,8},{10,11... | collective-permute-start | bytes 6291464 | tf_op jit(solution)/shard_map/ppermute | solution.py:77
  1122.2 69.5 %collective-permute-start.6 = (bf16[4,128,2048]{2,1,0:T(8,128)(2,1)}, bf16[4,128,2048]{2,1,0:T(8,128)(2,1)}, u32[]{:S(2)}, u32[]{:S(2)}) collective-permute-start(bf16[4,128,2048]{2,1,0:T(8,128)(2,1)} %get-tuple-element.523), channel_id=1, source_target_pairs={{0,2},{1,3},{2,0},{3,1},{4,6},{5,7},{6,4},{7,5},{8,10},{9,11},{10,... | collective-permute-start | bytes 6291464 | tf_op jit(solution)/shard_map/ppermute | solution.py:77
  1200.3 168.5 %reduce-scatter.8.cloned.1.call-start = ((), (), s32[]{:S(2)}) async-start(), calls=%async_computation.9 | async-start | bytes 7077888 | tf_op jit(solution)/shard_map/reduce_scatter | solution.py:1170
  1272.4 29.7 %copy-start.2 = (f32[256,2048]{1,0:T(8,128)}, f32[256,2048]{1,0:T(8,128)S(1)}, u32[]{:S(2)}) copy-start(f32[256,2048]{1,0:T(8,128)S(1)} %shard_map.353) | copy-start | bytes 6291460
  1272.4 29.7 %copy-start.16 = (bf16[256,2048]{1,0:T(8,128)(2,1)S(1)}, bf16[256,2048]{1,0:T(8,128)(2,1)}, u32[]{:S(2)}) copy-start(bf16[256,2048]{1,0:T(8,128)(2,1)} %param.25) | copy-start | bytes 3145732
  1303.4 31.0 %collective-permute-start.8 = (f32[22,2048]{1,0:T(8,128)S(1)}, f32[22,2048]{1,0:T(8,128)S(1)}, u32[]{:S(2)}, u32[]{:S(2)}) collective-permute-start(f32[22,2048]{1,0:T(8,128)S(1)} %concatenate.74), channel_id=1, source_target_pairs={{0,1},{1,0},{2,3},{3,2},{4,5},{5,4},{6,7},{7,6},{8,9},{9,8},{10,11... | collective-permute-start | bytes 540680 | tf_op jit(solution)/shard_map/ppermute | solution.py:77
  1334.5 5.7 collective-permute-start.9
  1340.2 1.5 collective-permute-start.10
  1341.7 8.3 collective-permute-start.11
  1350.1 12.0 collective-permute-start.12
  (74 other events, 443.3 us)
Sparse Core Ops, SparseCore 0:
  10.2 70.1 all-gather.2
  156.3 48.5 all-gather.4
  998.5 34.2 reduce-scatter.3
  1200.4 74.8 reduce-scatter.5
  1277.6 72.7 reduce-scatter.7

commit v3 on v2

--- a/solution.py
+++ b/solution.py
@@ -943,15 +943,13 @@
     normed_attn = (inputs * attn_rms * gain_one).astype(BF)
     upstream = cotangent.astype(F32)
     d_mixer = (live_rows * upstream).astype(BF)
-    d_mixer_own = d_mixer
-    if own_kernels:
-        normed_attn, d_mixer = gather_call([normed_attn, d_mixer], 1)
-    else:
-        normed_attn, d_mixer = spread(normed_attn, 1), spread(d_mixer, 1)
+    normed_attn = spread(normed_attn, 1)
     full_qkv = lax.all_gather(
         jnp.concatenate([w_query, w_key, w_value], 1), "fsdp", axis=0, tiled=True
     )
-    full_out_t = lax.all_gather(after(w_out.T, full_qkv), "fsdp", axis=0, tiled=True)
+    d_mixer_own = after(d_mixer, (full_qkv, normed_attn))
+    d_mixer = lax.all_gather(d_mixer_own, "sp", axis=0, tiled=True)
+    full_out_t = lax.all_gather(after(w_out.T, d_mixer), "fsdp", axis=0, tiled=True)
     share = shared_gate.shape[1] // fsdp_count
     packed = jnp.concatenate(
         [
@@ -1014,33 +1012,37 @@
     key_rot = rotate(key_lin.reshape(seq_len, local_heads, HEAD), cosine, sine_table).astype(BF)
 
     def block_scores(block_index):
-        offset = block_index * row_block
-        query_block = lax.dynamic_slice_in_dim(query_rot, offset, row_block)
+        start, stop = block_index * row_block, (block_index + 1) * row_block
+        query_block = query_rot[start:stop]
         raw_scores = (
-            jnp.einsum("qhd,khd->hqk", query_block, key_rot, preferred_element_type=jnp.float32)
+            jnp.einsum(
+                "qhd,khd->hqk", query_block, key_rot[:stop], preferred_element_type=jnp.float32
+            )
             * score_scale
         )
-        seg_block = lax.dynamic_slice_in_dim(segments, offset, row_block)
-        pos_block = offset + jnp.arange(row_block, dtype=jnp.int32)
         allowed = (
-            (seg_block[:, None] == segments[None, :]) & (position[None, :] <= pos_block[:, None])
+            (segments[start:stop, None] == segments[None, :stop])
+            & (position[None, :stop] <= position[start:stop, None])
         )[None]
         return (query_block, raw_scores, allowed)
 
     def attend_block(block_index):
-        score_parts = block_scores(block_index)
-        raw_scores = score_parts[1]
-        allowed = score_parts[2]
+        query_block, raw_scores, allowed = block_scores(block_index)
         row_max = jnp.max(jnp.where(allowed, raw_scores, -jnp.inf), axis=-1, keepdims=True)
         exponent = jnp.exp(jnp.where(allowed, raw_scores - row_max, -jnp.inf))
         row_total = jnp.sum(exponent, axis=-1, keepdims=True)
-        probability = (exponent / row_total).astype(jnp.bfloat16)
+        probability = (exponent / row_total).astype(BF)
         attended_block = jnp.einsum(
-            "hqk,khd->qhd", probability, value_rows, preferred_element_type=jnp.float32
-        ).astype(jnp.bfloat16)
-        return (attended_block, (row_max + jnp.log(row_total))[..., 0])
-
-    attended, log_total = lax.map(attend_block, jnp.arange(block_count))
+            "hqk,khd->qhd",
+            probability,
+            value_rows[: raw_scores.shape[2]],
+            preferred_element_type=jnp.float32,
+        ).astype(BF)
+        return (attended_block, row_max + jnp.log(row_total))
+
+    blocks = [attend_block(n) for n in range(block_count)]
+    log_total = [block[1] for block in blocks]
+    attended = jnp.concatenate([block[0] for block in blocks], 0)
     attended = attended.reshape(seq_len, local_heads * HEAD)
     attn_out = collect(nt_dot(attended, full_out_t), 2)
     hidden = inputs + live_rows * attn_out
@@ -1111,38 +1113,42 @@
         d_attended, slow = lax.optimization_barrier((d_attended, slow))
         slow = slow_second(*slow)
 
-    def attend_back(carry_in, block_index):
-        key_grad, value_grad = carry_in
+    def attend_back(block_index):
         query_block, raw_scores, allowed = block_scores(block_index)
-        offset = block_index * row_block
-        log_block = lax.dynamic_index_in_dim(log_total, block_index, keepdims=False)
-        prob_full = jnp.exp(jnp.where(allowed, raw_scores - log_block[..., None], -jnp.inf))
-        prob_low = prob_full.astype(jnp.bfloat16)
-        grad_block = lax.dynamic_slice_in_dim(d_attended, offset, row_block)
+        start, stop = block_index * row_block, (block_index + 1) * row_block
+        prob_full = jnp.exp(jnp.where(allowed, raw_scores - log_total[block_index], -jnp.inf))
+        prob_low = prob_full.astype(BF)
+        grad_block = d_attended[start:stop]
         d_prob = jnp.einsum(
-            "qhd,khd->hqk", grad_block, value_rows, preferred_element_type=jnp.float32
+            "qhd,khd->hqk", grad_block, value_rows[:stop], preferred_element_type=jnp.float32
         )
         d_scores = (
             prob_full * (d_prob - jnp.sum(prob_full * d_prob, axis=-1, keepdims=True))
-        ).astype(jnp.bfloat16)
+        ).astype(BF)
         query_grad = (
-            jnp.einsum("hqk,khd->qhd", d_scores, key_rot, preferred_element_type=jnp.float32)
+            jnp.einsum("hqk,khd->qhd", d_scores, key_rot[:stop], preferred_element_type=jnp.float32)
             * score_scale
         )
         key_grad = (
-            key_grad
-            + jnp.einsum("hqk,qhd->khd", d_scores, query_block, preferred_element_type=jnp.float32)
+            jnp.einsum("hqk,qhd->khd", d_scores, query_block, preferred_element_type=jnp.float32)
             * score_scale
         )
-        value_grad = value_grad + jnp.einsum(
+        value_grad = jnp.einsum(
             "hqk,qhd->khd", prob_low, grad_block, preferred_element_type=jnp.float32
         )
-        return ((key_grad, value_grad), query_grad)
-
-    zero_grad = jnp.zeros((seq_len, local_heads, HEAD), jnp.float32)
-    (key_grad, value_grad), query_grad = lax.scan(
-        attend_back, (zero_grad, zero_grad), jnp.arange(block_count)
-    )
+        return query_grad, key_grad, value_grad
+
+    query_grads = []
+    for block_index in range(block_count)[::-1]:
+        query_part, key_part, value_part = attend_back(block_index)
+        query_grads.insert(0, query_part)
+        if block_index == block_count - 1:
+            key_grad, value_grad = key_part, value_part
+        else:
+            stop = (block_index + 1) * row_block
+            key_grad = key_grad.at[:stop].add(key_part)
+            value_grad = value_grad.at[:stop].add(value_part)
+    query_grad = jnp.concatenate(query_grads, 0)
     if own_kernels:
         query_grad, slow, packed_grad, grad_w_out = lax.optimization_barrier(
             (query_grad, slow, packed_grad, grad_w_out)

time: 1390 us -> 1310 us (0.942)
  Pallas kernels: 759 us -> 729 us
  local copies, waits for them, and re-layouts: 151 us -> 129 us
  matrix products: 188 us -> 167 us
    pallas_call x2, Pallas kernels: 108 us -> 73.8 us  [gather_call(): pl.pallas_call(functools.partial(gather_kernel, count), out_shape=[whole]...]
    all_to_all x1, waiting for transfers between devices: 42.2 us -> 23.8 us  [local(): lax.all_to_all(after(packed, full_qkv), 'fsdp', split_axis=0, concat_axis...]
    all_gather x1 -> x2, waiting for transfers between devices: 0.01 us -> 15.7 us  [the longest x1 15.7 us: local(): lax.all_gather(after(w_out.T, d_mixer), 'fsdp', axis=0, tiled=True)]
    dot_general x10 -> x8, matrix products: 40.5 us -> 26.2 us  [the longest x2 10.9 us: attend_back(): jnp.einsum('qhd,khd->hqk', grad_block, value_rows[:stop], preferred_eleme...]
    unnamed x150 -> x173, local copies, waits for them, and re-layouts: 38.1 us -> 40.9 us
  transfers between devices with their start and end apart: 20 -> 21, of which waited for: 8 -> 10; matrix products, arithmetic and copies ran while one was open for 25% -> 24% of each run, Pallas kernels for 8% -> 8%
where the time goes in v3:
time: 1310 us
  Pallas kernels  729 us (56%)
  matrix products  167 us (13%)
  waiting for transfers between devices  130 us (10%)
  local copies, waits for them, and re-layouts  129 us (10%)
  other arithmetic  114 us (9%)
  starting transfers between devices  22.3 us (2%)
  between operations  16.1 us (1%)
    pallas_call x1, Pallas kernels, moe_call(): pl.pallas_call(kernel, grid=(seqs, experts + token_steps), in_specs=[toke...  405 us
    pallas_call x3, Pallas kernels, scatter_call(): pl.pallas_call(functools.partial(sum_kernel if more is None else scatter_...  250 us
    ppermute x13, waiting for transfers between devices, swap(): lax.ppermute(values, axis_name, [(i, i ^ mask) for i in range(count)])  90.2 us
    dot_general x7, matrix products, dot(): return jnp.dot(left, right, preferred_element_type=F32)  79.5 us
    pallas_call x2, Pallas kernels, gather_call(): pl.pallas_call(functools.partial(gather_kernel, count), out_shape=[whole]...  73.8 us
    unnamed x173, local copies, waits for them, and re-layouts  40.9 us
    dot_general x1, matrix products, expert_grads(): jnp.einsum('ecd,ecf->edf', flat(rows), flat(d_gu), preferred_element_type...  29.1 us
  transfers between devices with their start and end apart: 21, of which 10 were waited for; matrix products, arithmetic and copies ran while one was open for 24% of the time, Pallas kernels for 8%

profile of v3, /device:TPU:0, one launch (start us, length us, event | category | flops | bytes accessed | tf_op | source)
XLA Modules:
  0.0 1306.8 jit_solution(9713061625982638113)
XLA Ops:
  10.6 4.6 copy.154
  15.5 4.6 copy.153
  45.6 37.2 %shard_map.348 = bf16[1024,2048]{1,0:T(8,128)(2,1)} custom-call(bf16[256,2048]{1,0:T(8,128)(2,1)} %fusion.23.refs_0_), custom_call_target="tpu_custom_call" | custom-call | tf_op jit(solution)/shard_map/pallas_call | solution.py:182
  96.7 4.6 bitcast_select_fusion
  109.7 10.1 fusion.117
  127.5 4.7 fusion.110
  136.1 23.8 %all-to-all-done = bf16[8,256,528]{1,2,0:T(8,128)(2,1)} async-done(((bf16[8,256,528]{1,2,0:T(8,128)(2,1)}), bf16[8,256,528]{1,2,0:T(8,128)(2,1)}, u32[]{:S(2)}, u32[]{:S(2)}) %all-to-all-start) | async-done | bytes 2162720 | tf_op jit(solution)/shard_map/all_to_all | solution.py:962
  173.8 5.3 select_reduce_fusion
  179.2 4.9 fusion.1
  192.9 15.7 %all-gather.8.cloned.1.call-done = bf16[2048,512]{0,1:T(8,128)(2,1)} async-done(((bf16[256,512]{0,1:T(8,128)(2,1)}), bf16[2048,512]{0,1:T(8,128)(2,1)}) %all-gather.8.cloned.1.call-update) | async-done | bytes 2097168 | tf_op jit(solution)/shard_map/all_gather | solution.py:952
  212.6 38.3 %shard_map.349 = f32[256,2048]{1,0:T(8,128)S(1)} custom-call(bf16[1,4,256,2048]{3,2,1,0:T(8,128)(2,1)S(1)} %bitcast.195), custom_call_target="tpu_custom_call" | custom-call | bytes 140000000 | tf_op jit(solution)/shard_map/pallas_call | solution.py:309
  253.9 404.6 %shard_map.350 = (bf16[8,1024,2048]{2,1,0:T(8,128)(2,1)}, bf16[8,1024,2048]{2,1,0:T(8,128)(2,1)}, bf16[4,1024,2048]{2,1,0:T(8,128)(2,1)}, bf16[4,1024,2048]{2,1,...) custom-call(bf16[256,2048]{1,0:T(8,128)(2,1)} %multiply_convert_fusi, ...), custom_call_target="tpu_custom_call" | custom-call | flops 212600881152 | bytes 1073741824 | tf_op jit(solution)/shard_map/pallas_call | solution.py:764
  658.5 178.4 %shard_map.351 = f32[256,2048]{1,0:T(8,128)S(1)} custom-call(bf16[4,4,256,2048]{3,2,1,0:T(8,128)(2,1)} %bitcast.208, bf16[4,4,256,2048]{3,2,1,0:T(8,128)(2,1)} %bitcast.209), custom_call_target="tpu_custom_call" | custom-call | bytes 560000000 | tf_op jit(solution)/shard_map/pallas_call | solution.py:309
  840.7 36.6 %shard_map.352 = bf16[1024,2048]{1,0:T(8,128)(2,1)} custom-call(bf16[256,2048]{1,0:T(8,128)(2,1)} %multiply_convert_fusion.2.refs_0_), custom_call_target="tpu_custom_call" | custom-call | tf_op jit(solution)/shard_map/pallas_call | solution.py:182
  877.3 9.0 constant_dynamic-slice_fusion.1
  886.9 11.5 constant_dynamic-slice_fusion.2
  938.9 16.8 %convolution_bitcast_fusion.1 = bf16[2048,256]{0,1:T(8,128)(2,1)S(1)} fusion(bf16[8,1024,2048]{2,1,0:T(8,128)(2,1)} %get-tuple-element.109, bf16[8,1024,256]{2,1,0:T(8,128)(2,1)} %get-tuple-element.110), kind=kOutput, calls=%fused_computation.78 | convolution fusion | flops 8589934592 | bytes 38797312 | tf_op jit(solution)/shard_map/dot_general | solution.py:72
  957.8 25.1 %fusion.116 = (bf16[2048,512]{0,1:T(8,128)(2,1)S(1)}, f32[2048,512]{0,1:T(8,128)}) fusion(bf16[8,1024,2048]{2,1,0:T(8,128)(2,1)} %get-tuple-element.105, bf16[8,1024,512]{2,1,0:T(8,128)(2,1)} %get-tuple-element.108), kind=kOutput, calls=%fused_computation.249 | convolution fusion | flops 17180917760 | bytes 48234496 | tf_op jit(solution)/shard_map/dot_general | solution.py:72
  989.5 5.7 convolution_convert_fusion.4
  995.1 52.5 %collective-permute-done.4 = bf16[2,4,128,2048]{3,2,1,0:T(8,128)(2,1)} collective-permute-done((bf16[2,4,128,2048]{3,2,1,0:T(8,128)(2,1)}, bf16[2,4,128,2048]{3,2,1,0:T(8,128)(2,1)}, u32[]{:S(2)}, u32[]{:S(2)}) %collective-permute-start.4) | collective-permute-done | bytes 4194336 | tf_op jit(solution)/shard_map/ppermute | solution.py:77
  1069.7 7.4 multiply_reduce_fusion
  1081.3 7.2 multiply_convert_fusion
  1090.7 19.2 %collective-permute-done.6 = bf16[4,128,2048]{2,1,0:T(8,128)(2,1)} collective-permute-done((bf16[4,128,2048]{2,1,0:T(8,128)(2,1)}, bf16[4,128,2048]{2,1,0:T(8,128)(2,1)}, u32[]{:S(2)}, u32[]{:S(2)}) %collective-permute-start.6) | collective-permute-done | bytes 2097184 | tf_op jit(solution)/shard_map/ppermute | solution.py:77
  1120.5 6.8 fusion.8
  1145.4 9.0 convolution_convert_fusion
  1156.3 8.9 convolution_convert_fusion.1
  1165.2 33.8 %shard_map.353 = f32[256,2048]{1,0:T(8,128)S(1)} custom-call(bf16[1,4,256,2048]{3,2,1,0:T(8,128)(2,1)S(1)} %bitcast.194), custom_call_target="tpu_custom_call" | custom-call | bytes 140000000 | tf_op jit(solution)/shard_map/pallas_call | solution.py:309
  1199.1 29.1 %fusion.118 = f32[2,2048,768]{1,2,0:T(8,128)} fusion(bf16[2,3072,2048]{2,1,0:T(8,128)(2,1)} %bitcast.242, bf16[2,3072,768]{2,1,0:T(8,128)(2,1)} %bitcast.243), kind=kOutput, calls=%fused_computation.251 | convolution fusion | flops 19327352832 | bytes 47185920 | tf_op jit(solution)/shard_map/ecd,ecf->edf/dot_general | solution.py:832
  1231.4 10.8 fusion.106
  1242.3 17.4 %fusion.5 = f32[2,352,2048]{2,1,0:T(8,128)} fusion(bf16[2,3072,2048]{2,1,0:T(8,128)(2,1)} %bitcast.241, bf16[2,3072,384]{2,1,0:T(8,128)(2,1)} %bitcast.244), kind=kOutput, calls=%fused_computation.25 | convolution fusion | flops 8858370048 | bytes 35651584 | tf_op jit(solution)/shard_map/ecf,ecd->efd/dot_general | solution.py:834
  1279.1 11.2 collective-permute-done.12
  1292.4 4.7 fusion.27
  (354 shorter events, 231.3 us)
Async XLA Ops:
  7.2 89.5 %all-gather.4.cloned.1.call-start = ((), (), s32[]{:S(2)}) async-start(), calls=%async_computation.5 | async-start | bytes 7077888 | tf_op jit(solution)/shard_map/all_gather | solution.py:947
  9.3 169.8 %all-gather.6.cloned.1.call-start = ((), (), s32[]{:S(2)}) async-start(), calls=%async_computation.6 | async-start | bytes 5242880 | tf_op jit(solution)/shard_map/all_gather | solution.py:951
  9.4 23.2 %collective-permute-start = (s32[1,4,1024]{2,1,0:T(4,128)}, s32[1,4,1024]{2,1,0:T(4,128)S(1)}, u32[]{:S(2)}, u32[]{:S(2)}) collective-permute-start(s32[1,4,1024]{2,1,0:T(4,128)} %bitcast.227), channel_id=1, source_target_pairs={{0,4},{4,0},{8,12},{12,8},{16,20},{20,16},{24,28},{28,24},{1,5},{5... | collective-permute-start | bytes 49160 | tf_op jit(solution)/shard_map/ppermute | solution.py:77
  20.2 230.6 %copy-start.66 = (f32[256]{0:T(256)}, f32[256]{0:T(256)S(1)}, u32[]{:S(2)}) copy-start(f32[256]{0:T(256)S(1)} %compare_convert_fusion.1) | copy-start | bytes 3076
  20.8 163.3 %copy-start.46 = (pred[512,512]{0,1:T(8,128)(4,1)}, pred[512,512]{0,1:T(8,128)(4,1)S(1)}, u32[]{:S(2)}) copy-start(pred[512,512]{0,1:T(8,128)(4,1)S(1)} %compare_and_fusion) | copy-start | bytes 786436
  32.6 7.8 collective-permute-start.1
  40.4 46.4 %collective-permute-start.2 = (s32[4,4,1024]{2,1,0:T(4,128)S(1)}, s32[4,4,1024]{2,1,0:T(4,128)S(1)}, u32[]{:S(2)}, u32[]{:S(2)}) collective-permute-start(s32[4,4,1024]{2,1,0:T(4,128)S(1)} %pad_add_fusion.1), channel_id=1, source_target_pairs={{0,16},{4,20},{8,24},{12,28},{16,0},{20,4},{24,8},{28,12},{1,17},{... | collective-permute-start | bytes 196616 | tf_op jit(solution)/shard_map/ppermute | solution.py:77
  42.9 39.9 %copy-start.78 = (bf16[512]{0:T(512)(128)(2,1)S(1)}, bf16[512]{0:T(512)(128)(2,1)}, u32[]{:S(2)}) copy-start(bf16[512]{0:T(512)(128)(2,1)} %param.33) | copy-start | bytes 3076
  42.9 39.9 %copy-start.74 = (bf16[2048]{0:T(1024)(128)(2,1)S(1)}, bf16[2048]{0:T(1024)(128)(2,1)}, u32[]{:S(2)}) copy-start(bf16[2048]{0:T(1024)(128)(2,1)} %param.37) | copy-start | bytes 12292
  42.9 39.9 %copy-start.75 = (bf16[2048]{0:T(1024)(128)(2,1)S(1)}, bf16[2048]{0:T(1024)(128)(2,1)}, u32[]{:S(2)}) copy-start(bf16[2048]{0:T(1024)(128)(2,1)} %param.39) | copy-start | bytes 12292
  82.8 168.6 %copy-start.56 = (f32[2048]{0:T(1024)}, f32[2048]{0:T(1024)S(1)}, u32[]{:S(2)}) copy-start(f32[2048]{0:T(1024)S(1)} %convert_element_type.488) | copy-start | bytes 24580
  105.1 54.8 %all-to-all-start = ((bf16[8,256,528]{1,2,0:T(8,128)(2,1)}), bf16[8,256,528]{1,2,0:T(8,128)(2,1)}, u32[]{:S(2)}, u32[]{:S(2)}) async-start(bf16[8,256,528]{1,2,0:T(8,128)(2,1)} %maximum_bitcast_fusion), calls=%async_computation | async-start | bytes 4325376 | tf_op jit(solution)/shard_map/all_to_all | solution.py:962
  109.5 99.1 %all-gather.8.cloned.1.call-start = ((), (), s32[]{:S(2)}) async-start(), calls=%async_computation.7 | async-start | bytes 2359296 | tf_op jit(solution)/shard_map/all_gather | solution.py:952
  133.3 40.5 %copy-start.27 = (bf16[1024,4,64]{2,0,1:T(8,128)(2,1)}, bf16[1024,4,64]{2,0,1:T(8,128)(2,1)S(1)}, u32[]{:S(2)}) copy-start(bf16[1024,4,64]{2,0,1:T(8,128)(2,1)S(1)} %get-tuple-element.225) | copy-start | bytes 1572868
  161.8 92.1 %collective-permute-start.3 = (bf16[256,2048]{1,0:T(8,128)(2,1)}, bf16[256,2048]{1,0:T(8,128)(2,1)}, u32[]{:S(2)}, u32[]{:S(2)}) collective-permute-start(bf16[256,2048]{1,0:T(8,128)(2,1)} %fusion.28), channel_id=1, source_target_pairs={{0,8},{4,12},{8,0},{12,4},{16,24},{20,28},{24,16},{28,20},{1,9},{5... | collective-permute-start | bytes 3145736 | tf_op jit(solution)/shard_map/ppermute | solution.py:77
  179.1 899.2 %reduce-scatter.4.cloned.1.call-start = ((), (), s32[]{:S(2)}) async-start(), calls=%async_computation.8 | async-start | bytes 2359296 | tf_op jit(solution)/shard_map/reduce_scatter | solution.py:1095
  658.5 178.4 %copy-start.4 = (f32[256,2048]{1,0:T(8,128)S(1)}, f32[256,2048]{1,0:T(8,128)}, u32[]{:S(2)}) copy-start(f32[256,2048]{1,0:T(8,128)} %copy-done.3) | copy-start | bytes 6291460
  658.5 178.4 %copy-start.57 = (f32[2048]{0:T(1024)S(1)}, f32[2048]{0:T(1024)}, u32[]{:S(2)}) copy-start(f32[2048]{0:T(1024)} %copy-done.56) | copy-start | bytes 24580
  658.5 178.4 %copy-start.69 = (f32[256]{0:T(256)S(1)}, f32[256]{0:T(256)}, u32[]{:S(2)}) copy-start(f32[256]{0:T(256)} %copy-done.68) | copy-start | bytes 3076
  955.8 91.8 %collective-permute-start.4 = (bf16[2,4,128,2048]{3,2,1,0:T(8,128)(2,1)}, bf16[2,4,128,2048]{3,2,1,0:T(8,128)(2,1)}, u32[]{:S(2)}, u32[]{:S(2)}) collective-permute-start(bf16[2,4,128,2048]{3,2,1,0:T(8,128)(2,1)} %pad_maximum_fusion), channel_id=1, source_target_pairs={{0,1},{1,0},{2,3},{3,2},{4,5},{5,4},{6,7},{7,6},{8,9},{9,8},{10,11... | collective-permute-start | bytes 12582920 | tf_op jit(solution)/shard_map/ppermute | solution.py:77
  956.4 91.3 %collective-permute-start.5 = (bf16[2,4,128,2048]{3,2,1,0:T(8,128)(2,1)}, bf16[2,4,128,2048]{3,2,1,0:T(8,128)(2,1)}, u32[]{:S(2)}, u32[]{:S(2)}) collective-permute-start(bf16[2,4,128,2048]{3,2,1,0:T(8,128)(2,1)} %pad_maximum_fusion.1), channel_id=1, source_target_pairs={{0,2},{1,3},{2,0},{3,1},{4,6},{5,7},{6,4},{7,5},{8,10},{9,11},{10,... | collective-permute-start | bytes 12582920 | tf_op jit(solution)/shard_map/ppermute | solution.py:77
  984.8 105.9 %all-to-all-start.1 = ((bf16[8,256,528]{1,2,0:T(8,128)(2,1)}), bf16[8,256,528]{1,2,0:T(8,128)(2,1)}, u32[]{:S(2)}, u32[]{:S(2)}) async-start(bf16[8,256,528]{1,2,0:T(8,128)(2,1)} %bitcast.192), calls=%async_computation.1 | async-start | bytes 4325376 | tf_op jit(solution)/shard_map/all_to_all | solution.py:1107
  989.2 303.2 %reduce-scatter.6.cloned.1.call-start = ((), (), s32[]{:S(2)}) async-start(), calls=%async_computation.9 | async-start | bytes 5242880 | tf_op jit(solution)/shard_map/reduce_scatter | solution.py:936
  989.5 58.2 %copy-start.14 = (bf16[2,4,128,2048]{3,2,1,0:T(8,128)(2,1)S(1)}, bf16[2,4,128,2048]{3,2,1,0:T(8,128)(2,1)}, u32[]{:S(2)}) copy-start(bf16[2,4,128,2048]{3,2,1,0:T(8,128)(2,1)} %pad_maximum_fusion.2) | copy-start | bytes 12582916
  1064.0 45.9 %collective-permute-start.6 = (bf16[4,128,2048]{2,1,0:T(8,128)(2,1)}, bf16[4,128,2048]{2,1,0:T(8,128)(2,1)}, u32[]{:S(2)}, u32[]{:S(2)}) collective-permute-start(bf16[4,128,2048]{2,1,0:T(8,128)(2,1)} %get-tuple-element.235), channel_id=1, source_target_pairs={{0,2},{1,3},{2,0},{3,1},{4,6},{5,7},{6,4},{7,5},{8,10},{9,11},{10,... | collective-permute-start | bytes 6291464 | tf_op jit(solution)/shard_map/ppermute | solution.py:77
  1065.7 45.4 %collective-permute-start.7 = (bf16[4,128,2048]{2,1,0:T(8,128)(2,1)}, bf16[4,128,2048]{2,1,0:T(8,128)(2,1)}, u32[]{:S(2)}, u32[]{:S(2)}) collective-permute-start(bf16[4,128,2048]{2,1,0:T(8,128)(2,1)} %get-tuple-element.233), channel_id=1, source_target_pairs={{0,1},{1,0},{2,3},{3,2},{4,5},{5,4},{6,7},{7,6},{8,9},{9,8},{10,11... | collective-permute-start | bytes 6291464 | tf_op jit(solution)/shard_map/ppermute | solution.py:77
  1119.4 177.7 %reduce-scatter.8.cloned.1.call-start = ((), (), s32[]{:S(2)}) async-start(), calls=%async_computation.10 | async-start | bytes 7077888 | tf_op jit(solution)/shard_map/reduce_scatter | solution.py:1176
  1230.6 30.7 %collective-permute-start.8 = (f32[22,2048]{1,0:T(8,128)S(1)}, f32[22,2048]{1,0:T(8,128)S(1)}, u32[]{:S(2)}, u32[]{:S(2)}) collective-permute-start(f32[22,2048]{1,0:T(8,128)S(1)} %concatenate.86), channel_id=1, source_target_pairs={{0,1},{1,0},{2,3},{3,2},{4,5},{5,4},{6,7},{7,6},{8,9},{9,8},{10,11... | collective-permute-start | bytes 540680 | tf_op jit(solution)/shard_map/ppermute | solution.py:77
  1261.4 5.7 collective-permute-start.9
  1267.2 1.5 collective-permute-start.10
  1268.7 9.3 collective-permute-start.11
  1278.0 12.3 collective-permute-start.12
  (71 other events, 615.5 us)
Sparse Core Ops, SparseCore 0:
  10.2 70.1 all-gather.3
  96.8 52.1 all-gather.5
  179.3 29.2 all-gather.7
  939.0 33.6 reduce-scatter.3
  1119.5 73.9 reduce-scatter.5
  1195.8 70.3 reduce-scatter.7

commit v4 on v3

--- a/solution.py
+++ b/solution.py
@@ -880,7 +880,7 @@
     capacity = 3 * seq_len * top_count // (2 * expert_count)
     local_heads = w_query.shape[1] // HEAD
     head_width = w_query.shape[1]
-    row_block = min(512, seq_len)
+    row_block = min(256, seq_len)
     block_count = seq_len // row_block
     score_scale = HEAD ** (-0.5)
     own_segments = lax.dynamic_slice_in_dim(segments, sp_place * tok_count, tok_count)

time: 1310 us -> 1310 us (level)
    unnamed x173 -> x247, local copies, waits for them, and re-layouts: 40.9 us -> 42.4 us
  transfers between devices with their start and end apart: 21 -> 21, of which waited for: 10 -> 11; matrix products, arithmetic and copies ran while one was open for 24% -> 24% of each run, Pallas kernels for 8% -> 8%
where the time goes in v4:
time: 1310 us; the launch traced here: 1300 us
  Pallas kernels  729 us (56%)
  matrix products  160 us (12%)
  local copies, waits for them, and re-layouts  130 us (10%)
  waiting for transfers between devices  129 us (10%)
  other arithmetic  117 us (9%)
  starting transfers between devices  22.6 us (2%)
  between operations  16.1 us (1%)
    pallas_call x1, Pallas kernels, moe_call(): pl.pallas_call(kernel, grid=(seqs, experts + token_steps), in_specs=[toke...  405 us
    pallas_call x3, Pallas kernels, scatter_call(): pl.pallas_call(functools.partial(sum_kernel if more is None else scatter_...  251 us
    ppermute x13, waiting for transfers between devices, swap(): lax.ppermute(values, axis_name, [(i, i ^ mask) for i in range(count)])  95.3 us
    dot_general x7, matrix products, dot(): return jnp.dot(left, right, preferred_element_type=F32)  79 us
    pallas_call x2, Pallas kernels, gather_call(): pl.pallas_call(functools.partial(gather_kernel, count), out_shape=[whole]...  73.7 us
    unnamed x247, local copies, waits for them, and re-layouts  42.4 us
    dot_general x1, matrix products, expert_grads(): jnp.einsum('ecd,ecf->edf', flat(rows), flat(d_gu), preferred_element_type...  29.1 us
  transfers between devices with their start and end apart: 21, of which 11 were waited for; matrix products, arithmetic and copies ran while one was open for 24% of the time, Pallas kernels for 8%

profile of v4, /device:TPU:0, one launch (start us, length us, event | category | flops | bytes accessed | tf_op | source)
XLA Modules:
  0.0 1304.4 jit_solution(4615383177764596603)
XLA Ops:
  9.9 4.6 copy.186
  14.9 4.7 copy.185
  45.7 37.1 %shard_map.348 = bf16[1024,2048]{1,0:T(8,128)(2,1)} custom-call(bf16[256,2048]{1,0:T(8,128)(2,1)} %fusion.15.refs_0_), custom_call_target="tpu_custom_call" | custom-call | tf_op jit(solution)/shard_map/pallas_call | solution.py:182
  88.6 4.5 reduce-window.6
  96.4 4.6 bitcast_select_fusion
  110.0 10.0 fusion.166
  128.1 4.7 fusion.159
  136.6 22.7 %all-to-all-done = bf16[8,256,528]{1,2,0:T(8,128)(2,1)} async-done(((bf16[8,256,528]{1,2,0:T(8,128)(2,1)}), bf16[8,256,528]{1,2,0:T(8,128)(2,1)}, u32[]{:S(2)}, u32[]{:S(2)}) %all-to-all-start) | async-done | bytes 2162720 | tf_op jit(solution)/shard_map/all_to_all | solution.py:962
  180.1 4.4 copy.200.refs_5_
  196.7 10.2 all-gather.8.cloned.1.call-done
  210.9 38.3 %shard_map.349 = f32[256,2048]{1,0:T(8,128)S(1)} custom-call(bf16[1,4,256,2048]{3,2,1,0:T(8,128)(2,1)S(1)} %bitcast.249), custom_call_target="tpu_custom_call" | custom-call | bytes 140000000 | tf_op jit(solution)/shard_map/pallas_call | solution.py:309
  252.3 404.6 %shard_map.350 = (bf16[8,1024,2048]{2,1,0:T(8,128)(2,1)}, bf16[8,1024,2048]{2,1,0:T(8,128)(2,1)}, bf16[4,1024,2048]{2,1,0:T(8,128)(2,1)}, bf16[4,1024,2048]{2,1,...) custom-call(bf16[256,2048]{1,0:T(8,128)(2,1)} %multiply_convert_fusi, ...), custom_call_target="tpu_custom_call" | custom-call | flops 212600881152 | bytes 1073741824 | tf_op jit(solution)/shard_map/pallas_call | solution.py:764
  656.9 178.3 %shard_map.351 = f32[256,2048]{1,0:T(8,128)S(1)} custom-call(bf16[4,4,256,2048]{3,2,1,0:T(8,128)(2,1)} %bitcast.260, bf16[4,4,256,2048]{3,2,1,0:T(8,128)(2,1)} %bitcast.261), custom_call_target="tpu_custom_call" | custom-call | bytes 560000000 | tf_op jit(solution)/shard_map/pallas_call | solution.py:309
  839.1 36.6 %shard_map.352 = bf16[1024,2048]{1,0:T(8,128)(2,1)} custom-call(bf16[256,2048]{1,0:T(8,128)(2,1)} %multiply_convert_fusion.3.refs_0_), custom_call_target="tpu_custom_call" | custom-call | tf_op jit(solution)/shard_map/pallas_call | solution.py:182
  875.7 9.0 constant_dynamic-slice_fusion.1
  885.2 11.5 constant_dynamic-slice_fusion.2
  937.1 17.0 %convolution_bitcast_fusion.1 = bf16[2048,256]{0,1:T(8,128)(2,1)S(1)} fusion(bf16[8,1024,2048]{2,1,0:T(8,128)(2,1)} %get-tuple-element.157, bf16[8,1024,256]{2,1,0:T(8,128)(2,1)} %get-tuple-element.158), kind=kOutput, calls=%fused_computation.70 | convolution fusion | flops 8589934592 | bytes 38797312 | tf_op jit(solution)/shard_map/dot_general | solution.py:72
  956.2 25.1 %fusion.165 = (bf16[2048,512]{0,1:T(8,128)(2,1)S(1)}, f32[2048,512]{0,1:T(8,128)}) fusion(bf16[8,1024,2048]{2,1,0:T(8,128)(2,1)} %get-tuple-element.153, bf16[8,1024,512]{2,1,0:T(8,128)(2,1)} %get-tuple-element.156), kind=kOutput, calls=%fused_computation.332 | convolution fusion | flops 17180917760 | bytes 48234496 | tf_op jit(solution)/shard_map/dot_general | solution.py:72
  988.6 5.2 convolution_convert_fusion.4
  993.8 52.1 %collective-permute-done.4 = bf16[2,4,128,2048]{3,2,1,0:T(8,128)(2,1)} collective-permute-done((bf16[2,4,128,2048]{3,2,1,0:T(8,128)(2,1)}, bf16[2,4,128,2048]{3,2,1,0:T(8,128)(2,1)}, u32[]{:S(2)}, u32[]{:S(2)}) %collective-permute-start.4) | collective-permute-done | bytes 4194336 | tf_op jit(solution)/shard_map/ppermute | solution.py:77
  1046.9 5.8 add_convert_fusion.1
  1084.9 15.9 %collective-permute-done.6 = bf16[4,128,2048]{2,1,0:T(8,128)(2,1)} collective-permute-done((bf16[4,128,2048]{2,1,0:T(8,128)(2,1)}, bf16[4,128,2048]{2,1,0:T(8,128)(2,1)}, u32[]{:S(2)}, u32[]{:S(2)}) %collective-permute-start.6) | collective-permute-done | bytes 2097184 | tf_op jit(solution)/shard_map/ppermute | solution.py:77
  1100.9 7.7 collective-permute-done.7
  1144.4 9.0 convolution_convert_fusion
  1155.2 8.9 convolution_convert_fusion.1
  1164.1 34.3 %shard_map.353 = f32[256,2048]{1,0:T(8,128)S(1)} custom-call(bf16[1,4,256,2048]{3,2,1,0:T(8,128)(2,1)S(1)} %bitcast.248), custom_call_target="tpu_custom_call" | custom-call | bytes 140000000 | tf_op jit(solution)/shard_map/pallas_call | solution.py:309
  1198.6 29.1 %fusion.167 = f32[2,2048,768]{1,2,0:T(8,128)} fusion(bf16[2,3072,2048]{2,1,0:T(8,128)(2,1)} %bitcast.296, bf16[2,3072,768]{2,1,0:T(8,128)(2,1)} %bitcast.297), kind=kOutput, calls=%fused_computation.334 | convolution fusion | flops 19327352832 | bytes 47185920 | tf_op jit(solution)/shard_map/ecd,ecf->edf/dot_general | solution.py:832
  1231.8 10.8 fusion.155
  1242.6 17.3 %fusion.4 = f32[2,352,2048]{2,1,0:T(8,128)} fusion(bf16[2,3072,2048]{2,1,0:T(8,128)(2,1)} %bitcast.295, bf16[2,3072,384]{2,1,0:T(8,128)(2,1)} %bitcast.298), kind=kOutput, calls=%fused_computation.18 | convolution fusion | flops 8858370048 | bytes 35651584 | tf_op jit(solution)/shard_map/ecf,ecd->efd/dot_general | solution.py:834
  1262.1 5.3 collective-permute-done.9
  1277.0 11.3 collective-permute-done.12
  1290.3 4.7 fusion.19
  (456 shorter events, 242.9 us)
Async XLA Ops:
  7.2 97.3 %all-gather.4.cloned.1.call-start = ((), (), s32[]{:S(2)}) async-start(), calls=%async_computation.5 | async-start | bytes 7077888 | tf_op jit(solution)/shard_map/all_gather | solution.py:947
  9.3 23.5 %collective-permute-start = (s32[1,4,1024]{2,1,0:T(4,128)S(1)}, s32[1,4,1024]{2,1,0:T(4,128)S(1)}, u32[]{:S(2)}, u32[]{:S(2)}) collective-permute-start(s32[1,4,1024]{2,1,0:T(4,128)S(1)} %bitcast.279), channel_id=1, source_target_pairs={{0,4},{4,0},{8,12},{12,8},{16,20},{20,16},{24,28},{28,24},{1,5},{5... | collective-permute-start | bytes 49160 | tf_op jit(solution)/shard_map/ppermute | solution.py:77
  20.9 167.2 %copy-start.58 = (pred[256,512]{1,0:T(8,128)(4,1)}, pred[256,512]{1,0:T(8,128)(4,1)S(1)}, u32[]{:S(2)}) copy-start(pred[256,512]{1,0:T(8,128)(4,1)S(1)} %compare_and_fusion.1) | copy-start | bytes 393220
  22.2 168.3 %copy-start.38 = (pred[256,1024]{1,0:T(8,128)(4,1)}, pred[256,1024]{1,0:T(8,128)(4,1)S(1)}, u32[]{:S(2)}) copy-start(pred[256,1024]{1,0:T(8,128)(4,1)S(1)} %fusion.85) | copy-start | bytes 786436
  32.8 7.5 collective-permute-start.1
  40.3 46.3 %collective-permute-start.2 = (s32[4,4,1024]{2,1,0:T(4,128)S(1)}, s32[4,4,1024]{2,1,0:T(4,128)S(1)}, u32[]{:S(2)}, u32[]{:S(2)}) collective-permute-start(s32[4,4,1024]{2,1,0:T(4,128)S(1)} %pad_add_fusion.1), channel_id=1, source_target_pairs={{0,16},{4,20},{8,24},{12,28},{16,0},{20,4},{24,8},{28,12},{1,17},{... | collective-permute-start | bytes 196616 | tf_op jit(solution)/shard_map/ppermute | solution.py:77
  45.7 38.3 %copy-start.118 = (bf16[512]{0:T(512)(128)(2,1)S(1)}, bf16[512]{0:T(512)(128)(2,1)}, u32[]{:S(2)}) copy-start(bf16[512]{0:T(512)(128)(2,1)} %param.41) | copy-start | bytes 3076
  45.7 38.9 %copy-start.114 = (bf16[2048]{0:T(1024)(128)(2,1)S(1)}, bf16[2048]{0:T(1024)(128)(2,1)}, u32[]{:S(2)}) copy-start(bf16[2048]{0:T(1024)(128)(2,1)} %param.45) | copy-start | bytes 12292
  45.7 38.9 %copy-start.115 = (bf16[2048]{0:T(1024)(128)(2,1)S(1)}, bf16[2048]{0:T(1024)(128)(2,1)}, u32[]{:S(2)}) copy-start(bf16[2048]{0:T(1024)(128)(2,1)} %param.47) | copy-start | bytes 12292
  45.7 38.9 %copy-start.68 = (bf16[2,352,2048]{2,1,0:T(8,128)(2,1)S(1)}, bf16[2,352,2048]{2,1,0:T(8,128)(2,1)}, u32[]{:S(2)}) copy-start(bf16[2,352,2048]{2,1,0:T(8,128)(2,1)} %param.53) | copy-start | bytes 8650756
  84.6 165.2 %copy-start.80 = (f32[2048]{0:T(1024)}, f32[2048]{0:T(1024)S(1)}, u32[]{:S(2)}) copy-start(f32[2048]{0:T(1024)S(1)} %convert_element_type.524) | copy-start | bytes 24580
  104.5 54.9 %all-to-all-start = ((bf16[8,256,528]{1,2,0:T(8,128)(2,1)}), bf16[8,256,528]{1,2,0:T(8,128)(2,1)}, u32[]{:S(2)}, u32[]{:S(2)}) async-start(bf16[8,256,528]{1,2,0:T(8,128)(2,1)} %maximum_bitcast_fusion), calls=%async_computation | async-start | bytes 4325376 | tf_op jit(solution)/shard_map/all_to_all | solution.py:962
  108.9 68.4 %all-gather.6.cloned.1.call-start = ((), (), s32[]{:S(2)}) async-start(), calls=%async_computation.6 | async-start | bytes 5242880 | tf_op jit(solution)/shard_map/all_gather | solution.py:951
  109.7 97.3 %all-gather.8.cloned.1.call-start = ((), (), s32[]{:S(2)}) async-start(), calls=%async_computation.7 | async-start | bytes 2359296 | tf_op jit(solution)/shard_map/all_gather | solution.py:952
  122.9 42.0 %copy-start.32 = (bf16[1024,512]{1,0:T(8,128)(2,1)}, bf16[1024,512]{1,0:T(8,128)(2,1)S(1)}, u32[]{:S(2)}) copy-start(bf16[1024,512]{1,0:T(8,128)(2,1)S(1)} %get-tuple-element.270) | copy-start | bytes 3145732
  161.4 90.9 %collective-permute-start.3 = (bf16[256,2048]{1,0:T(8,128)(2,1)}, bf16[256,2048]{1,0:T(8,128)(2,1)}, u32[]{:S(2)}, u32[]{:S(2)}) collective-permute-start(bf16[256,2048]{1,0:T(8,128)(2,1)} %fusion.20), channel_id=1, source_target_pairs={{0,8},{4,12},{8,0},{12,4},{16,24},{20,28},{24,16},{28,20},{1,9},{5... | collective-permute-start | bytes 3145736 | tf_op jit(solution)/shard_map/ppermute | solution.py:77
  177.3 888.6 %reduce-scatter.4.cloned.1.call-start = ((), (), s32[]{:S(2)}) async-start(), calls=%async_computation.8 | async-start | bytes 2359296 | tf_op jit(solution)/shard_map/reduce_scatter | solution.py:1095
  656.9 178.4 %copy-start.8 = (f32[256,2048]{1,0:T(8,128)S(1)}, f32[256,2048]{1,0:T(8,128)}, u32[]{:S(2)}) copy-start(f32[256,2048]{1,0:T(8,128)} %copy-done.7) | copy-start | bytes 6291460
  656.9 178.4 %copy-start.81 = (f32[2048]{0:T(1024)S(1)}, f32[2048]{0:T(1024)}, u32[]{:S(2)}) copy-start(f32[2048]{0:T(1024)} %copy-done.80) | copy-start | bytes 24580
  656.9 178.4 %copy-start.99 = (f32[256]{0:T(256)S(1)}, f32[256]{0:T(256)}, u32[]{:S(2)}) copy-start(f32[256]{0:T(256)} %copy-done.98) | copy-start | bytes 3076
  954.1 91.8 %collective-permute-start.4 = (bf16[2,4,128,2048]{3,2,1,0:T(8,128)(2,1)}, bf16[2,4,128,2048]{3,2,1,0:T(8,128)(2,1)}, u32[]{:S(2)}, u32[]{:S(2)}) collective-permute-start(bf16[2,4,128,2048]{3,2,1,0:T(8,128)(2,1)} %pad_maximum_fusion), channel_id=1, source_target_pairs={{0,1},{1,0},{2,3},{3,2},{4,5},{5,4},{6,7},{7,6},{8,9},{9,8},{10,11... | collective-permute-start | bytes 12582920 | tf_op jit(solution)/shard_map/ppermute | solution.py:77
  954.8 91.2 %collective-permute-start.5 = (bf16[2,4,128,2048]{3,2,1,0:T(8,128)(2,1)}, bf16[2,4,128,2048]{3,2,1,0:T(8,128)(2,1)}, u32[]{:S(2)}, u32[]{:S(2)}) collective-permute-start(bf16[2,4,128,2048]{3,2,1,0:T(8,128)(2,1)} %pad_maximum_fusion.1), channel_id=1, source_target_pairs={{0,2},{1,3},{2,0},{3,1},{4,6},{5,7},{6,4},{7,5},{8,10},{9,11},{10,... | collective-permute-start | bytes 12582920 | tf_op jit(solution)/shard_map/ppermute | solution.py:77
  984.2 100.7 %all-to-all-start.1 = ((bf16[8,256,528]{1,2,0:T(8,128)(2,1)}), bf16[8,256,528]{1,2,0:T(8,128)(2,1)}, u32[]{:S(2)}, u32[]{:S(2)}) async-start(bf16[8,256,528]{1,2,0:T(8,128)(2,1)} %bitcast.244), calls=%async_computation.1 | async-start | bytes 4325376 | tf_op jit(solution)/shard_map/all_to_all | solution.py:1107
  988.6 301.7 %reduce-scatter.6.cloned.1.call-start = ((), (), s32[]{:S(2)}) async-start(), calls=%async_computation.9 | async-start | bytes 5242880 | tf_op jit(solution)/shard_map/reduce_scatter | solution.py:936
  1055.1 45.8 %collective-permute-start.6 = (bf16[4,128,2048]{2,1,0:T(8,128)(2,1)}, bf16[4,128,2048]{2,1,0:T(8,128)(2,1)}, u32[]{:S(2)}, u32[]{:S(2)}) collective-permute-start(bf16[4,128,2048]{2,1,0:T(8,128)(2,1)} %get-tuple-element.283), channel_id=1, source_target_pairs={{0,2},{1,3},{2,0},{3,1},{4,6},{5,7},{6,4},{7,5},{8,10},{9,11},{10,... | collective-permute-start | bytes 6291464 | tf_op jit(solution)/shard_map/ppermute | solution.py:77
  1063.1 45.4 %collective-permute-start.7 = (bf16[4,128,2048]{2,1,0:T(8,128)(2,1)}, bf16[4,128,2048]{2,1,0:T(8,128)(2,1)}, u32[]{:S(2)}, u32[]{:S(2)}) collective-permute-start(bf16[4,128,2048]{2,1,0:T(8,128)(2,1)} %get-tuple-element.281), channel_id=1, source_target_pairs={{0,1},{1,0},{2,3},{3,2},{4,5},{5,4},{6,7},{7,6},{8,9},{9,8},{10,11... | collective-permute-start | bytes 6291464 | tf_op jit(solution)/shard_map/ppermute | solution.py:77
  1116.9 178.1 %reduce-scatter.8.cloned.1.call-start = ((), (), s32[]{:S(2)}) async-start(), calls=%async_computation.10 | async-start | bytes 7077888 | tf_op jit(solution)/shard_map/reduce_scatter | solution.py:1176
  1230.0 31.7 %collective-permute-start.8 = (f32[22,2048]{1,0:T(8,128)S(1)}, f32[22,2048]{1,0:T(8,128)S(1)}, u32[]{:S(2)}, u32[]{:S(2)}) collective-permute-start(f32[22,2048]{1,0:T(8,128)S(1)} %concatenate.94), channel_id=1, source_target_pairs={{0,1},{1,0},{2,3},{3,2},{4,5},{5,4},{6,7},{7,6},{8,9},{9,8},{10,11... | collective-permute-start | bytes 540680 | tf_op jit(solution)/shard_map/ppermute | solution.py:77
  1261.7 5.7 collective-permute-start.9
  1267.5 1.5 collective-permute-start.10
  1269.0 7.2 collective-permute-start.11
  1276.2 12.0 collective-permute-start.12
  (111 other events, 763.6 us)
Sparse Core Ops, SparseCore 0:
  10.3 70.1 all-gather.3
  111.6 53.0 all-gather.5
  177.4 29.4 all-gather.7
  937.2 33.8 reduce-scatter.3
  1117.0 74.6 reduce-scatter.5
  1193.9 70.3 reduce-scatter.7
